TPU v7x, 32 devices: a whole 2x2x4 slice. The times are simulated.
32 devices in a mesh: mom: 4 (over x, core), en: 8 (over z, y).
Axes of the slice: x: 2, y: 2, z: 4, core: 2. Of those that a mesh axis runs over, the one named last changes fastest.
Arguments:
- green_less: bfloat16 [8, 192, 8, 288], P('mom', 'en'), may hold values from -6 to 6
- green_greater: bfloat16 [8, 192, 8, 288], P('mom', 'en'), may hold values from -6 to 6
- derivative: float32 [2, 3, 144], replicated, may hold values from -1.75 to 1.75
- neighbours: int32 [2, 4], replicated, may hold values from 0 to 1
- phonon: bfloat16 [2, 8, 24, 3, 8], replicated, may hold values from 0.0099487305 to 0.099609375
Outputs:
- self_energy: bfloat16 [8, 192, 8, 288], P('mom', 'en')
- polarisation: float32 [8, 24, 3, 8], P('mom')
All inputs are finite; a program needn't handle non-finite values.
Results may differ from a plain program's by a relative error of at most 0.0034.
Values may be sent and summed in bfloat16 or wider, within the bound.
No kernel may reach another device: no remote copies, remote signals or barrier semaphores. Data moves between devices by JAX's collectives and lax.ppermute only.
A program may use at most 64 MiB of HBM per device.

v0:
```python
import functools

import jax
import jax.numpy as jnp
import numpy as np
from jax import lax
from jax.experimental import pallas as pl
from jax.experimental.pallas import tpu as pltpu
from jax.sharding import PartitionSpec as P

NO = 12
NB = 4
LANES = 128
BF = jnp.bfloat16
F32 = jnp.float32
HIGHEST = lax.Precision.HIGHEST
VMEM = pl.BlockSpec(memory_space=pltpu.VMEM)
HBM = pl.BlockSpec(memory_space=pltpu.HBM)
PARAMS = pltpu.CompilerParams(vmem_limit_bytes=24 * 1024 * 1024)


def dot(a, b):
    return jnp.dot(a, b, preferred_element_type=F32)


def dot_t(a, b):
    return lax.dot_general(a, b, (((1,), (1,)), ((), ())), preferred_element_type=F32)


def call(kernel, outs, ins, scratch=(), specs=None):
    return pl.pallas_call(
        kernel,
        out_shape=outs,
        in_specs=specs or [VMEM] * len(ins),
        out_specs=[VMEM] * len(outs),
        scratch_shapes=list(scratch),
        compiler_params=PARAMS,
    )(*ins)


def my_core():
    return lax.rem(lax.axis_index("mom"), 2).astype(jnp.int32)


def index(dims, axis):
    return lax.broadcasted_iota(jnp.int32, dims, axis)


def split(value, count):
    whole = jnp.floor((value.astype(F32) + 0.5) * (1.0 / count)).astype(jnp.int32)
    return whole, value - count * whole


def ones_at(condition):
    return condition.astype(F32).astype(BF)


def shape(dims, dtype):
    return jax.ShapeDtypeStruct(dims, dtype)


def pack_kernel(g_hbm, b_hbm, g_own, b_own, g_far, b_far, g_ref, b_ref, halves, sems):
    core = my_core()
    copies = []
    for i, (src, dst) in enumerate(((g_hbm, g_ref), (b_hbm, b_ref))):
        copies.append(pltpu.make_async_copy(src, dst, sems.at[i]))
        copies[-1].start()
    rows = g_own.shape[0]
    pairs = g_ref.shape[2]
    entries = g_ref.shape[3]
    half = pairs // 2
    dims = (rows, rows * pairs)
    gap = index(dims, 1) - pairs * index(dims, 0)
    perm = jnp.concatenate([ones_at(gap == p) for p in range(pairs)], axis=0)
    for copy, src, own, far in ((copies[0], g_ref, g_own, g_far), (copies[1], b_ref, b_own, b_far)):
        copy.wait()
        sorted_rows = dot(perm, src[...].reshape(rows * pairs, entries))
        for h in range(2):
            parts = [sorted_rows[(h * half + j) * rows : (h * half + j + 1) * rows] for j in range(half)]
            halves[h] = jnp.concatenate(parts, axis=1)
        own[...] = halves[core].astype(BF)
        far[...] = halves[1 - core].astype(BF)


def table_kernel(
    near_hbm, deriv_hbm, phonon_hbm, hi_ref, lo_ref, t_ref, perm_ref, join_ref, turn_ref, sort_ref,
    near_ref, deriv_ref, phonon_ref, factors, bases, sems, *, half, local_k, local_e,
):
    copies = []
    for i, (src, dst) in enumerate(((near_hbm, near_ref), (deriv_hbm, deriv_ref), (phonon_hbm, phonon_ref))):
        copies.append(pltpu.make_async_copy(src, dst, sems.at[i]))
        copies[-1].start()
    core = my_core()
    _, momenta, _, pairs, window = phonon_ref.shape
    size = NO * NO
    chip_k = 2 * local_k
    dims = perm_ref.shape
    e, k = split(index(dims, 0), momenta)
    perm_ref[...] = ones_at(index(dims, 1) == k * local_e + e)
    dims = join_ref.shape
    row, p = split(index(dims, 0), pairs)
    join_ref[...] = ones_at(index(dims, 1) == p * (local_k * local_e) + row)
    dims = sort_ref.shape
    k, i = split(index(dims, 0), 2 * local_e)
    at = jnp.where(i < local_e, (chip_k + k) * local_e + local_e - 1 - i, k * local_e + 2 * local_e - 1 - i)
    sort_ref[...] = ones_at((index(dims, 1) == at) & (k < chip_k))
    dims = turn_ref.shape[1:]
    u, i = split(index(dims, 0), NO)
    turn = ((index(dims, 1) == i * NO + u) & (u < NO)).astype(F32)
    for j in range(2 * half):
        shift = size * j % LANES
        moved = pltpu.roll(pltpu.roll(turn, shift, 0), shift, 1) if shift else turn
        turn_ref[j] = (moved * (1.0 - 2.0 * (j % 2))).astype(BF)
    x = (size, 2 * LANES)
    outer, inner = split(index(x, 0), NO)
    lane_outer, lane_inner = split(index(x, 1), NO)
    pick_l = ones_at(outer == lane_outer)
    pick_r = ones_at((outer == lane_inner) & (lane_outer < NO))
    picks = jnp.concatenate([pick_l, pick_r], axis=1)
    x = (size, 32)
    outer, inner = split(index(x, 0), NO)
    slot = split(index(x, 1), 16)[1]
    rows_l = ones_at(outer == slot)
    rows_r = ones_at(inner == slot)
    x = (16, size)
    mask = (split(index(x, 1), NO)[1] == index(x, 0)).astype(F32)
    for copy in copies:
        copy.wait()
    atoms = deriv_ref.shape[1]
    spread = []
    for m in range(3):
        for atom in range(atoms):
            spread.append(deriv_ref[m, atom : atom + 1, :] * mask)
    spread = jnp.concatenate(spread, axis=0)
    spread_hi = spread.astype(BF)
    spread_lo = (spread - spread_hi.astype(F32)).astype(BF)
    for i, part in enumerate((spread_hi, spread_lo)):
        rows = dot(part, picks)
        for n in range(3 * atoms):
            factors[n, 16 * i : 16 * i + 16] = rows[16 * n : 16 * n + 16]
    for p in range(half):
        pair = core * half + p
        atom = pair // NB
        other = near_ref[atom, pair % NB]
        for m in range(3):
            u = factors[m * atoms + atom][:, : 2 * LANES]
            v = factors[m * atoms + other][:, 2 * LANES :]
            for c in range(2):
                j = 2 * p + c
                shift = size * j % LANES
                uj = pltpu.roll(u, shift, 1) if shift else u
                vj = pltpu.roll(v, shift, 1) if shift else v
                kron = dot(rows_l, uj.astype(BF)) * dot(rows_r, vj.astype(BF))
                k_hi = kron.astype(BF)
                hi_ref[j * 3 + m] = k_hi
                lo_ref[j * 3 + m] = (kron - k_hi.astype(F32)).astype(BF)
    tiles = 3 * local_e // 8
    step = 8 * momenta
    first = momenta * (3 * local_e - 8)
    length = bases.shape[3]
    middle = 2 * local_e - 8
    dims = (window, length)
    lane = index(dims, 1)
    depth = index(dims, 0) + 1
    line = None
    for side in range(2):
        gap = lane - momenta * (middle + depth if side else middle - depth)
        for q in range(momenta):
            place = ones_at(gap == (-q) % momenta)
            weights = phonon_ref[side, q].astype(F32).reshape(3 * pairs, window).astype(BF)
            term = dot(weights, place)
            line = term if line is None else line + term
    lane = index((1, length), 1)
    k = split(lane, momenta)[1]
    for a in range(chip_k):
        moved = line
        if a:
            moved = jnp.where(k >= a, pltpu.roll(line, a, 1), pltpu.roll(line, length - momenta + a, 1))
        bases[a] = moved.reshape(3, pairs, length)
    for p in range(half):
        for m in range(3):
            grid = {}
            for a in range(chip_k):
                row = bases[a, m, pl.ds(core * half + p, 1), :]
                block = pltpu.roll(jnp.broadcast_to(row, (8, length)), 0, 1, stride=momenta, stride_axis=0)
                moved = {0: block}
                for t in range(tiles):
                    offset = first - step * t
                    part = offset % LANES
                    if part not in moved:
                        moved[part] = pltpu.roll(block, length - part, 1)
                    start = offset - part
                    grid[(t, a)] = moved[part][:, start : start + 2 * LANES]
            order = []
            per = local_e // 8
            for blk in range(3):
                for a in range(chip_k):
                    order += [grid[(blk * per + i, a)] for i in range(per)]
            t_ref[p * 3 + m] = jnp.concatenate(order, axis=0).astype(BF)


def product_kernel(*refs, half, entries, chips):
    core = my_core()
    blocks = refs[: 2 * chips]
    perm_ref, hi_ref, lo_ref, t_ref = refs[2 * chips : 2 * chips + 4]
    g1_ref, own_ref, low_ref, up_ref, gathered, result = refs[2 * chips + 4 :]
    for s in range(chips):
        gathered[2 * s + core] = blocks[2 * s][...]
        gathered[2 * s + 1 - core] = blocks[2 * s + 1][...]
    count, rows, width = gathered.shape
    depth = count * rows
    tiles = width // LANES
    g = dot(perm_ref[...], gathered[...].reshape(depth, width)).astype(BF)
    block_rows = hi_ref.shape[1]
    sums = [[None] * tiles for _ in range(3)]
    for j in range(2 * half):
        start = (entries // 2) * j // LANES * LANES
        shift = (entries // 2) * j - start
        lhs = g[:, start : start + 2 * LANES]

        def padded(ref, n):
            parts = [ref[n]]
            if shift:
                parts = [jnp.zeros((shift, 2 * LANES), BF)] + parts
            rest = 2 * LANES - shift - block_rows
            if rest:
                parts = parts + [jnp.zeros((rest, 2 * LANES), BF)]
            return jnp.concatenate(parts, axis=0)

        for m in range(3):
            r = dot(lhs, padded(hi_ref, j * 3 + m)) + dot(lhs, padded(lo_ref, j * 3 + m))
            for i in range(2):
                tile = start // LANES + i
                piece = r[:, i * LANES : (i + 1) * LANES]
                sums[m][tile] = piece if sums[m][tile] is None else sums[m][tile] + piece
    high = [[None] * tiles for _ in range(3)]
    low = [[None] * tiles for _ in range(3)]
    for m in range(3):
        for i in range(tiles):
            high[m][i] = sums[m][i].astype(BF)
            low[m][i] = (sums[m][i] - high[m][i].astype(F32)).astype(BF)
            g1_ref[m, :, i * LANES : (i + 1) * LANES] = high[m][i]
    lane = index((1, LANES), 1)
    carried = None
    for p in range(half):
        begin = entries * p
        first = begin // LANES
        last = (begin + entries - 1) // LANES
        total = None
        for m in range(3):
            t = t_ref[p * 3 + m][:, :depth]
            for part in (high, low):
                term = dot(t, jnp.concatenate(part[m][first : last + 1], axis=1))
                total = term if total is None else total + term
        for i in range(first, last + 1):
            tile = total[:, (i - first) * LANES : (i - first + 1) * LANES]
            if i == first and begin % LANES:
                tile = jnp.where(lane < begin % LANES, carried, tile)
            if i == last and (begin + entries) % LANES:
                carried = tile
            else:
                for r in range(6):
                    result[r, :, i * LANES : (i + 1) * LANES] = tile[r * rows : (r + 1) * rows]
    place = lax.axis_index("en")
    below = jnp.where(place == 0, 0.0, 1.0)
    above = jnp.where(place == lax.axis_size("en") - 1, 0.0, 1.0)
    for i, c in enumerate((core, 1 - core)):
        low_ref[i] = (result[c] * below).astype(BF)
        own_ref[i] = result[2 + c]
        up_ref[i] = (result[4 + c] * above).astype(BF)


def polar_kernel(b_own, b_far, prev_own, prev_far, turn_ref, sort_ref, g1_ref, out_ref, gathered, *, half, entries, local_k, local_e, scale):
    core = my_core()
    present = jnp.where(lax.axis_index("en") == 0, 0.0, 1.0)
    gathered[core] = (prev_own[...].astype(F32) * present).astype(BF)
    gathered[1 - core] = (prev_far[...].astype(F32) * present).astype(BF)
    gathered[2 + core] = b_own[...]
    gathered[3 - core] = b_far[...]
    count, rows, width = gathered.shape
    tiles = width // LANES
    b = dot(sort_ref[...], gathered[...].reshape(count * rows, width)).astype(BF)
    sums = [None] * tiles
    for j in range(2 * half):
        start = (entries // 2) * j // LANES * LANES
        r = dot(b[:, start : start + 2 * LANES], turn_ref[j])
        for i in range(2):
            tile = start // LANES + i
            piece = r[:, i * LANES : (i + 1) * LANES]
            sums[tile] = piece if sums[tile] is None else sums[tile] + piece
    chip_k = 2 * local_k
    group = 2 * local_e
    columns = sort_ref.shape[0]
    window = local_e
    momenta = g1_ref.shape[1] // local_e
    lane = index((1, LANES), 1)
    pieces = []
    for p in range(half):
        begin = entries * p
        first = begin // LANES
        last = (begin + entries - 1) // LANES
        parts = []
        for i in range(first, last + 1):
            tile = sums[i]
            if i == first and begin % LANES:
                tile = jnp.where(lane < begin % LANES, 0.0, tile)
            if i == last and (begin + entries) % LANES:
                tile = jnp.where(lane < (begin + entries) % LANES, tile, 0.0)
            parts.append(tile.astype(BF))
        rhs = jnp.concatenate(parts, axis=1)
        held = None
        for m in range(3):
            s = dot_t(g1_ref[m][:, first * LANES : (last + 1) * LANES], rhs)
            acc = None
            for e in range(local_e):
                row = pltpu.roll(s[e * momenta : (e + 1) * momenta], columns - (local_e - e), 1)
                acc = row if acc is None else acc + row
            total = None
            for a in range(chip_k):
                piece = acc if a == 0 else pltpu.roll(acc, columns - group * a, 1)
                piece = piece[:, :LANES]
                if a:
                    piece = pltpu.roll(piece, momenta - a, 0)
                total = piece if total is None else total + piece
            total = jnp.where(lane < window, total * scale, 0.0)
            if m:
                total = pltpu.roll(total, m * (LANES // 4), 1)
            held = total if held is None else held + total
        pieces.append(held)
    targets, en = out_ref.shape[:2]
    for t in range(targets):
        tile = jnp.concatenate(
            [pieces[p][t * local_k + i : t * local_k + i + 1] for i in range(local_k) for p in range(half)], axis=0
        )
        for e in range(en):
            out_ref[t, e] = tile


def total_kernel(in_ref, out_ref, *, half):
    targets, en = in_ref.shape[:2]
    local_k, _, _, window = out_ref.shape
    sums = []
    for c in range(2):
        total = None
        for t in range(c, targets, 2):
            for e in range(en):
                total = in_ref[t, e] if total is None else total + in_ref[t, e]
        sums.append(total)
    for i in range(local_k):
        tile = jnp.concatenate([sums[c][i * half : (i + 1) * half] for c in range(2)], axis=0)
        for m in range(3):
            moved = pltpu.roll(tile, LANES - m * (LANES // 4), 1) if m else tile
            out_ref[i, m] = moved[:, :window]


def sum_kernel(own, below, above, mine, theirs):
    for i, out in enumerate((mine, theirs)):
        out[...] = (own[i] + below[i].astype(F32) + above[i].astype(F32)).astype(BF)


def join_kernel(mine, other, perm_ref, out_ref, halves):
    core = my_core()
    pairs = out_ref.shape[2]
    entries = out_ref.shape[3]
    half = pairs // 2
    halves[core] = mine[...].astype(F32)
    halves[1 - core] = other[...].astype(F32)
    parts = []
    for p in range(pairs):
        begin = entries * (p % half)
        parts.append(halves[p // half][:, begin : begin + entries])
    stacked = jnp.concatenate(parts, axis=0).astype(BF)
    out_ref[...] = dot(perm_ref[...], stacked).astype(BF).reshape(out_ref.shape)


def body(green_less, green_greater, derivative, neighbours, phonon, *, mom, en):
    local_k, local_e, pairs, entries = green_less.shape
    momenta, window = phonon.shape[1], phonon.shape[2]
    atoms = derivative.shape[0]
    half = pairs // 2
    rows = local_k * local_e
    width = half * entries
    chips = mom // 2
    chip_k = 2 * local_k
    total_e = local_e * en
    size = NO * NO

    g_own, b_own, g_far, b_far = call(
        pack_kernel,
        [shape((rows, width), BF)] * 4,
        [green_less, green_greater],
        [
            pltpu.VMEM(green_less.shape, BF),
            pltpu.VMEM(green_less.shape, BF),
            pltpu.VMEM((2, rows, width), F32),
            pltpu.SemaphoreType.DMA((2,)),
        ],
        [HBM, HBM],
    )

    def move(value, dchip, dcore, de):
        links = []
        for m in range(mom):
            target = ((m // 2 + dchip) % chips) * 2 + (m % 2 if dcore == 0 else 1 - m % 2)
            for e in range(en):
                links.append((m * en + e, target * en + (e + de) % en))
        return lax.ppermute(value, ("mom", "en"), links)

    blocks = [g_own, move(g_far, 0, 1, 0)]
    for s in range(1, chips):
        blocks += [move(g_own, -s, 0, 0), move(g_far, -s, 1, 0)]
    b_core = move(b_far, 0, 1, 0)
    prev_own = move(b_own, 0, 0, 1)
    prev_far = move(b_far, 0, 1, 1)

    near = neighbours.astype(jnp.int32)
    deriv = derivative.transpose(1, 0, 2)
    weights = phonon.transpose(0, 1, 3, 4, 2)
    columns = -(-chip_k * 2 * local_e // LANES) * LANES
    k_hi, k_lo, toeplitz, to_energy, to_rows, turn, sort_e = call(
        functools.partial(table_kernel, half=half, local_k=local_k, local_e=local_e),
        [
            shape((6 * half, size, 2 * LANES), BF),
            shape((6 * half, size, 2 * LANES), BF),
            shape((3 * half, 3 * chip_k * local_e, 2 * LANES), BF),
            shape((momenta * local_e,) * 2, BF),
            shape((rows * pairs,) * 2, BF),
            shape((2 * half, 2 * LANES, 2 * LANES), BF),
            shape((columns, 2 * chip_k * local_e), BF),
        ],
        [near, deriv, weights],
        [
            pltpu.SMEM(near.shape, jnp.int32),
            pltpu.VMEM(deriv.shape, F32),
            pltpu.VMEM(weights.shape, BF),
            pltpu.VMEM((3 * atoms, 32, 4 * LANES), F32),
            pltpu.VMEM((chip_k, 3, pairs, 4 * local_e * momenta), F32),
            pltpu.SemaphoreType.DMA((3,)),
        ],
        [HBM, HBM, HBM],
    )

    g1, own, low, up = call(
        functools.partial(product_kernel, half=half, entries=entries, chips=chips),
        [
            shape((3, momenta * local_e, width), BF),
            shape((2, rows, width), F32),
            shape((2, rows, width), BF),
            shape((2, rows, width), BF),
        ],
        blocks + [to_energy, k_hi, k_lo, toeplitz],
        [pltpu.VMEM((2 * chips, rows, width), BF), pltpu.VMEM((6, rows, width), F32)],
    )
    from_above = move(low, 0, 0, -1)
    from_below = move(up, 0, 0, 1)

    (partial,) = call(
        functools.partial(
            polar_kernel, half=half, entries=entries, local_k=local_k, local_e=local_e,
            scale=1.0 / (NO * float(np.sqrt(momenta * total_e))),
        ),
        [shape((mom, en, local_k * half, LANES), F32)],
        [b_own, b_core, prev_own, prev_far, turn, sort_e, g1],
        [pltpu.VMEM((4, rows, width), BF)],
    )
    terms = lax.all_to_all(
        partial.reshape(mom * en, local_k * half, LANES), ("mom", "en"), split_axis=0, concat_axis=0, tiled=True
    )
    (polar,) = call(
        functools.partial(total_kernel, half=half),
        [shape((local_k, 3, pairs, window), F32)],
        [terms.reshape(mom, en, local_k * half, LANES)],
    )
    polar = polar.transpose(0, 3, 1, 2)

    mine, theirs = call(
        sum_kernel, [shape((rows, width), BF)] * 2, [own, from_below, from_above]
    )
    other = move(theirs, 0, 1, 0)
    (self_energy,) = call(
        join_kernel,
        [shape(green_less.shape, BF)],
        [mine, other, to_rows],
        [pltpu.VMEM((2, rows, width), F32)],
    )
    return (self_energy, polar)


def solution(mesh):
    return jax.shard_map(
        functools.partial(body, mom=mesh.shape["mom"], en=mesh.shape["en"]),
        mesh=mesh,
        in_specs=(P("mom", "en", None, None), P("mom", "en", None, None), P(), P(), P()),
        out_specs=(P("mom", "en", None, None), P("mom", None, None, None)),
        check_vma=False,
    )
```

profile of v0, /device:TPU:0, one launch (start us, length us, event | category | flops | bytes accessed | tf_op | source)
XLA Modules:
  0.0 38.6 jit_solution(9764987022758397921)
XLA Ops:
  0.6 1.0 %copy-done = bf16[2,24,8,288]{3,2,1,0:T(8,128)(2,1)S(1)} copy-done((bf16[2,24,8,288]{3,2,1,0:T(8,128)(2,1)S(1)}, bf16[2,24,8,288]{3,2,1,0:T(8,128)(2,1)}, u32[]{:S(2)}) %copy-start) | copy-done | bytes 221208
  1.6 1.0 %copy-done.1 = bf16[2,24,8,288]{3,2,1,0:T(8,128)(2,1)S(1)} copy-done((bf16[2,24,8,288]{3,2,1,0:T(8,128)(2,1)S(1)}, bf16[2,24,8,288]{3,2,1,0:T(8,128)(2,1)}, u32[]{:S(2)}) %copy-start.1) | copy-done | bytes 221208
  2.6 1.1 %shard_map.68 = (bf16[48,1152]{1,0:T(8,128)(2,1)S(1)}, bf16[48,1152]{1,0:T(8,128)(2,1)S(1)}, bf16[48,1152]{1,0:T(8,128)(2,1)S(1)}, bf16[48,1152]{1,0:T(8,128)(2,1)S(1)}) custom-call(bf16[2,24,8,288]{3,2,1,0:T(8,128)(2,1)S(1)} %copy-done, bf16[2,24,8,288]{3,2,1,0:T(8,128)(2,1)S(1)} %copy-done.1), custom_call_target="tpu_custom_call" | custom-call | tf_op jit(solution)/shard_map/pallas_call | solution.py:31
  3.7 0.5 %collective-permute-start = (bf16[48,1152]{1,0:T(8,128)(2,1)S(1)}, bf16[48,1152]{1,0:T(8,128)(2,1)S(1)}, u32[]{:S(2)}, u32[]{:S(2)}) collective-permute-start(bf16[48,1152]{1,0:T(8,128)(2,1)S(1)} %get-tuple-element.20), channel_id=1, source_target_pairs={{0,8},{1,9},{2,10},{3,11},{4,12},{5,13},{6,14},{7,15},{8,0},{9,1},... | collective-permute-start | bytes 331784 | tf_op jit(solution)/shard_map/ppermute | solution.py:407
  4.2 2.6 %collective-permute-start.1 = (bf16[48,1152]{1,0:T(8,128)(2,1)S(1)}, bf16[48,1152]{1,0:T(8,128)(2,1)S(1)}, u32[]{:S(2)}, u32[]{:S(2)}) collective-permute-start(bf16[48,1152]{1,0:T(8,128)(2,1)S(1)} %get-tuple-element.19.refs_0_), channel_id=1, source_target_pairs={{0,16},{1,17},{2,18},{3,19},{4,20},{5,21},{6,22},{7,23},{8,24},{9,... | collective-permute-start | bytes 331784 | tf_op jit(solution)/shard_map/ppermute | solution.py:407
  6.8 0.1 collective-permute-start.2
  6.9 0.1 collective-permute-start.6
  7.0 2.0 %collective-permute-start.7 = (bf16[48,1152]{1,0:T(8,128)(2,1)S(1)}, bf16[48,1152]{1,0:T(8,128)(2,1)S(1)}, u32[]{:S(2)}, u32[]{:S(2)}) collective-permute-start(bf16[48,1152]{1,0:T(8,128)(2,1)S(1)} %get-tuple-element.31.b_own), channel_id=1, source_target_pairs={{0,1},{1,2},{2,3},{3,4},{4,5},{5,6},{6,7},{7,0},{8,9},{9,10},{10,1... | collective-permute-start | bytes 331784 | tf_op jit(solution)/shard_map/ppermute | solution.py:407
  9.0 0.0 collective-permute-done.refs_1_
  9.0 1.0 %collective-permute-start.8 = (bf16[48,1152]{1,0:T(8,128)(2,1)S(1)}, bf16[48,1152]{1,0:T(8,128)(2,1)S(1)}, u32[]{:S(2)}, u32[]{:S(2)}) collective-permute-start(bf16[48,1152]{1,0:T(8,128)(2,1)S(1)} %get-tuple-element.32), channel_id=1, source_target_pairs={{0,9},{1,10},{2,11},{3,12},{4,13},{5,14},{6,15},{7,8},{8,1},{9,2},... | collective-permute-start | bytes 331784 | tf_op jit(solution)/shard_map/ppermute | solution.py:407
  10.0 0.9 %copy-done.2 = bf16[2,8,24,3,8]{2,4,3,1,0:T(8,128)(2,1)S(1)} copy-done((bf16[2,8,24,3,8]{2,4,3,1,0:T(8,128)(2,1)S(1)}, bf16[2,8,24,3,8]{2,4,3,1,0:T(8,128)(2,1)}, u32[]{:S(2)}) %copy-start.2) | copy-done | bytes 18456
  10.9 0.7 %copy-done.3 = f32[2,3,144]{2,0,1:T(2,128)S(1)} copy-done((f32[2,3,144]{2,0,1:T(2,128)S(1)}, f32[2,3,144]{2,0,1:T(2,128)}, u32[]{:S(2)}) %copy-start.3) | copy-done | bytes 3480
  11.6 0.7 %copy-done.4 = s32[2,4]{1,0:T(2,128)S(1)} copy-done((s32[2,4]{1,0:T(2,128)S(1)}, s32[2,4]{1,0:T(2,128)}, u32[]{:S(2)}) %copy-start.4) | copy-done | bytes 56
  12.2 2.9 %shard_map.69 = (bf16[24,144,256]{2,1,0:T(8,128)(2,1)S(1)}, bf16[24,144,256]{2,1,0:T(8,128)(2,1)S(1)}, bf16[12,288,256]{2,1,0:T(8,128)(2,1)S(1)}, bf16[192,192]{...) custom-call(s32[2,4]{1,0:T(2,128)S(1)} %copy-done.4, ...), custom_call_target="tpu_custom_call" | custom-call | tf_op jit(solution)/shard_map/pallas_call | solution.py:31
  15.1 0.0 collective-permute-done.1.refs_2_
  15.1 0.0 collective-permute-done.2.refs_3_
  15.1 3.7 %shard_map.70 = (bf16[3,192,1152]{2,1,0:T(8,128)(2,1)S(1)}, f32[2,48,1152]{2,1,0:T(8,128)S(1)}, bf16[2,48,1152]{2,1,0:T(8,128)(2,1)S(1)}, bf16[2,48,1152]{2,1,0:T(8,128)(2,1)S(1)}) custom-call(bf16[48,1152]{1,0:T(8,128)(2,1)S(1)} %get-tuple-element.19.refs_0_, bf16[48,1152]{1,0:T(8,128)(2,1)S(1)} %collective-permute-done.refs_1_, ...), custom_call_target="tpu_custom_call" | custom-call | tf_op jit(solution)/shard_map/pallas_call | solution.py:31
  18.9 1.6 %collective-permute-start.3 = (bf16[2,48,1152]{2,1,0:T(8,128)(2,1)S(1)}, bf16[2,48,1152]{2,1,0:T(8,128)(2,1)S(1)}, u32[]{:S(2)}, u32[]{:S(2)}) collective-permute-start(bf16[2,48,1152]{2,1,0:T(8,128)(2,1)S(1)} %get-tuple-element.26), channel_id=1, source_target_pairs={{0,1},{1,2},{2,3},{3,4},{4,5},{5,6},{6,7},{7,0},{8,9},{9,10},{10,1... | collective-permute-start | bytes 663560 | tf_op jit(solution)/shard_map/ppermute | solution.py:407
  20.4 3.2 %collective-permute-start.4 = (bf16[2,48,1152]{2,1,0:T(8,128)(2,1)S(1)}, bf16[2,48,1152]{2,1,0:T(8,128)(2,1)S(1)}, u32[]{:S(2)}, u32[]{:S(2)}) collective-permute-start(bf16[2,48,1152]{2,1,0:T(8,128)(2,1)S(1)} %get-tuple-element.27), channel_id=1, source_target_pairs={{0,7},{1,0},{2,1},{3,2},{4,3},{5,4},{6,5},{7,6},{8,15},{9,8},{10,9... | collective-permute-start | bytes 663560 | tf_op jit(solution)/shard_map/ppermute | solution.py:407
  23.6 0.0 collective-permute-done.6.b_far
  23.6 0.0 collective-permute-done.7.prev_own
  23.7 0.0 collective-permute-done.8.prev_far
  23.7 2.7 %shard_map.73 = f32[4,8,8,128]{3,2,1,0:T(8,128)} custom-call(bf16[48,1152]{1,0:T(8,128)(2,1)S(1)} %get-tuple-element.31.b_own, bf16[48,1152]{1,0:T(8,128)(2,1)S(1)} %collective-permute-done.6.b_far, bf16[48,1152]{1,0:T(8,128)(2,1)S(1)} %collective-permute-done.7.prev_own, bf16[48,1152]{1,0:T(8,128)(2,1)S(1)} %collective-permute-done.8.prev_far, ...), custom_call_target="tpu_custom_call" | custom-call | tf_op jit(solution)/shard_map/pallas_call | solution.py:31
  26.4 2.6 %all-to-all-start = ((f32[32,8,128]{2,1,0:T(8,128)}), f32[32,8,128]{2,1,0:T(8,128)S(1)}, u32[]{:S(2)}, u32[]{:S(2)}) async-start(f32[32,8,128]{2,1,0:T(8,128)} %bitcast.2), calls=%async_computation | async-start | bytes 262144 | tf_op jit(solution)/shard_map/all_to_all | solution.py:466
  29.0 1.8 %collective-permute-done.3.below = bf16[2,48,1152]{2,1,0:T(8,128)(2,1)S(1)} collective-permute-done((bf16[2,48,1152]{2,1,0:T(8,128)(2,1)S(1)}, bf16[2,48,1152]{2,1,0:T(8,128)(2,1)S(1)}, u32[]{:S(2)}, u32[]{:S(2)}) %collective-permute-start.3) | collective-permute-done | bytes 221216 | tf_op jit(solution)/shard_map/ppermute | solution.py:407
  30.8 2.4 %collective-permute-done.4.above = bf16[2,48,1152]{2,1,0:T(8,128)(2,1)S(1)} collective-permute-done((bf16[2,48,1152]{2,1,0:T(8,128)(2,1)S(1)}, bf16[2,48,1152]{2,1,0:T(8,128)(2,1)S(1)}, u32[]{:S(2)}, u32[]{:S(2)}) %collective-permute-start.4) | collective-permute-done | bytes 221216 | tf_op jit(solution)/shard_map/ppermute | solution.py:407
  33.1 0.1 shard_map.71
  33.2 0.1 collective-permute-start.5
  33.3 3.4 %all-to-all-done = f32[32,8,128]{2,1,0:T(8,128)S(1)} async-done(((f32[32,8,128]{2,1,0:T(8,128)}), f32[32,8,128]{2,1,0:T(8,128)S(1)}, u32[]{:S(2)}, u32[]{:S(2)}) %all-to-all-start) | async-done | bytes 131104 | tf_op jit(solution)/shard_map/all_to_all | solution.py:466
  36.7 0.7 %shard_map.74 = f32[2,3,8,24]{3,2,1,0:T(8,128)} custom-call(f32[4,8,8,128]{3,2,1,0:T(8,128)S(1)} %bitcast.5), custom_call_target="tpu_custom_call" | custom-call | tf_op jit(solution)/shard_map/pallas_call | solution.py:31
  37.4 0.0 collective-permute-done.5.other
  37.4 1.2 %shard_map.72 = bf16[2,24,8,288]{3,2,1,0:T(8,128)(2,1)} custom-call(bf16[48,1152]{1,0:T(8,128)(2,1)S(1)} %get-tuple-element.28.mine, bf16[48,1152]{1,0:T(8,128)(2,1)S(1)} %collective-permute-done.5.other, bf16[384,384]{1,0:T(8,128)(2,1)S(1)} %get-tuple-element.30.perm_ref), custom_call_target="tpu_custom_call" | custom-call | tf_op jit(solution)/shard_map/pallas_call | solution.py:31
  (5 shorter events, 0.0 us)
Async XLA Ops:
  0.6 1.0 %copy-start = (bf16[2,24,8,288]{3,2,1,0:T(8,128)(2,1)S(1)}, bf16[2,24,8,288]{3,2,1,0:T(8,128)(2,1)}, u32[]{:S(2)}) copy-start(bf16[2,24,8,288]{3,2,1,0:T(8,128)(2,1)} %g_hbm.1) | copy-start | bytes 663556
  1.6 1.0 %copy-start.1 = (bf16[2,24,8,288]{3,2,1,0:T(8,128)(2,1)S(1)}, bf16[2,24,8,288]{3,2,1,0:T(8,128)(2,1)}, u32[]{:S(2)}) copy-start(bf16[2,24,8,288]{3,2,1,0:T(8,128)(2,1)} %b_hbm.1) | copy-start | bytes 663556
  3.7 5.3 %collective-permute-start = (bf16[48,1152]{1,0:T(8,128)(2,1)S(1)}, bf16[48,1152]{1,0:T(8,128)(2,1)S(1)}, u32[]{:S(2)}, u32[]{:S(2)}) collective-permute-start(bf16[48,1152]{1,0:T(8,128)(2,1)S(1)} %get-tuple-element.20), channel_id=1, source_target_pairs={{0,8},{1,9},{2,10},{3,11},{4,12},{5,13},{6,14},{7,15},{8,0},{9,1},... | collective-permute-start | bytes 331784 | tf_op jit(solution)/shard_map/ppermute | solution.py:407
  4.2 10.9 %collective-permute-start.1 = (bf16[48,1152]{1,0:T(8,128)(2,1)S(1)}, bf16[48,1152]{1,0:T(8,128)(2,1)S(1)}, u32[]{:S(2)}, u32[]{:S(2)}) collective-permute-start(bf16[48,1152]{1,0:T(8,128)(2,1)S(1)} %get-tuple-element.19.refs_0_), channel_id=1, source_target_pairs={{0,16},{1,17},{2,18},{3,19},{4,20},{5,21},{6,22},{7,23},{8,24},{9,... | collective-permute-start | bytes 331784 | tf_op jit(solution)/shard_map/ppermute | solution.py:407
  6.8 8.3 %collective-permute-start.2 = (bf16[48,1152]{1,0:T(8,128)(2,1)S(1)}, bf16[48,1152]{1,0:T(8,128)(2,1)S(1)}, u32[]{:S(2)}, u32[]{:S(2)}) collective-permute-start(bf16[48,1152]{1,0:T(8,128)(2,1)S(1)} %get-tuple-element.20), channel_id=1, source_target_pairs={{0,24},{1,25},{2,26},{3,27},{4,28},{5,29},{6,30},{7,31},{8,16},{9,... | collective-permute-start | bytes 331784 | tf_op jit(solution)/shard_map/ppermute | solution.py:407
  6.9 16.8 %collective-permute-start.6 = (bf16[48,1152]{1,0:T(8,128)(2,1)S(1)}, bf16[48,1152]{1,0:T(8,128)(2,1)S(1)}, u32[]{:S(2)}, u32[]{:S(2)}) collective-permute-start(bf16[48,1152]{1,0:T(8,128)(2,1)S(1)} %get-tuple-element.32), channel_id=1, source_target_pairs={{0,8},{1,9},{2,10},{3,11},{4,12},{5,13},{6,14},{7,15},{8,0},{9,1},... | collective-permute-start | bytes 331784 | tf_op jit(solution)/shard_map/ppermute | solution.py:407
  7.0 16.7 %collective-permute-start.7 = (bf16[48,1152]{1,0:T(8,128)(2,1)S(1)}, bf16[48,1152]{1,0:T(8,128)(2,1)S(1)}, u32[]{:S(2)}, u32[]{:S(2)}) collective-permute-start(bf16[48,1152]{1,0:T(8,128)(2,1)S(1)} %get-tuple-element.31.b_own), channel_id=1, source_target_pairs={{0,1},{1,2},{2,3},{3,4},{4,5},{5,6},{6,7},{7,0},{8,9},{9,10},{10,1... | collective-permute-start | bytes 331784 | tf_op jit(solution)/shard_map/ppermute | solution.py:407
  9.0 14.7 %collective-permute-start.8 = (bf16[48,1152]{1,0:T(8,128)(2,1)S(1)}, bf16[48,1152]{1,0:T(8,128)(2,1)S(1)}, u32[]{:S(2)}, u32[]{:S(2)}) collective-permute-start(bf16[48,1152]{1,0:T(8,128)(2,1)S(1)} %get-tuple-element.32), channel_id=1, source_target_pairs={{0,9},{1,10},{2,11},{3,12},{4,13},{5,14},{6,15},{7,8},{8,1},{9,2},... | collective-permute-start | bytes 331784 | tf_op jit(solution)/shard_map/ppermute | solution.py:407
  10.0 0.9 %copy-start.2 = (bf16[2,8,24,3,8]{2,4,3,1,0:T(8,128)(2,1)S(1)}, bf16[2,8,24,3,8]{2,4,3,1,0:T(8,128)(2,1)}, u32[]{:S(2)}) copy-start(bf16[2,8,24,3,8]{2,4,3,1,0:T(8,128)(2,1)} %param.9) | copy-start | bytes 55300
  10.9 0.7 %copy-start.3 = (f32[2,3,144]{2,0,1:T(2,128)S(1)}, f32[2,3,144]{2,0,1:T(2,128)}, u32[]{:S(2)}) copy-start(f32[2,3,144]{2,0,1:T(2,128)} %param.7) | copy-start | bytes 10372
  11.6 0.7 %copy-start.4 = (s32[2,4]{1,0:T(2,128)S(1)}, s32[2,4]{1,0:T(2,128)}, u32[]{:S(2)}) copy-start(s32[2,4]{1,0:T(2,128)} %near_hbm.1) | copy-start | bytes 100
  18.9 11.9 %collective-permute-start.3 = (bf16[2,48,1152]{2,1,0:T(8,128)(2,1)S(1)}, bf16[2,48,1152]{2,1,0:T(8,128)(2,1)S(1)}, u32[]{:S(2)}, u32[]{:S(2)}) collective-permute-start(bf16[2,48,1152]{2,1,0:T(8,128)(2,1)S(1)} %get-tuple-element.26), channel_id=1, source_target_pairs={{0,1},{1,2},{2,3},{3,4},{4,5},{5,6},{6,7},{7,0},{8,9},{9,10},{10,1... | collective-permute-start | bytes 663560 | tf_op jit(solution)/shard_map/ppermute | solution.py:407
  20.4 12.7 %collective-permute-start.4 = (bf16[2,48,1152]{2,1,0:T(8,128)(2,1)S(1)}, bf16[2,48,1152]{2,1,0:T(8,128)(2,1)S(1)}, u32[]{:S(2)}, u32[]{:S(2)}) collective-permute-start(bf16[2,48,1152]{2,1,0:T(8,128)(2,1)S(1)} %get-tuple-element.27), channel_id=1, source_target_pairs={{0,7},{1,0},{2,1},{3,2},{4,3},{5,4},{6,5},{7,6},{8,15},{9,8},{10,9... | collective-permute-start | bytes 663560 | tf_op jit(solution)/shard_map/ppermute | solution.py:407
  26.4 10.3 %all-to-all-start = ((f32[32,8,128]{2,1,0:T(8,128)}), f32[32,8,128]{2,1,0:T(8,128)S(1)}, u32[]{:S(2)}, u32[]{:S(2)}) async-start(f32[32,8,128]{2,1,0:T(8,128)} %bitcast.2), calls=%async_computation | async-start | bytes 262144 | tf_op jit(solution)/shard_map/all_to_all | solution.py:466
  33.2 4.2 %collective-permute-start.5 = (bf16[48,1152]{1,0:T(8,128)(2,1)S(1)}, bf16[48,1152]{1,0:T(8,128)(2,1)S(1)}, u32[]{:S(2)}, u32[]{:S(2)}) collective-permute-start(bf16[48,1152]{1,0:T(8,128)(2,1)S(1)} %get-tuple-element.29), channel_id=1, source_target_pairs={{0,8},{1,9},{2,10},{3,11},{4,12},{5,13},{6,14},{7,15},{8,0},{9,1},... | collective-permute-start | bytes 331784 | tf_op jit(solution)/shard_map/ppermute | solution.py:407
where the time goes:
time: 38.9 us; the launch traced here: 38.6 us
  starting transfers between devices  13.7 us (35%)
  Pallas kernels  12.4 us (32%)
  waiting for transfers between devices  7.59 us (20%)
  local copies, waits for them, and re-layouts  4.18 us (11%)
  between operations  0.71 us (2%)
    pallas_call x7, Pallas kernels, call(): pl.pallas_call(kernel, out_shape=outs, in_specs=specs or [VMEM] * len(ins...  12.4 us
    ppermute x9, starting transfers between devices, move(): return lax.ppermute(value, ('mom', 'en'), links)  11.1 us
    ppermute x9, waiting for transfers between devices, move(): return lax.ppermute(value, ('mom', 'en'), links)  4.18 us
    unnamed x10, local copies, waits for them, and re-layouts  4.18 us
    all_to_all x1, waiting for transfers between devices, body(): lax.all_to_all(partial.reshape(mom * en, local_k * half, LANES), ('mom',...  3.41 us
    all_to_all x1, starting transfers between devices, body(): lax.all_to_all(partial.reshape(mom * en, local_k * half, LANES), ('mom',...  2.58 us
  transfers between devices with their start and end apart: 10, of which 3 were waited for; matrix products, arithmetic and copies ran while one was open for 0% of the time, Pallas kernels for 26%

commit v1 on v0

--- a/solution.py
+++ b/solution.py
@@ -16,7 +16,7 @@
 HIGHEST = lax.Precision.HIGHEST
 VMEM = pl.BlockSpec(memory_space=pltpu.VMEM)
 HBM = pl.BlockSpec(memory_space=pltpu.HBM)
-PARAMS = pltpu.CompilerParams(vmem_limit_bytes=24 * 1024 * 1024)
+MIB = 1024 * 1024
 
 
 def dot(a, b):
@@ -27,14 +27,15 @@
     return lax.dot_general(a, b, (((1,), (1,)), ((), ())), preferred_element_type=F32)
 
 
-def call(kernel, outs, ins, scratch=(), specs=None):
+def call(kernel, outs, ins, work, scratch=(), specs=None, limit=24):
     return pl.pallas_call(
         kernel,
         out_shape=outs,
         in_specs=specs or [VMEM] * len(ins),
         out_specs=[VMEM] * len(outs),
         scratch_shapes=list(scratch),
-        compiler_params=PARAMS,
+        compiler_params=pltpu.CompilerParams(vmem_limit_bytes=int(limit * MIB)),
+        cost_estimate=pl.CostEstimate(flops=int(work * 1e9), bytes_accessed=0, transcendentals=0),
     )(*ins)
 
 
@@ -83,13 +84,9 @@
 
 
 def table_kernel(
-    near_hbm, deriv_hbm, phonon_hbm, hi_ref, lo_ref, t_ref, perm_ref, join_ref, turn_ref, sort_ref,
-    near_ref, deriv_ref, phonon_ref, factors, bases, sems, *, half, local_k, local_e,
+    near_ref, deriv_ref, phonon_ref, hi_ref, lo_ref, t_ref, perm_ref, join_ref, turn_ref, sort_ref,
+    factors, bases, *, half, local_k, local_e,
 ):
-    copies = []
-    for i, (src, dst) in enumerate(((near_hbm, near_ref), (deriv_hbm, deriv_ref), (phonon_hbm, phonon_ref))):
-        copies.append(pltpu.make_async_copy(src, dst, sems.at[i]))
-        copies[-1].start()
     core = my_core()
     _, momenta, _, pairs, window = phonon_ref.shape
     size = NO * NO
@@ -124,8 +121,6 @@
     rows_r = ones_at(inner == slot)
     x = (16, size)
     mask = (split(index(x, 1), NO)[1] == index(x, 0)).astype(F32)
-    for copy in copies:
-        copy.wait()
     atoms = deriv_ref.shape[1]
     spread = []
     for m in range(3):
@@ -336,7 +331,7 @@
             out_ref[t, e] = tile
 
 
-def total_kernel(in_ref, out_ref, *, half):
+def total_kernel(in_ref, after_ref, out_ref, *, half):
     targets, en = in_ref.shape[:2]
     local_k, _, _, window = out_ref.shape
     sums = []
@@ -358,7 +353,7 @@
         out[...] = (own[i] + below[i].astype(F32) + above[i].astype(F32)).astype(BF)
 
 
-def join_kernel(mine, other, perm_ref, out_ref, halves):
+def join_kernel(mine, other, perm_ref, out_ref, mark_ref, halves):
     core = my_core()
     pairs = out_ref.shape[2]
     entries = out_ref.shape[3]
@@ -370,6 +365,7 @@
         begin = entries * (p % half)
         parts.append(halves[p // half][:, begin : begin + entries])
     stacked = jnp.concatenate(parts, axis=0).astype(BF)
+    mark_ref[...] = jnp.zeros(mark_ref.shape, F32)
     out_ref[...] = dot(perm_ref[...], stacked).astype(BF).reshape(out_ref.shape)
 
 
@@ -385,17 +381,21 @@
     total_e = local_e * en
     size = NO * NO
 
+    deriv = derivative.transpose(1, 0, 2)
+    weights = phonon.transpose(0, 1, 3, 4, 2)
     g_own, b_own, g_far, b_far = call(
         pack_kernel,
         [shape((rows, width), BF)] * 4,
         [green_less, green_greater],
+        1.5,
         [
             pltpu.VMEM(green_less.shape, BF),
             pltpu.VMEM(green_less.shape, BF),
             pltpu.VMEM((2, rows, width), F32),
             pltpu.SemaphoreType.DMA((2,)),
         ],
-        [HBM, HBM],
+        [HBM] * 2,
+        limit=53.25,
     )
 
     def move(value, dchip, dcore, de):
@@ -414,8 +414,6 @@
     prev_far = move(b_far, 0, 1, 1)
 
     near = neighbours.astype(jnp.int32)
-    deriv = derivative.transpose(1, 0, 2)
-    weights = phonon.transpose(0, 1, 3, 4, 2)
     columns = -(-chip_k * 2 * local_e // LANES) * LANES
     k_hi, k_lo, toeplitz, to_energy, to_rows, turn, sort_e = call(
         functools.partial(table_kernel, half=half, local_k=local_k, local_e=local_e),
@@ -429,15 +427,12 @@
             shape((columns, 2 * chip_k * local_e), BF),
         ],
         [near, deriv, weights],
+        3,
         [
-            pltpu.SMEM(near.shape, jnp.int32),
-            pltpu.VMEM(deriv.shape, F32),
-            pltpu.VMEM(weights.shape, BF),
             pltpu.VMEM((3 * atoms, 32, 4 * LANES), F32),
             pltpu.VMEM((chip_k, 3, pairs, 4 * local_e * momenta), F32),
-            pltpu.SemaphoreType.DMA((3,)),
         ],
-        [HBM, HBM, HBM],
+        [pl.BlockSpec(memory_space=pltpu.SMEM), VMEM, VMEM],
     )
 
     g1, own, low, up = call(
@@ -449,6 +444,7 @@
             shape((2, rows, width), BF),
         ],
         blocks + [to_energy, k_hi, k_lo, toeplitz],
+        4,
         [pltpu.VMEM((2 * chips, rows, width), BF), pltpu.VMEM((6, rows, width), F32)],
     )
     from_above = move(low, 0, 0, -1)
@@ -461,28 +457,30 @@
         ),
         [shape((mom, en, local_k * half, LANES), F32)],
         [b_own, b_core, prev_own, prev_far, turn, sort_e, g1],
+        3,
         [pltpu.VMEM((4, rows, width), BF)],
     )
     terms = lax.all_to_all(
         partial.reshape(mom * en, local_k * half, LANES), ("mom", "en"), split_axis=0, concat_axis=0, tiled=True
+    )
+    mine, theirs = call(
+        sum_kernel, [shape((rows, width), BF)] * 2, [own, from_below, from_above], 0.1
+    )
+    other = move(theirs, 0, 1, 0)
+    self_energy, mark = call(
+        join_kernel,
+        [shape(green_less.shape, BF), shape((8, LANES), F32)],
+        [mine, other, to_rows],
+        1,
+        [pltpu.VMEM((2, rows, width), F32)],
     )
     (polar,) = call(
         functools.partial(total_kernel, half=half),
         [shape((local_k, 3, pairs, window), F32)],
-        [terms.reshape(mom, en, local_k * half, LANES)],
+        [terms.reshape(mom, en, local_k * half, LANES), mark],
+        0.5,
     )
     polar = polar.transpose(0, 3, 1, 2)
-
-    mine, theirs = call(
-        sum_kernel, [shape((rows, width), BF)] * 2, [own, from_below, from_above]
-    )
-    other = move(theirs, 0, 1, 0)
-    (self_energy,) = call(
-        join_kernel,
-        [shape(green_less.shape, BF)],
-        [mine, other, to_rows],
-        [pltpu.VMEM((2, rows, width), F32)],
-    )
     return (self_energy, polar)
 
 

time: 38.9 us -> 35.1 us (0.902)
  local copies, waits for them, and re-layouts: 4.18 us -> 0.01 us
  waiting for transfers between devices: 7.59 us -> 6.41 us
  Pallas kernels: 12.4 us -> 13.4 us
  starting transfers between devices: 13.7 us -> 14.4 us
    unnamed x10 -> x6, local copies, waits for them, and re-layouts: 4.18 us -> 0.01 us
    all_to_all x1, waiting for transfers between devices: 3.41 us -> 2.4 us  [body(): lax.all_to_all(partial.reshape(mom * en, local_k * half, LANES), ('mom',...]
    pallas_call x7, Pallas kernels: 12.4 us -> 13.4 us  [call(): pl.pallas_call(kernel, out_shape=outs, in_specs=specs or [VMEM] * len(ins...]
    ppermute x9, starting transfers between devices: 11.1 us -> 11.7 us  [move(): return lax.ppermute(value, ('mom', 'en'), links)]
  transfers between devices with their start and end apart: 10 -> 10, of which waited for: 3 -> 4; matrix products, arithmetic and copies ran while one was open for 0% -> 0% of each run, Pallas kernels for 26% -> 31%
where the time goes in v1:
time: 35.1 us; the launch traced here: 34.9 us
  starting transfers between devices  14.4 us (41%)
  Pallas kernels  13.4 us (38%)
  waiting for transfers between devices  6.41 us (18%)
  between operations  0.72 us (2%)
    pallas_call x7, Pallas kernels, call(): pl.pallas_call(kernel, out_shape=outs, in_specs=specs or [VMEM] * len(ins...  13.4 us
    ppermute x9, starting transfers between devices, move(): return lax.ppermute(value, ('mom', 'en'), links)  11.7 us
    ppermute x9, waiting for transfers between devices, move(): return lax.ppermute(value, ('mom', 'en'), links)  4 us
    all_to_all x1, starting transfers between devices, body(): lax.all_to_all(partial.reshape(mom * en, local_k * half, LANES), ('mom',...  2.65 us
    all_to_all x1, waiting for transfers between devices, body(): lax.all_to_all(partial.reshape(mom * en, local_k * half, LANES), ('mom',...  2.4 us
  transfers between devices with their start and end apart: 10, of which 4 were waited for; matrix products, arithmetic and copies ran while one was open for 0% of the time, Pallas kernels for 31%

profile of v1, /device:TPU:0, one launch (start us, length us, event | category | flops | bytes accessed | tf_op | source)
XLA Modules:
  0.0 34.9 jit_solution(9120575986804520892)
XLA Ops:
  0.6 0.0 copy-start.1
  0.6 0.0 copy-start
  0.7 0.0 copy-start.2
  0.7 2.0 %shard_map.68 = (bf16[48,1152]{1,0:T(8,128)(2,1)S(1)}, bf16[48,1152]{1,0:T(8,128)(2,1)S(1)}, bf16[48,1152]{1,0:T(8,128)(2,1)S(1)}, bf16[48,1152]{1,0:T(8,128)(2,1)S(1)}) custom-call(bf16[2,24,8,288]{3,2,1,0:T(8,128)(2,1)} %g_hbm.1, bf16[2,24,8,288]{3,2,1,0:T(8,128)(2,1)} %b_hbm.1), custom_call_target="tpu_custom_call" | custom-call | flops 1500000000 | tf_op jit(solution)/shard_map/pallas_call | solution.py:31
  2.7 0.5 %collective-permute-start = (bf16[48,1152]{1,0:T(8,128)(2,1)S(1)}, bf16[48,1152]{1,0:T(8,128)(2,1)S(1)}, u32[]{:S(2)}, u32[]{:S(2)}) collective-permute-start(bf16[48,1152]{1,0:T(8,128)(2,1)S(1)} %get-tuple-element.22), channel_id=1, source_target_pairs={{0,8},{1,9},{2,10},{3,11},{4,12},{5,13},{6,14},{7,15},{8,0},{9,1},... | collective-permute-start | bytes 331784 | tf_op jit(solution)/shard_map/ppermute | solution.py:407
  3.2 2.6 %collective-permute-start.2 = (bf16[48,1152]{1,0:T(8,128)(2,1)S(1)}, bf16[48,1152]{1,0:T(8,128)(2,1)S(1)}, u32[]{:S(2)}, u32[]{:S(2)}) collective-permute-start(bf16[48,1152]{1,0:T(8,128)(2,1)S(1)} %get-tuple-element.22), channel_id=1, source_target_pairs={{0,24},{1,25},{2,26},{3,27},{4,28},{5,29},{6,30},{7,31},{8,16},{9,... | collective-permute-start | bytes 331784 | tf_op jit(solution)/shard_map/ppermute | solution.py:407
  5.8 0.1 collective-permute-start.6
  5.9 1.6 %collective-permute-start.8 = (bf16[48,1152]{1,0:T(8,128)(2,1)S(1)}, bf16[48,1152]{1,0:T(8,128)(2,1)S(1)}, u32[]{:S(2)}, u32[]{:S(2)}) collective-permute-start(bf16[48,1152]{1,0:T(8,128)(2,1)S(1)} %get-tuple-element.35), channel_id=1, source_target_pairs={{0,9},{1,10},{2,11},{3,12},{4,13},{5,14},{6,15},{7,8},{8,1},{9,2},... | collective-permute-start | bytes 331784 | tf_op jit(solution)/shard_map/ppermute | solution.py:407
  7.5 0.5 %collective-permute-start.1 = (bf16[48,1152]{1,0:T(8,128)(2,1)S(1)}, bf16[48,1152]{1,0:T(8,128)(2,1)S(1)}, u32[]{:S(2)}, u32[]{:S(2)}) collective-permute-start(bf16[48,1152]{1,0:T(8,128)(2,1)S(1)} %get-tuple-element.21.refs_0_), channel_id=1, source_target_pairs={{0,16},{1,17},{2,18},{3,19},{4,20},{5,21},{6,22},{7,23},{8,24},{9,... | collective-permute-start | bytes 331784 | tf_op jit(solution)/shard_map/ppermute | solution.py:407
  8.0 0.0 copy-done.1
  8.0 0.0 copy-done.2
  8.0 2.9 %shard_map.69 = (bf16[24,144,256]{2,1,0:T(8,128)(2,1)S(1)}, bf16[24,144,256]{2,1,0:T(8,128)(2,1)S(1)}, bf16[12,288,256]{2,1,0:T(8,128)(2,1)S(1)}, bf16[192,192]{...) custom-call(s32[2,4]{1,0:T(2,128)S(1)} %copy-done.2, ...), custom_call_target="tpu_custom_call" | custom-call | flops 3000000000 | tf_op jit(solution)/shard_map/pallas_call | solution.py:31
  10.9 0.0 collective-permute-done.refs_1_
  11.0 1.6 %collective-permute-start.7 = (bf16[48,1152]{1,0:T(8,128)(2,1)S(1)}, bf16[48,1152]{1,0:T(8,128)(2,1)S(1)}, u32[]{:S(2)}, u32[]{:S(2)}) collective-permute-start(bf16[48,1152]{1,0:T(8,128)(2,1)S(1)} %get-tuple-element.34.b_own), channel_id=1, source_target_pairs={{0,1},{1,2},{2,3},{3,4},{4,5},{5,6},{6,7},{7,0},{8,9},{9,10},{10,1... | collective-permute-start | bytes 331784 | tf_op jit(solution)/shard_map/ppermute | solution.py:407
  12.5 0.0 collective-permute-done.1.refs_2_
  12.5 0.0 collective-permute-done.2.refs_3_
  12.5 3.7 %shard_map.70 = (bf16[3,192,1152]{2,1,0:T(8,128)(2,1)S(1)}, f32[2,48,1152]{2,1,0:T(8,128)S(1)}, bf16[2,48,1152]{2,1,0:T(8,128)(2,1)S(1)}, bf16[2,48,1152]{2,1,0:T(8,128)(2,1)S(1)}) custom-call(bf16[48,1152]{1,0:T(8,128)(2,1)S(1)} %get-tuple-element.21.refs_0_, bf16[48,1152]{1,0:T(8,128)(2,1)S(1)} %collective-permute-done.refs_1_, ...), custom_call_target="tpu_custom_call" | custom-call | flops 4000000000 | tf_op jit(solution)/shard_map/pallas_call | solution.py:31
  16.3 1.6 %collective-permute-start.3 = (bf16[2,48,1152]{2,1,0:T(8,128)(2,1)S(1)}, bf16[2,48,1152]{2,1,0:T(8,128)(2,1)S(1)}, u32[]{:S(2)}, u32[]{:S(2)}) collective-permute-start(bf16[2,48,1152]{2,1,0:T(8,128)(2,1)S(1)} %get-tuple-element.28), channel_id=1, source_target_pairs={{0,1},{1,2},{2,3},{3,4},{4,5},{5,6},{6,7},{7,0},{8,9},{9,10},{10,1... | collective-permute-start | bytes 663560 | tf_op jit(solution)/shard_map/ppermute | solution.py:407
  17.8 3.2 %collective-permute-start.4 = (bf16[2,48,1152]{2,1,0:T(8,128)(2,1)S(1)}, bf16[2,48,1152]{2,1,0:T(8,128)(2,1)S(1)}, u32[]{:S(2)}, u32[]{:S(2)}) collective-permute-start(bf16[2,48,1152]{2,1,0:T(8,128)(2,1)S(1)} %get-tuple-element.29), channel_id=1, source_target_pairs={{0,7},{1,0},{2,1},{3,2},{4,3},{5,4},{6,5},{7,6},{8,15},{9,8},{10,9... | collective-permute-start | bytes 663560 | tf_op jit(solution)/shard_map/ppermute | solution.py:407
  21.1 0.0 collective-permute-done.6.b_far
  21.1 0.0 collective-permute-done.7.prev_own
  21.1 0.0 collective-permute-done.8.prev_far
  21.1 2.7 %shard_map.73 = f32[4,8,8,128]{3,2,1,0:T(8,128)} custom-call(bf16[48,1152]{1,0:T(8,128)(2,1)S(1)} %get-tuple-element.34.b_own, bf16[48,1152]{1,0:T(8,128)(2,1)S(1)} %collective-permute-done.6.b_far, bf16[48,1152]{1,0:T(8,128)(2,1)S(1)} %collective-permute-done.7.prev_own, bf16[48,1152]{1,0:T(8,128)(2,1)S(1)} %collective-permute-done.8.prev_far, ...), custom_call_target="tpu_custom_call" | custom-call | flops 3000000000 | tf_op jit(solution)/shard_map/pallas_call | solution.py:31
  23.8 2.7 %all-to-all-start = ((f32[32,8,128]{2,1,0:T(8,128)}), f32[32,8,128]{2,1,0:T(8,128)S(1)}, u32[]{:S(2)}, u32[]{:S(2)}) async-start(f32[32,8,128]{2,1,0:T(8,128)} %bitcast.2), calls=%async_computation | async-start | bytes 262144 | tf_op jit(solution)/shard_map/all_to_all | solution.py:463
  26.5 0.5 %collective-permute-done.3.below = bf16[2,48,1152]{2,1,0:T(8,128)(2,1)S(1)} collective-permute-done((bf16[2,48,1152]{2,1,0:T(8,128)(2,1)S(1)}, bf16[2,48,1152]{2,1,0:T(8,128)(2,1)S(1)}, u32[]{:S(2)}, u32[]{:S(2)}) %collective-permute-start.3) | collective-permute-done | bytes 221216 | tf_op jit(solution)/shard_map/ppermute | solution.py:407
  27.0 2.2 %collective-permute-done.4.above = bf16[2,48,1152]{2,1,0:T(8,128)(2,1)S(1)} collective-permute-done((bf16[2,48,1152]{2,1,0:T(8,128)(2,1)S(1)}, bf16[2,48,1152]{2,1,0:T(8,128)(2,1)S(1)}, u32[]{:S(2)}, u32[]{:S(2)}) %collective-permute-start.4) | collective-permute-done | bytes 221216 | tf_op jit(solution)/shard_map/ppermute | solution.py:407
  29.2 0.1 shard_map.71
  29.2 0.1 collective-permute-start.5
  29.3 1.3 %collective-permute-done.5.other = bf16[48,1152]{1,0:T(8,128)(2,1)S(1)} collective-permute-done((bf16[48,1152]{1,0:T(8,128)(2,1)S(1)}, bf16[48,1152]{1,0:T(8,128)(2,1)S(1)}, u32[]{:S(2)}, u32[]{:S(2)}) %collective-permute-start.5) | collective-permute-done | bytes 110624 | tf_op jit(solution)/shard_map/ppermute | solution.py:407
  30.6 1.2 %shard_map.72 = (bf16[2,24,8,288]{3,2,1,0:T(8,128)(2,1)}, f32[8,128]{1,0:T(8,128)S(1)}) custom-call(bf16[48,1152]{1,0:T(8,128)(2,1)S(1)} %get-tuple-element.30.mine, bf16[48,1152]{1,0:T(8,128)(2,1)S(1)} %collective-permute-done.5.other, bf16[384,384]{1,0:T(8,128)(2,1)S(1)} %get-tuple-element.32.perm_ref), custom_call_target="tpu_custom_call" | custom-call | flops 1000000000 | tf_op jit(solution)/shard_map/pallas_call | solution.py:31
  31.8 2.4 %all-to-all-done = f32[32,8,128]{2,1,0:T(8,128)S(1)} async-done(((f32[32,8,128]{2,1,0:T(8,128)}), f32[32,8,128]{2,1,0:T(8,128)S(1)}, u32[]{:S(2)}, u32[]{:S(2)}) %all-to-all-start) | async-done | bytes 131104 | tf_op jit(solution)/shard_map/all_to_all | solution.py:463
  34.2 0.7 %shard_map.74 = f32[2,3,8,24]{3,2,1,0:T(8,128)} custom-call(f32[4,8,8,128]{3,2,1,0:T(8,128)S(1)} %bitcast.5, f32[8,128]{1,0:T(8,128)S(1)} %get-tuple-element.39.after_ref), custom_call_target="tpu_custom_call" | custom-call | flops 500000000 | tf_op jit(solution)/shard_map/pallas_call | solution.py:31
  (1 shorter events, 0.0 us)
Async XLA Ops:
  0.6 7.4 %copy-start.1 = (f32[2,3,144]{2,0,1:T(2,128)S(1)}, f32[2,3,144]{2,0,1:T(2,128)}, u32[]{:S(2)}) copy-start(f32[2,3,144]{2,0,1:T(2,128)} %param.7) | copy-start | bytes 10372
  0.6 7.4 %copy-start = (bf16[2,8,24,3,8]{2,4,3,1,0:T(8,128)(2,1)S(1)}, bf16[2,8,24,3,8]{2,4,3,1,0:T(8,128)(2,1)}, u32[]{:S(2)}) copy-start(bf16[2,8,24,3,8]{2,4,3,1,0:T(8,128)(2,1)} %param.9) | copy-start | bytes 55300
  0.7 7.4 %copy-start.2 = (s32[2,4]{1,0:T(2,128)S(1)}, s32[2,4]{1,0:T(2,128)}, u32[]{:S(2)}) copy-start(s32[2,4]{1,0:T(2,128)} %near_ref.1) | copy-start | bytes 100
  2.7 8.2 %collective-permute-start = (bf16[48,1152]{1,0:T(8,128)(2,1)S(1)}, bf16[48,1152]{1,0:T(8,128)(2,1)S(1)}, u32[]{:S(2)}, u32[]{:S(2)}) collective-permute-start(bf16[48,1152]{1,0:T(8,128)(2,1)S(1)} %get-tuple-element.22), channel_id=1, source_target_pairs={{0,8},{1,9},{2,10},{3,11},{4,12},{5,13},{6,14},{7,15},{8,0},{9,1},... | collective-permute-start | bytes 331784 | tf_op jit(solution)/shard_map/ppermute | solution.py:407
  3.2 9.3 %collective-permute-start.2 = (bf16[48,1152]{1,0:T(8,128)(2,1)S(1)}, bf16[48,1152]{1,0:T(8,128)(2,1)S(1)}, u32[]{:S(2)}, u32[]{:S(2)}) collective-permute-start(bf16[48,1152]{1,0:T(8,128)(2,1)S(1)} %get-tuple-element.22), channel_id=1, source_target_pairs={{0,24},{1,25},{2,26},{3,27},{4,28},{5,29},{6,30},{7,31},{8,16},{9,... | collective-permute-start | bytes 331784 | tf_op jit(solution)/shard_map/ppermute | solution.py:407
  5.8 15.2 %collective-permute-start.6 = (bf16[48,1152]{1,0:T(8,128)(2,1)S(1)}, bf16[48,1152]{1,0:T(8,128)(2,1)S(1)}, u32[]{:S(2)}, u32[]{:S(2)}) collective-permute-start(bf16[48,1152]{1,0:T(8,128)(2,1)S(1)} %get-tuple-element.35), channel_id=1, source_target_pairs={{0,8},{1,9},{2,10},{3,11},{4,12},{5,13},{6,14},{7,15},{8,0},{9,1},... | collective-permute-start | bytes 331784 | tf_op jit(solution)/shard_map/ppermute | solution.py:407
  5.9 15.2 %collective-permute-start.8 = (bf16[48,1152]{1,0:T(8,128)(2,1)S(1)}, bf16[48,1152]{1,0:T(8,128)(2,1)S(1)}, u32[]{:S(2)}, u32[]{:S(2)}) collective-permute-start(bf16[48,1152]{1,0:T(8,128)(2,1)S(1)} %get-tuple-element.35), channel_id=1, source_target_pairs={{0,9},{1,10},{2,11},{3,12},{4,13},{5,14},{6,15},{7,8},{8,1},{9,2},... | collective-permute-start | bytes 331784 | tf_op jit(solution)/shard_map/ppermute | solution.py:407
  7.5 5.1 %collective-permute-start.1 = (bf16[48,1152]{1,0:T(8,128)(2,1)S(1)}, bf16[48,1152]{1,0:T(8,128)(2,1)S(1)}, u32[]{:S(2)}, u32[]{:S(2)}) collective-permute-start(bf16[48,1152]{1,0:T(8,128)(2,1)S(1)} %get-tuple-element.21.refs_0_), channel_id=1, source_target_pairs={{0,16},{1,17},{2,18},{3,19},{4,20},{5,21},{6,22},{7,23},{8,24},{9,... | collective-permute-start | bytes 331784 | tf_op jit(solution)/shard_map/ppermute | solution.py:407
  11.0 10.1 %collective-permute-start.7 = (bf16[48,1152]{1,0:T(8,128)(2,1)S(1)}, bf16[48,1152]{1,0:T(8,128)(2,1)S(1)}, u32[]{:S(2)}, u32[]{:S(2)}) collective-permute-start(bf16[48,1152]{1,0:T(8,128)(2,1)S(1)} %get-tuple-element.34.b_own), channel_id=1, source_target_pairs={{0,1},{1,2},{2,3},{3,4},{4,5},{5,6},{6,7},{7,0},{8,9},{9,10},{10,1... | collective-permute-start | bytes 331784 | tf_op jit(solution)/shard_map/ppermute | solution.py:407
  16.3 10.7 %collective-permute-start.3 = (bf16[2,48,1152]{2,1,0:T(8,128)(2,1)S(1)}, bf16[2,48,1152]{2,1,0:T(8,128)(2,1)S(1)}, u32[]{:S(2)}, u32[]{:S(2)}) collective-permute-start(bf16[2,48,1152]{2,1,0:T(8,128)(2,1)S(1)} %get-tuple-element.28), channel_id=1, source_target_pairs={{0,1},{1,2},{2,3},{3,4},{4,5},{5,6},{6,7},{7,0},{8,9},{9,10},{10,1... | collective-permute-start | bytes 663560 | tf_op jit(solution)/shard_map/ppermute | solution.py:407
  17.8 11.3 %collective-permute-start.4 = (bf16[2,48,1152]{2,1,0:T(8,128)(2,1)S(1)}, bf16[2,48,1152]{2,1,0:T(8,128)(2,1)S(1)}, u32[]{:S(2)}, u32[]{:S(2)}) collective-permute-start(bf16[2,48,1152]{2,1,0:T(8,128)(2,1)S(1)} %get-tuple-element.29), channel_id=1, source_target_pairs={{0,7},{1,0},{2,1},{3,2},{4,3},{5,4},{6,5},{7,6},{8,15},{9,8},{10,9... | collective-permute-start | bytes 663560 | tf_op jit(solution)/shard_map/ppermute | solution.py:407
  23.8 10.4 %all-to-all-start = ((f32[32,8,128]{2,1,0:T(8,128)}), f32[32,8,128]{2,1,0:T(8,128)S(1)}, u32[]{:S(2)}, u32[]{:S(2)}) async-start(f32[32,8,128]{2,1,0:T(8,128)} %bitcast.2), calls=%async_computation | async-start | bytes 262144 | tf_op jit(solution)/shard_map/all_to_all | solution.py:463
  29.2 1.4 %collective-permute-start.5 = (bf16[48,1152]{1,0:T(8,128)(2,1)S(1)}, bf16[48,1152]{1,0:T(8,128)(2,1)S(1)}, u32[]{:S(2)}, u32[]{:S(2)}) collective-permute-start(bf16[48,1152]{1,0:T(8,128)(2,1)S(1)} %get-tuple-element.31), channel_id=1, source_target_pairs={{0,8},{1,9},{2,10},{3,11},{4,12},{5,13},{6,14},{7,15},{8,0},{9,1},... | collective-permute-start | bytes 331784 | tf_op jit(solution)/shard_map/ppermute | solution.py:407

commit v2 on v1

--- a/solution.py
+++ b/solution.py
@@ -188,7 +188,7 @@
                     grid[(t, a)] = moved[part][:, start : start + 2 * LANES]
             order = []
             per = local_e // 8
-            for blk in range(3):
+            for blk in (0, 2, 1):
                 for a in range(chip_k):
                     order += [grid[(blk * per + i, a)] for i in range(per)]
             t_ref[p * 3 + m] = jnp.concatenate(order, axis=0).astype(BF)
@@ -198,7 +198,7 @@
     core = my_core()
     blocks = refs[: 2 * chips]
     perm_ref, hi_ref, lo_ref, t_ref = refs[2 * chips : 2 * chips + 4]
-    g1_ref, own_ref, low_ref, up_ref, gathered, result = refs[2 * chips + 4 :]
+    high_ref, rest_ref, pair_ref, next_ref, gathered, result = refs[2 * chips + 4 :]
     for s in range(chips):
         gathered[2 * s + core] = blocks[2 * s][...]
         gathered[2 * s + 1 - core] = blocks[2 * s + 1][...]
@@ -228,24 +228,39 @@
                 tile = start // LANES + i
                 piece = r[:, i * LANES : (i + 1) * LANES]
                 sums[m][tile] = piece if sums[m][tile] is None else sums[m][tile] + piece
-    high = [[None] * tiles for _ in range(3)]
-    low = [[None] * tiles for _ in range(3)]
     for m in range(3):
         for i in range(tiles):
-            high[m][i] = sums[m][i].astype(BF)
-            low[m][i] = (sums[m][i] - high[m][i].astype(F32)).astype(BF)
-            g1_ref[m, :, i * LANES : (i + 1) * LANES] = high[m][i]
+            at = slice(i * LANES, (i + 1) * LANES)
+            high = sums[m][i].astype(BF)
+            high_ref[m, :, at] = high
+            rest_ref[m, :, at] = (sums[m][i] - high.astype(F32)).astype(BF)
+    correlate(t_ref, 0, 4, high_ref, rest_ref, result, entries)
+    place = lax.axis_index("en")
+    odd = lax.rem(place, 2)
+    below = jnp.where(place == 0, 0.0, 1.0)
+    above = jnp.where(place == lax.axis_size("en") - 1, 0.0, 1.0)
+    keep_pair = jnp.where(odd == 1, below, above)
+    keep_next = jnp.where(odd == 1, above, below)
+    for i, c in enumerate((core, 1 - core)):
+        pair_ref[i] = (result[2 - 2 * odd + c] * keep_pair).astype(BF)
+        next_ref[i] = (result[2 * odd + c] * keep_next).astype(BF)
+
+
+def correlate(t_ref, begin_row, count, high_ref, rest_ref, result, entries):
+    _, rows, width = result.shape
+    depth = high_ref.shape[1]
     lane = index((1, LANES), 1)
+    at_rows = slice(begin_row * rows, (begin_row + count) * rows)
     carried = None
-    for p in range(half):
+    for p in range(width // entries):
         begin = entries * p
         first = begin // LANES
         last = (begin + entries - 1) // LANES
         total = None
         for m in range(3):
-            t = t_ref[p * 3 + m][:, :depth]
-            for part in (high, low):
-                term = dot(t, jnp.concatenate(part[m][first : last + 1], axis=1))
+            t = t_ref[p * 3 + m, at_rows, :][:, :depth]
+            for part in (high_ref, rest_ref):
+                term = dot(t, part[m, :, first * LANES : (last + 1) * LANES])
                 total = term if total is None else total + term
         for i in range(first, last + 1):
             tile = total[:, (i - first) * LANES : (i - first + 1) * LANES]
@@ -254,18 +269,15 @@
             if i == last and (begin + entries) % LANES:
                 carried = tile
             else:
-                for r in range(6):
+                for r in range(count):
                     result[r, :, i * LANES : (i + 1) * LANES] = tile[r * rows : (r + 1) * rows]
-    place = lax.axis_index("en")
-    below = jnp.where(place == 0, 0.0, 1.0)
-    above = jnp.where(place == lax.axis_size("en") - 1, 0.0, 1.0)
-    for i, c in enumerate((core, 1 - core)):
-        low_ref[i] = (result[c] * below).astype(BF)
-        own_ref[i] = result[2 + c]
-        up_ref[i] = (result[4 + c] * above).astype(BF)
-
-
-def polar_kernel(b_own, b_far, prev_own, prev_far, turn_ref, sort_ref, g1_ref, out_ref, gathered, *, half, entries, local_k, local_e, scale):
+
+
+def own_kernel(t_ref, high_ref, rest_ref, after_ref, own_ref, *, entries):
+    correlate(t_ref, 4, 2, high_ref, rest_ref, own_ref, entries)
+
+
+def polar_kernel(b_own, b_far, prev_own, prev_far, turn_ref, sort_ref, g1_ref, out_ref, mark_ref, gathered, *, half, entries, local_k, local_e, scale):
     core = my_core()
     present = jnp.where(lax.axis_index("en") == 0, 0.0, 1.0)
     gathered[core] = (prev_own[...].astype(F32) * present).astype(BF)
@@ -289,6 +301,7 @@
     window = local_e
     momenta = g1_ref.shape[1] // local_e
     lane = index((1, LANES), 1)
+    mark_ref[...] = jnp.zeros(mark_ref.shape, F32)
     pieces = []
     for p in range(half):
         begin = entries * p
@@ -348,9 +361,10 @@
             out_ref[i, m] = moved[:, :window]
 
 
-def sum_kernel(own, below, above, mine, theirs):
-    for i, out in enumerate((mine, theirs)):
-        out[...] = (own[i] + below[i].astype(F32) + above[i].astype(F32)).astype(BF)
+def sum_kernel(own, pair, after, mine, theirs):
+    core = my_core()
+    for n, i, out in ((0, core, mine), (1, 1 - core, theirs)):
+        out[...] = (own[i] + pair[n].astype(F32) + after[n].astype(F32)).astype(BF)
 
 
 def join_kernel(mine, other, perm_ref, out_ref, mark_ref, halves):
@@ -398,20 +412,30 @@
         limit=53.25,
     )
 
-    def move(value, dchip, dcore, de):
+    def move(value, dchip, dcore, to=lambda e: e):
         links = []
         for m in range(mom):
             target = ((m // 2 + dchip) % chips) * 2 + (m % 2 if dcore == 0 else 1 - m % 2)
             for e in range(en):
-                links.append((m * en + e, target * en + (e + de) % en))
+                links.append((m * en + e, target * en + to(e)))
         return lax.ppermute(value, ("mom", "en"), links)
 
-    blocks = [g_own, move(g_far, 0, 1, 0)]
+    def onward(e):
+        return (e + 1) % en
+
+    def to_pair(e):
+        return e ^ 1 if e ^ 1 < en else e
+
+    def to_next(e):
+        other = e + 1 if e % 2 else e - 1
+        return other if 0 <= other < en else e
+
+    blocks = [g_own, move(g_far, 0, 1)]
     for s in range(1, chips):
-        blocks += [move(g_own, -s, 0, 0), move(g_far, -s, 1, 0)]
-    b_core = move(b_far, 0, 1, 0)
-    prev_own = move(b_own, 0, 0, 1)
-    prev_far = move(b_far, 0, 1, 1)
+        blocks += [move(g_own, -s, 0), move(g_far, -s, 1)]
+    b_core = move(b_far, 0, 1)
+    prev_own = move(b_own, 0, 0, onward)
+    prev_far = move(b_far, 0, 1, onward)
 
     near = neighbours.astype(jnp.int32)
     columns = -(-chip_k * 2 * local_e // LANES) * LANES
@@ -435,27 +459,26 @@
         [pl.BlockSpec(memory_space=pltpu.SMEM), VMEM, VMEM],
     )
 
-    g1, own, low, up = call(
+    g1, g2, to_pair_rows, to_next_rows = call(
         functools.partial(product_kernel, half=half, entries=entries, chips=chips),
         [
             shape((3, momenta * local_e, width), BF),
-            shape((2, rows, width), F32),
+            shape((3, momenta * local_e, width), BF),
             shape((2, rows, width), BF),
             shape((2, rows, width), BF),
         ],
         blocks + [to_energy, k_hi, k_lo, toeplitz],
         4,
-        [pltpu.VMEM((2 * chips, rows, width), BF), pltpu.VMEM((6, rows, width), F32)],
-    )
-    from_above = move(low, 0, 0, -1)
-    from_below = move(up, 0, 0, 1)
-
-    (partial,) = call(
+        [pltpu.VMEM((2 * chips, rows, width), BF), pltpu.VMEM((4, rows, width), F32)],
+    )
+    from_pair = move(to_pair_rows, 0, 0, to_pair)
+    from_next = move(to_next_rows, 0, 0, to_next)
+    partial, done = call(
         functools.partial(
             polar_kernel, half=half, entries=entries, local_k=local_k, local_e=local_e,
             scale=1.0 / (NO * float(np.sqrt(momenta * total_e))),
         ),
-        [shape((mom, en, local_k * half, LANES), F32)],
+        [shape((mom, en, local_k * half, LANES), F32), shape((8, LANES), F32)],
         [b_own, b_core, prev_own, prev_far, turn, sort_e, g1],
         3,
         [pltpu.VMEM((4, rows, width), BF)],
@@ -463,10 +486,14 @@
     terms = lax.all_to_all(
         partial.reshape(mom * en, local_k * half, LANES), ("mom", "en"), split_axis=0, concat_axis=0, tiled=True
     )
+    (own,) = call(
+        functools.partial(own_kernel, entries=entries), [shape((2, rows, width), F32)], [toeplitz, g1, g2, done], 1
+    )
+
     mine, theirs = call(
-        sum_kernel, [shape((rows, width), BF)] * 2, [own, from_below, from_above], 0.1
-    )
-    other = move(theirs, 0, 1, 0)
+        sum_kernel, [shape((rows, width), BF)] * 2, [own, from_pair, from_next], 0.1
+    )
+    other = move(theirs, 0, 1)
     self_energy, mark = call(
         join_kernel,
         [shape(green_less.shape, BF), shape((8, LANES), F32)],

time: 35.1 us -> 38.1 us (1.085)
  local copies, waits for them, and re-layouts: 0.01 us -> 2.68 us
  waiting for transfers between devices: 6.41 us -> 4.09 us
  starting transfers between devices: 14.4 us -> 16 us
  Pallas kernels: 13.4 us -> 14.4 us
    all_to_all x1, starting transfers between devices: 2.65 us -> 5.81 us  [body(): lax.all_to_all(partial.reshape(mom * en, local_k * half, LANES), ('mom',...]
    ppermute x9, waiting for transfers between devices: 4 us -> 1.16 us  [move(): return lax.ppermute(value, ('mom', 'en'), links)]
    unnamed x6 -> x16, local copies, waits for them, and re-layouts: 0.01 us -> 2.68 us
    ppermute x9, starting transfers between devices: 11.7 us -> 10.2 us  [move(): return lax.ppermute(value, ('mom', 'en'), links)]
    pallas_call x7 -> x8, Pallas kernels: 13.4 us -> 14.4 us  [call(): pl.pallas_call(kernel, out_shape=outs, in_specs=specs or [VMEM] * len(ins...]
    all_to_all x1, waiting for transfers between devices: 2.4 us -> 2.93 us  [body(): lax.all_to_all(partial.reshape(mom * en, local_k * half, LANES), ('mom',...]
  transfers between devices with their start and end apart: 10 -> 10, of which waited for: 4 -> 2; matrix products, arithmetic and copies ran while one was open for 0% -> 0% of each run, Pallas kernels for 31% -> 28%
where the time goes in v2:
time: 38.1 us; the launch traced here: 37.9 us
  starting transfers between devices  16 us (42%)
  Pallas kernels  14.4 us (38%)
  waiting for transfers between devices  4.09 us (11%)
  local copies, waits for them, and re-layouts  2.68 us (7%)
  between operations  0.76 us (2%)
    pallas_call x8, Pallas kernels, call(): pl.pallas_call(kernel, out_shape=outs, in_specs=specs or [VMEM] * len(ins...  14.4 us
    ppermute x9, starting transfers between devices, move(): return lax.ppermute(value, ('mom', 'en'), links)  10.2 us
    all_to_all x1, starting transfers between devices, body(): lax.all_to_all(partial.reshape(mom * en, local_k * half, LANES), ('mom',...  5.81 us
    all_to_all x1, waiting for transfers between devices, body(): lax.all_to_all(partial.reshape(mom * en, local_k * half, LANES), ('mom',...  2.93 us
    unnamed x16, local copies, waits for them, and re-layouts  2.68 us
    ppermute x9, waiting for transfers between devices, move(): return lax.ppermute(value, ('mom', 'en'), links)  1.16 us
  transfers between devices with their start and end apart: 10, of which 2 were waited for; matrix products, arithmetic and copies ran while one was open for 0% of the time, Pallas kernels for 28%

profile of v2, /device:TPU:0, one launch (start us, length us, event | category | flops | bytes accessed | tf_op | source)
XLA Modules:
  0.0 37.9 jit_solution(5890027391593099609)
XLA Ops:
  0.7 2.0 %shard_map.69 = (bf16[48,1152]{1,0:T(8,128)(2,1)S(1)}, bf16[48,1152]{1,0:T(8,128)(2,1)S(1)}, bf16[48,1152]{1,0:T(8,128)(2,1)S(1)}, bf16[48,1152]{1,0:T(8,128)(2,1)S(1)}) custom-call(bf16[2,24,8,288]{3,2,1,0:T(8,128)(2,1)} %g_hbm.1, bf16[2,24,8,288]{3,2,1,0:T(8,128)(2,1)} %b_hbm.1), custom_call_target="tpu_custom_call" | custom-call | flops 1500000000 | tf_op jit(solution)/shard_map/pallas_call | solution.py:31
  2.7 0.5 %collective-permute-start = (bf16[48,1152]{1,0:T(8,128)(2,1)S(1)}, bf16[48,1152]{1,0:T(8,128)(2,1)S(1)}, u32[]{:S(2)}, u32[]{:S(2)}) collective-permute-start(bf16[48,1152]{1,0:T(8,128)(2,1)S(1)} %get-tuple-element.25), channel_id=1, source_target_pairs={{0,8},{1,9},{2,10},{3,11},{4,12},{5,13},{6,14},{7,15},{8,0},{9,1},... | collective-permute-start | bytes 331784 | tf_op jit(solution)/shard_map/ppermute | solution.py:421
  3.2 2.6 %collective-permute-start.2 = (bf16[48,1152]{1,0:T(8,128)(2,1)S(1)}, bf16[48,1152]{1,0:T(8,128)(2,1)S(1)}, u32[]{:S(2)}, u32[]{:S(2)}) collective-permute-start(bf16[48,1152]{1,0:T(8,128)(2,1)S(1)} %get-tuple-element.25), channel_id=1, source_target_pairs={{0,24},{1,25},{2,26},{3,27},{4,28},{5,29},{6,30},{7,31},{8,16},{9,... | collective-permute-start | bytes 331784 | tf_op jit(solution)/shard_map/ppermute | solution.py:421
  5.8 0.1 collective-permute-start.3
  5.9 1.6 %collective-permute-start.5 = (bf16[48,1152]{1,0:T(8,128)(2,1)S(1)}, bf16[48,1152]{1,0:T(8,128)(2,1)S(1)}, u32[]{:S(2)}, u32[]{:S(2)}) collective-permute-start(bf16[48,1152]{1,0:T(8,128)(2,1)S(1)} %get-tuple-element.32), channel_id=1, source_target_pairs={{0,9},{1,10},{2,11},{3,12},{4,13},{5,14},{6,15},{7,8},{8,1},{9,2},... | collective-permute-start | bytes 331784 | tf_op jit(solution)/shard_map/ppermute | solution.py:421
  7.5 0.5 %collective-permute-start.1 = (bf16[48,1152]{1,0:T(8,128)(2,1)S(1)}, bf16[48,1152]{1,0:T(8,128)(2,1)S(1)}, u32[]{:S(2)}, u32[]{:S(2)}) collective-permute-start(bf16[48,1152]{1,0:T(8,128)(2,1)S(1)} %get-tuple-element.24.refs_0_), channel_id=1, source_target_pairs={{0,16},{1,17},{2,18},{3,19},{4,20},{5,21},{6,22},{7,23},{8,24},{9,... | collective-permute-start | bytes 331784 | tf_op jit(solution)/shard_map/ppermute | solution.py:421
  8.0 2.9 %shard_map.68 = (bf16[24,144,256]{2,1,0:T(8,128)(2,1)S(1)}, bf16[24,144,256]{2,1,0:T(8,128)(2,1)S(1)}, bf16[12,288,256]{2,1,0:T(8,128)(2,1)S(1)}, bf16[192,192]{...) custom-call(s32[2,4]{1,0:T(2,128)S(1)} %copy-done.5, ...), custom_call_target="tpu_custom_call" | custom-call | flops 3000000000 | tf_op jit(solution)/shard_map/pallas_call | solution.py:31
  10.9 0.0 copy-start.6
  11.0 0.7 %copy-done.6 = bf16[384,384]{1,0:T(8,128)(2,1)} copy-done((bf16[384,384]{1,0:T(8,128)(2,1)}, bf16[384,384]{1,0:T(8,128)(2,1)S(1)}, u32[]{:S(2)}) %copy-start.6) | copy-done | bytes 294936
  11.7 0.0 collective-permute-done.refs_1_
  11.7 1.5 %collective-permute-start.4 = (bf16[48,1152]{1,0:T(8,128)(2,1)S(1)}, bf16[48,1152]{1,0:T(8,128)(2,1)S(1)}, u32[]{:S(2)}, u32[]{:S(2)}) collective-permute-start(bf16[48,1152]{1,0:T(8,128)(2,1)S(1)} %get-tuple-element.31.b_own), channel_id=1, source_target_pairs={{0,1},{1,2},{2,3},{3,4},{4,5},{5,6},{6,7},{7,0},{8,9},{9,10},{10,1... | collective-permute-start | bytes 331784 | tf_op jit(solution)/shard_map/ppermute | solution.py:421
  13.2 0.0 collective-permute-done.1.refs_2_
  13.2 0.0 collective-permute-done.2.refs_3_
  13.2 3.7 %shard_map.70 = (bf16[3,192,1152]{2,1,0:T(8,128)(2,1)S(1)}, bf16[3,192,1152]{2,1,0:T(8,128)(2,1)S(1)}, bf16[2,48,1152]{2,1,0:T(8,128)(2,1)}, bf16[2,48,1152]{2,1,0:T(8,128)(2,1)}) custom-call(bf16[48,1152]{1,0:T(8,128)(2,1)S(1)} %get-tuple-element.24.refs_0_, bf16[48,1152]{1,0:T(8,128)(2,1)S(1)} %collective-permute-done.refs_1_, ...), custom_call_target="tpu_custom_call" | custom-call | flops 4000000000 | tf_op jit(solution)/shard_map/pallas_call | solution.py:31
  16.9 1.5 %collective-permute-start.6 = (bf16[2,48,1152]{2,1,0:T(8,128)(2,1)}, bf16[2,48,1152]{2,1,0:T(8,128)(2,1)S(1)}, u32[]{:S(2)}, u32[]{:S(2)}) collective-permute-start(bf16[2,48,1152]{2,1,0:T(8,128)(2,1)} %get-tuple-element.36), channel_id=1, source_target_pairs={{0,1},{1,0},{2,3},{3,2},{4,5},{5,4},{6,7},{7,6},{8,9},{9,8},{10,11... | collective-permute-start | bytes 663560 | tf_op jit(solution)/shard_map/ppermute | solution.py:421
  18.4 1.6 %collective-permute-start.7 = (bf16[2,48,1152]{2,1,0:T(8,128)(2,1)}, bf16[2,48,1152]{2,1,0:T(8,128)(2,1)S(1)}, u32[]{:S(2)}, u32[]{:S(2)}) collective-permute-start(bf16[2,48,1152]{2,1,0:T(8,128)(2,1)} %get-tuple-element.37), channel_id=1, source_target_pairs={{0,0},{1,2},{2,1},{3,4},{4,3},{5,6},{6,5},{7,7},{8,8},{9,10},{10,9... | collective-permute-start | bytes 663560 | tf_op jit(solution)/shard_map/ppermute | solution.py:421
  20.0 0.0 collective-permute-done.3.b_far
  20.0 0.0 collective-permute-done.4.prev_own
  20.0 0.0 collective-permute-done.5.prev_far
  20.0 2.0 %shard_map.71 = (f32[4,8,8,128]{3,2,1,0:T(8,128)S(1)}, f32[8,128]{1,0:T(8,128)S(1)}) custom-call(bf16[48,1152]{1,0:T(8,128)(2,1)S(1)} %get-tuple-element.31.b_own, bf16[48,1152]{1,0:T(8,128)(2,1)S(1)} %collective-permute-done.3.b_far, bf16[48,1152]{1,0:T(8,128)(2,1)S(1)} %collective-permute-done.4.prev_own, ...), custom_call_target="tpu_custom_call" | custom-call | flops 3000000000 | tf_op jit(solution)/shard_map/pallas_call | solution.py:31
  22.1 0.6 %copy-done.2 = f32[4,8,8,128]{3,2,1,0:T(8,128)} copy-done((f32[4,8,8,128]{3,2,1,0:T(8,128)}, f32[4,8,8,128]{3,2,1,0:T(8,128)S(1)}, u32[]{:S(2)}) %copy-start.2) | copy-done | bytes 131096
  22.7 5.8 %all-to-all-start = ((f32[32,8,128]{2,1,0:T(8,128)}), f32[32,8,128]{2,1,0:T(8,128)}, u32[]{:S(2)}, u32[]{:S(2)}) async-start(f32[32,8,128]{2,1,0:T(8,128)} %bitcast.5), calls=%async_computation | async-start | bytes 262144 | tf_op jit(solution)/shard_map/all_to_all | solution.py:486
  28.6 1.3 %copy-done.1 = bf16[3,192,1152]{2,1,0:T(8,128)(2,1)S(1)} copy-done((bf16[3,192,1152]{2,1,0:T(8,128)(2,1)S(1)}, bf16[3,192,1152]{2,1,0:T(8,128)(2,1)}, u32[]{:S(2)}) %copy-start.1) | copy-done | bytes 1327128
  29.9 0.8 %shard_map.72.own = f32[2,48,1152]{2,1,0:T(8,128)S(1)} custom-call(bf16[12,288,256]{2,1,0:T(8,128)(2,1)S(1)} %get-tuple-element.23.refs_7_.t_ref, bf16[3,192,1152]{2,1,0:T(8,128)(2,1)S(1)} %get-tuple-element.29.g1_ref.high_ref, bf16[3,192,1152]{2,1,0:T(8,128)(2,1)S(1)} %copy-done.1, f32[8,128]{1,0:T(8,128)S(1)} %get-tuple-element.35.after_ref), custom_call_target="tpu_custom_call" | custom-call | flops 1000000000 | tf_op jit(solution)/shard_map/pallas_call | solution.py:31
  30.6 0.0 collective-permute-done.6.pair
  30.7 0.0 collective-permute-done.7.after
  30.7 0.1 shard_map.73
  30.8 0.2 collective-permute-start.8
  31.0 1.1 %collective-permute-done.8.other = bf16[48,1152]{1,0:T(8,128)(2,1)S(1)} collective-permute-done((bf16[48,1152]{1,0:T(8,128)(2,1)S(1)}, bf16[48,1152]{1,0:T(8,128)(2,1)S(1)}, u32[]{:S(2)}, u32[]{:S(2)}) %collective-permute-start.8) | collective-permute-done | bytes 110624 | tf_op jit(solution)/shard_map/ppermute | solution.py:421
  32.1 1.2 %shard_map.74 = (bf16[2,24,8,288]{3,2,1,0:T(8,128)(2,1)}, f32[8,128]{1,0:T(8,128)S(1)}) custom-call(bf16[48,1152]{1,0:T(8,128)(2,1)S(1)} %get-tuple-element.38.mine, bf16[48,1152]{1,0:T(8,128)(2,1)S(1)} %collective-permute-done.8.other, bf16[384,384]{1,0:T(8,128)(2,1)S(1)} %copy-done.7), custom_call_target="tpu_custom_call" | custom-call | flops 1000000000 | tf_op jit(solution)/shard_map/pallas_call | solution.py:31
  33.3 2.9 %all-to-all-done = f32[32,8,128]{2,1,0:T(8,128)} async-done(((f32[32,8,128]{2,1,0:T(8,128)}), f32[32,8,128]{2,1,0:T(8,128)}, u32[]{:S(2)}, u32[]{:S(2)}) %all-to-all-start) | async-done | bytes 131104 | tf_op jit(solution)/shard_map/all_to_all | solution.py:486
  36.3 1.6 %shard_map.75 = f32[2,3,8,24]{3,2,1,0:T(8,128)} custom-call(f32[4,8,8,128]{3,2,1,0:T(8,128)} %bitcast.3.in_ref, f32[8,128]{1,0:T(8,128)S(1)} %get-tuple-element.43.after_ref), custom_call_target="tpu_custom_call" | custom-call | flops 500000000 | tf_op jit(solution)/shard_map/pallas_call | solution.py:31
  (12 shorter events, 0.0 us)
Async XLA Ops:
  0.6 7.4 %copy-start.4 = (f32[2,3,144]{2,0,1:T(2,128)S(1)}, f32[2,3,144]{2,0,1:T(2,128)}, u32[]{:S(2)}) copy-start(f32[2,3,144]{2,0,1:T(2,128)} %param.7) | copy-start | bytes 10372
  0.6 7.4 %copy-start.3 = (bf16[2,8,24,3,8]{2,4,3,1,0:T(8,128)(2,1)S(1)}, bf16[2,8,24,3,8]{2,4,3,1,0:T(8,128)(2,1)}, u32[]{:S(2)}) copy-start(bf16[2,8,24,3,8]{2,4,3,1,0:T(8,128)(2,1)} %param.9) | copy-start | bytes 55300
  0.7 7.4 %copy-start.5 = (s32[2,4]{1,0:T(2,128)S(1)}, s32[2,4]{1,0:T(2,128)}, u32[]{:S(2)}) copy-start(s32[2,4]{1,0:T(2,128)} %near_ref.1) | copy-start | bytes 100
  2.7 9.0 %collective-permute-start = (bf16[48,1152]{1,0:T(8,128)(2,1)S(1)}, bf16[48,1152]{1,0:T(8,128)(2,1)S(1)}, u32[]{:S(2)}, u32[]{:S(2)}) collective-permute-start(bf16[48,1152]{1,0:T(8,128)(2,1)S(1)} %get-tuple-element.25), channel_id=1, source_target_pairs={{0,8},{1,9},{2,10},{3,11},{4,12},{5,13},{6,14},{7,15},{8,0},{9,1},... | collective-permute-start | bytes 331784 | tf_op jit(solution)/shard_map/ppermute | solution.py:421
  3.2 10.0 %collective-permute-start.2 = (bf16[48,1152]{1,0:T(8,128)(2,1)S(1)}, bf16[48,1152]{1,0:T(8,128)(2,1)S(1)}, u32[]{:S(2)}, u32[]{:S(2)}) collective-permute-start(bf16[48,1152]{1,0:T(8,128)(2,1)S(1)} %get-tuple-element.25), channel_id=1, source_target_pairs={{0,24},{1,25},{2,26},{3,27},{4,28},{5,29},{6,30},{7,31},{8,16},{9,... | collective-permute-start | bytes 331784 | tf_op jit(solution)/shard_map/ppermute | solution.py:421
  5.8 14.2 %collective-permute-start.3 = (bf16[48,1152]{1,0:T(8,128)(2,1)S(1)}, bf16[48,1152]{1,0:T(8,128)(2,1)S(1)}, u32[]{:S(2)}, u32[]{:S(2)}) collective-permute-start(bf16[48,1152]{1,0:T(8,128)(2,1)S(1)} %get-tuple-element.32), channel_id=1, source_target_pairs={{0,8},{1,9},{2,10},{3,11},{4,12},{5,13},{6,14},{7,15},{8,0},{9,1},... | collective-permute-start | bytes 331784 | tf_op jit(solution)/shard_map/ppermute | solution.py:421
  5.9 14.1 %collective-permute-start.5 = (bf16[48,1152]{1,0:T(8,128)(2,1)S(1)}, bf16[48,1152]{1,0:T(8,128)(2,1)S(1)}, u32[]{:S(2)}, u32[]{:S(2)}) collective-permute-start(bf16[48,1152]{1,0:T(8,128)(2,1)S(1)} %get-tuple-element.32), channel_id=1, source_target_pairs={{0,9},{1,10},{2,11},{3,12},{4,13},{5,14},{6,15},{7,8},{8,1},{9,2},... | collective-permute-start | bytes 331784 | tf_op jit(solution)/shard_map/ppermute | solution.py:421
  7.5 5.7 %collective-permute-start.1 = (bf16[48,1152]{1,0:T(8,128)(2,1)S(1)}, bf16[48,1152]{1,0:T(8,128)(2,1)S(1)}, u32[]{:S(2)}, u32[]{:S(2)}) collective-permute-start(bf16[48,1152]{1,0:T(8,128)(2,1)S(1)} %get-tuple-element.24.refs_0_), channel_id=1, source_target_pairs={{0,16},{1,17},{2,18},{3,19},{4,20},{5,21},{6,22},{7,23},{8,24},{9,... | collective-permute-start | bytes 331784 | tf_op jit(solution)/shard_map/ppermute | solution.py:421
  10.9 0.7 %copy-start.6 = (bf16[384,384]{1,0:T(8,128)(2,1)}, bf16[384,384]{1,0:T(8,128)(2,1)S(1)}, u32[]{:S(2)}) copy-start(bf16[384,384]{1,0:T(8,128)(2,1)S(1)} %get-tuple-element.40.perm_ref) | copy-start | bytes 884740
  11.7 8.3 %collective-permute-start.4 = (bf16[48,1152]{1,0:T(8,128)(2,1)S(1)}, bf16[48,1152]{1,0:T(8,128)(2,1)S(1)}, u32[]{:S(2)}, u32[]{:S(2)}) collective-permute-start(bf16[48,1152]{1,0:T(8,128)(2,1)S(1)} %get-tuple-element.31.b_own), channel_id=1, source_target_pairs={{0,1},{1,2},{2,3},{3,4},{4,5},{5,6},{6,7},{7,0},{8,9},{9,10},{10,1... | collective-permute-start | bytes 331784 | tf_op jit(solution)/shard_map/ppermute | solution.py:421
  16.9 5.2 %copy-start = (bf16[3,192,1152]{2,1,0:T(8,128)(2,1)}, bf16[3,192,1152]{2,1,0:T(8,128)(2,1)S(1)}, u32[]{:S(2)}) copy-start(bf16[3,192,1152]{2,1,0:T(8,128)(2,1)S(1)} %get-tuple-element.30.rest_ref) | copy-start | bytes 3981316
  16.9 13.7 %collective-permute-start.6 = (bf16[2,48,1152]{2,1,0:T(8,128)(2,1)}, bf16[2,48,1152]{2,1,0:T(8,128)(2,1)S(1)}, u32[]{:S(2)}, u32[]{:S(2)}) collective-permute-start(bf16[2,48,1152]{2,1,0:T(8,128)(2,1)} %get-tuple-element.36), channel_id=1, source_target_pairs={{0,1},{1,0},{2,3},{3,2},{4,5},{5,4},{6,7},{7,6},{8,9},{9,8},{10,11... | collective-permute-start | bytes 663560 | tf_op jit(solution)/shard_map/ppermute | solution.py:421
  18.4 12.2 %collective-permute-start.7 = (bf16[2,48,1152]{2,1,0:T(8,128)(2,1)}, bf16[2,48,1152]{2,1,0:T(8,128)(2,1)S(1)}, u32[]{:S(2)}, u32[]{:S(2)}) collective-permute-start(bf16[2,48,1152]{2,1,0:T(8,128)(2,1)} %get-tuple-element.37), channel_id=1, source_target_pairs={{0,0},{1,2},{2,1},{3,4},{4,3},{5,6},{6,5},{7,7},{8,8},{9,10},{10,9... | collective-permute-start | bytes 663560 | tf_op jit(solution)/shard_map/ppermute | solution.py:421
  22.1 0.6 %copy-start.2 = (f32[4,8,8,128]{3,2,1,0:T(8,128)}, f32[4,8,8,128]{3,2,1,0:T(8,128)S(1)}, u32[]{:S(2)}) copy-start(f32[4,8,8,128]{3,2,1,0:T(8,128)S(1)} %get-tuple-element.42) | copy-start | bytes 393220
  22.7 13.5 %all-to-all-start = ((f32[32,8,128]{2,1,0:T(8,128)}), f32[32,8,128]{2,1,0:T(8,128)}, u32[]{:S(2)}, u32[]{:S(2)}) async-start(f32[32,8,128]{2,1,0:T(8,128)} %bitcast.5), calls=%async_computation | async-start | bytes 262144 | tf_op jit(solution)/shard_map/all_to_all | solution.py:486
  28.5 1.3 %copy-start.1 = (bf16[3,192,1152]{2,1,0:T(8,128)(2,1)S(1)}, bf16[3,192,1152]{2,1,0:T(8,128)(2,1)}, u32[]{:S(2)}) copy-start(bf16[3,192,1152]{2,1,0:T(8,128)(2,1)} %copy-done) | copy-start | bytes 3981316
  29.9 2.3 %copy-start.7 = (bf16[384,384]{1,0:T(8,128)(2,1)S(1)}, bf16[384,384]{1,0:T(8,128)(2,1)}, u32[]{:S(2)}) copy-start(bf16[384,384]{1,0:T(8,128)(2,1)} %copy-done.6) | copy-start | bytes 884740
  30.8 1.4 %collective-permute-start.8 = (bf16[48,1152]{1,0:T(8,128)(2,1)S(1)}, bf16[48,1152]{1,0:T(8,128)(2,1)S(1)}, u32[]{:S(2)}, u32[]{:S(2)}) collective-permute-start(bf16[48,1152]{1,0:T(8,128)(2,1)S(1)} %get-tuple-element.39), channel_id=1, source_target_pairs={{0,8},{1,9},{2,10},{3,11},{4,12},{5,13},{6,14},{7,15},{8,0},{9,1},... | collective-permute-start | bytes 331784 | tf_op jit(solution)/shard_map/ppermute | solution.py:421

commit v3 on v2

--- a/solution.py
+++ b/solution.py
@@ -27,7 +27,7 @@
     return lax.dot_general(a, b, (((1,), (1,)), ((), ())), preferred_element_type=F32)
 
 
-def call(kernel, outs, ins, work, scratch=(), specs=None, limit=24):
+def call(kernel, outs, ins, work, scratch=(), specs=None, limit=12):
     return pl.pallas_call(
         kernel,
         out_shape=outs,
@@ -191,17 +191,19 @@
             for blk in (0, 2, 1):
                 for a in range(chip_k):
                     order += [grid[(blk * per + i, a)] for i in range(per)]
-            t_ref[p * 3 + m] = jnp.concatenate(order, axis=0).astype(BF)
+            table = jnp.where(index((1, 2 * LANES), 1) < momenta * local_e, jnp.concatenate(order, axis=0), 0.0)
+            t_ref[p, :, m * 2 * LANES : (m + 1) * 2 * LANES] = table.astype(BF)
 
 
 def product_kernel(*refs, half, entries, chips):
     core = my_core()
     blocks = refs[: 2 * chips]
     perm_ref, hi_ref, lo_ref, t_ref = refs[2 * chips : 2 * chips + 4]
-    high_ref, rest_ref, pair_ref, next_ref, gathered, result = refs[2 * chips + 4 :]
+    terms_ref, pair_ref, next_ref, gathered, result = refs[2 * chips + 4 :]
     for s in range(chips):
-        gathered[2 * s + core] = blocks[2 * s][...]
-        gathered[2 * s + 1 - core] = blocks[2 * s + 1][...]
+        n = 2 * ((s - 1) % chips)
+        gathered[2 * s + core] = blocks[n][...]
+        gathered[2 * s + 1 - core] = blocks[n + 1][...]
     count, rows, width = gathered.shape
     depth = count * rows
     tiles = width // LANES
@@ -212,29 +214,29 @@
         start = (entries // 2) * j // LANES * LANES
         shift = (entries // 2) * j - start
         lhs = g[:, start : start + 2 * LANES]
-
-        def padded(ref, n):
-            parts = [ref[n]]
-            if shift:
-                parts = [jnp.zeros((shift, 2 * LANES), BF)] + parts
-            rest = 2 * LANES - shift - block_rows
-            if rest:
-                parts = parts + [jnp.zeros((rest, 2 * LANES), BF)]
-            return jnp.concatenate(parts, axis=0)
-
+        lhs = jnp.concatenate([lhs, lhs], axis=1)
+        above = [jnp.zeros((shift, 2 * LANES), BF)] if shift else []
+        rest = 2 * LANES - shift - block_rows
+        under = [jnp.zeros((rest, 2 * LANES), BF)] if rest else []
         for m in range(3):
-            r = dot(lhs, padded(hi_ref, j * 3 + m)) + dot(lhs, padded(lo_ref, j * 3 + m))
+            parts = above + [hi_ref[j * 3 + m]] + under + above + [lo_ref[j * 3 + m]] + under
+            r = dot(lhs, jnp.concatenate(parts, axis=0))
             for i in range(2):
                 tile = start // LANES + i
                 piece = r[:, i * LANES : (i + 1) * LANES]
                 sums[m][tile] = piece if sums[m][tile] is None else sums[m][tile] + piece
+    spare = 2 * LANES - depth
     for m in range(3):
+        for n in range(2):
+            at = (3 * n + m) * 2 * LANES
+            if spare:
+                terms_ref[at + depth : at + 2 * LANES, :] = jnp.zeros((spare, width), BF)
         for i in range(tiles):
-            at = slice(i * LANES, (i + 1) * LANES)
             high = sums[m][i].astype(BF)
-            high_ref[m, :, at] = high
-            rest_ref[m, :, at] = (sums[m][i] - high.astype(F32)).astype(BF)
-    correlate(t_ref, 0, 4, high_ref, rest_ref, result, entries)
+            for n, part in enumerate((high, (sums[m][i] - high.astype(F32)).astype(BF))):
+                at = (3 * n + m) * 2 * LANES
+                terms_ref[at : at + depth, i * LANES : (i + 1) * LANES] = part
+    correlate(t_ref, 0, 4, terms_ref, result, entries)
     place = lax.axis_index("en")
     odd = lax.rem(place, 2)
     below = jnp.where(place == 0, 0.0, 1.0)
@@ -246,22 +248,16 @@
         next_ref[i] = (result[2 * odd + c] * keep_next).astype(BF)
 
 
-def correlate(t_ref, begin_row, count, high_ref, rest_ref, result, entries):
+def correlate(t_ref, begin_row, count, terms_ref, result, entries):
     _, rows, width = result.shape
-    depth = high_ref.shape[1]
     lane = index((1, LANES), 1)
-    at_rows = slice(begin_row * rows, (begin_row + count) * rows)
     carried = None
     for p in range(width // entries):
         begin = entries * p
         first = begin // LANES
         last = (begin + entries - 1) // LANES
-        total = None
-        for m in range(3):
-            t = t_ref[p * 3 + m, at_rows, :][:, :depth]
-            for part in (high_ref, rest_ref):
-                term = dot(t, part[m, :, first * LANES : (last + 1) * LANES])
-                total = term if total is None else total + term
+        t = t_ref[p, begin_row * rows : (begin_row + count) * rows, :]
+        total = dot(jnp.concatenate([t, t], axis=1), terms_ref[:, first * LANES : (last + 1) * LANES])
         for i in range(first, last + 1):
             tile = total[:, (i - first) * LANES : (i - first + 1) * LANES]
             if i == first and begin % LANES:
@@ -273,11 +269,11 @@
                     result[r, :, i * LANES : (i + 1) * LANES] = tile[r * rows : (r + 1) * rows]
 
 
-def own_kernel(t_ref, high_ref, rest_ref, after_ref, own_ref, *, entries):
-    correlate(t_ref, 4, 2, high_ref, rest_ref, own_ref, entries)
-
-
-def polar_kernel(b_own, b_far, prev_own, prev_far, turn_ref, sort_ref, g1_ref, out_ref, mark_ref, gathered, *, half, entries, local_k, local_e, scale):
+def own_kernel(t_ref, terms_ref, after_ref, own_ref, *, entries):
+    correlate(t_ref, 4, 2, terms_ref, own_ref, entries)
+
+
+def polar_kernel(b_own, b_far, prev_own, prev_far, turn_ref, sort_ref, terms_ref, out_ref, mark_ref, gathered, *, half, entries, momenta, local_k, local_e, scale):
     core = my_core()
     present = jnp.where(lax.axis_index("en") == 0, 0.0, 1.0)
     gathered[core] = (prev_own[...].astype(F32) * present).astype(BF)
@@ -299,7 +295,7 @@
     group = 2 * local_e
     columns = sort_ref.shape[0]
     window = local_e
-    momenta = g1_ref.shape[1] // local_e
+    depth = local_e * momenta
     lane = index((1, LANES), 1)
     mark_ref[...] = jnp.zeros(mark_ref.shape, F32)
     pieces = []
@@ -318,7 +314,7 @@
         rhs = jnp.concatenate(parts, axis=1)
         held = None
         for m in range(3):
-            s = dot_t(g1_ref[m][:, first * LANES : (last + 1) * LANES], rhs)
+            s = dot_t(terms_ref[m * 2 * LANES : m * 2 * LANES + depth, first * LANES : (last + 1) * LANES], rhs)
             acc = None
             for e in range(local_e):
                 row = pltpu.roll(s[e * momenta : (e + 1) * momenta], columns - (local_e - e), 1)
@@ -361,7 +357,7 @@
             out_ref[i, m] = moved[:, :window]
 
 
-def sum_kernel(own, pair, after, mine, theirs):
+def sum_kernel(own, after, pair, mine, theirs):
     core = my_core()
     for n, i, out in ((0, core, mine), (1, 1 - core, theirs)):
         out[...] = (own[i] + pair[n].astype(F32) + after[n].astype(F32)).astype(BF)
@@ -430,9 +426,10 @@
         other = e + 1 if e % 2 else e - 1
         return other if 0 <= other < en else e
 
-    blocks = [g_own, move(g_far, 0, 1)]
+    blocks = []
     for s in range(1, chips):
-        blocks += [move(g_own, -s, 0), move(g_far, -s, 1)]
+        blocks += [move(g_far, -s, 1), move(g_own, -s, 0)][::-1]
+    blocks += [g_own, move(g_far, 0, 1)]
     b_core = move(b_far, 0, 1)
     prev_own = move(b_own, 0, 0, onward)
     prev_far = move(b_far, 0, 1, onward)
@@ -444,7 +441,7 @@
         [
             shape((6 * half, size, 2 * LANES), BF),
             shape((6 * half, size, 2 * LANES), BF),
-            shape((3 * half, 3 * chip_k * local_e, 2 * LANES), BF),
+            shape((half, 3 * chip_k * local_e, 6 * LANES), BF),
             shape((momenta * local_e,) * 2, BF),
             shape((rows * pairs,) * 2, BF),
             shape((2 * half, 2 * LANES, 2 * LANES), BF),
@@ -459,11 +456,10 @@
         [pl.BlockSpec(memory_space=pltpu.SMEM), VMEM, VMEM],
     )
 
-    g1, g2, to_pair_rows, to_next_rows = call(
+    source_terms, to_pair_rows, to_next_rows = call(
         functools.partial(product_kernel, half=half, entries=entries, chips=chips),
         [
-            shape((3, momenta * local_e, width), BF),
-            shape((3, momenta * local_e, width), BF),
+            shape((12 * LANES, width), BF),
             shape((2, rows, width), BF),
             shape((2, rows, width), BF),
         ],
@@ -471,15 +467,15 @@
         4,
         [pltpu.VMEM((2 * chips, rows, width), BF), pltpu.VMEM((4, rows, width), F32)],
     )
+    from_next = move(to_next_rows, 0, 0, to_next)
     from_pair = move(to_pair_rows, 0, 0, to_pair)
-    from_next = move(to_next_rows, 0, 0, to_next)
     partial, done = call(
         functools.partial(
-            polar_kernel, half=half, entries=entries, local_k=local_k, local_e=local_e,
+            polar_kernel, half=half, entries=entries, momenta=momenta, local_k=local_k, local_e=local_e,
             scale=1.0 / (NO * float(np.sqrt(momenta * total_e))),
         ),
         [shape((mom, en, local_k * half, LANES), F32), shape((8, LANES), F32)],
-        [b_own, b_core, prev_own, prev_far, turn, sort_e, g1],
+        [b_own, b_core, prev_own, prev_far, turn, sort_e, source_terms],
         3,
         [pltpu.VMEM((4, rows, width), BF)],
     )
@@ -487,11 +483,11 @@
         partial.reshape(mom * en, local_k * half, LANES), ("mom", "en"), split_axis=0, concat_axis=0, tiled=True
     )
     (own,) = call(
-        functools.partial(own_kernel, entries=entries), [shape((2, rows, width), F32)], [toeplitz, g1, g2, done], 1
+        functools.partial(own_kernel, entries=entries), [shape((2, rows, width), F32)], [toeplitz, source_terms, done], 1
     )
 
     mine, theirs = call(
-        sum_kernel, [shape((rows, width), BF)] * 2, [own, from_pair, from_next], 0.1
+        sum_kernel, [shape((rows, width), BF)] * 2, [own, from_next, from_pair], 0.1
     )
     other = move(theirs, 0, 1)
     self_energy, mark = call(

time: 38.1 us -> 39.6 us (1.039)
  Pallas kernels: 14.4 us -> 15.7 us
  waiting for transfers between devices: 4.09 us -> 3.53 us
  starting transfers between devices: 16 us -> 16.4 us
    ppermute x9, starting transfers between devices: 10.2 us -> 12 us  [move(): return lax.ppermute(value, ('mom', 'en'), links)]
    all_to_all x1, starting transfers between devices: 5.81 us -> 4.37 us  [body(): lax.all_to_all(partial.reshape(mom * en, local_k * half, LANES), ('mom',...]
    pallas_call x8, Pallas kernels: 14.4 us -> 15.7 us  [call(): pl.pallas_call(kernel, out_shape=outs, in_specs=specs or [VMEM] * len(ins...]
    all_to_all x1, waiting for transfers between devices: 2.93 us -> 1.6 us  [body(): lax.all_to_all(partial.reshape(mom * en, local_k * half, LANES), ('mom',...]
    ppermute x9, waiting for transfers between devices: 1.16 us -> 1.92 us  [move(): return lax.ppermute(value, ('mom', 'en'), links)]
  transfers between devices with their start and end apart: 10 -> 10, of which waited for: 2 -> 3; matrix products, arithmetic and copies ran while one was open for 0% -> 0% of each run, Pallas kernels for 28% -> 31%
where the time goes in v3:
time: 39.6 us; the launch traced here: 39.2 us
  starting transfers between devices  16.4 us (41%)
  Pallas kernels  15.7 us (40%)
  waiting for transfers between devices  3.53 us (9%)
  local copies, waits for them, and re-layouts  2.84 us (7%)
  between operations  0.75 us (2%)
    pallas_call x8, Pallas kernels, call(): pl.pallas_call(kernel, out_shape=outs, in_specs=specs or [VMEM] * len(ins...  15.7 us
    ppermute x9, starting transfers between devices, move(): return lax.ppermute(value, ('mom', 'en'), links)  12 us
    all_to_all x1, starting transfers between devices, body(): lax.all_to_all(partial.reshape(mom * en, local_k * half, LANES), ('mom',...  4.37 us
    unnamed x16, local copies, waits for them, and re-layouts  2.84 us
    ppermute x9, waiting for transfers between devices, move(): return lax.ppermute(value, ('mom', 'en'), links)  1.92 us
    all_to_all x1, waiting for transfers between devices, body(): lax.all_to_all(partial.reshape(mom * en, local_k * half, LANES), ('mom',...  1.6 us
  transfers between devices with their start and end apart: 10, of which 3 were waited for; matrix products, arithmetic and copies ran while one was open for 0% of the time, Pallas kernels for 31%

profile of v3, /device:TPU:0, one launch (start us, length us, event | category | flops | bytes accessed | tf_op | source)
XLA Modules:
  0.0 39.2 jit_solution(12676893403072125811)
XLA Ops:
  0.7 2.0 %shard_map.69 = (bf16[48,1152]{1,0:T(8,128)(2,1)S(1)}, bf16[48,1152]{1,0:T(8,128)(2,1)S(1)}, bf16[48,1152]{1,0:T(8,128)(2,1)S(1)}, bf16[48,1152]{1,0:T(8,128)(2,1)S(1)}) custom-call(bf16[2,24,8,288]{3,2,1,0:T(8,128)(2,1)} %g_hbm.1, bf16[2,24,8,288]{3,2,1,0:T(8,128)(2,1)} %b_hbm.1), custom_call_target="tpu_custom_call" | custom-call | flops 1500000000 | tf_op jit(solution)/shard_map/pallas_call | solution.py:31
  2.7 2.4 %collective-permute-start.1 = (bf16[48,1152]{1,0:T(8,128)(2,1)S(1)}, bf16[48,1152]{1,0:T(8,128)(2,1)S(1)}, u32[]{:S(2)}, u32[]{:S(2)}) collective-permute-start(bf16[48,1152]{1,0:T(8,128)(2,1)S(1)} %get-tuple-element.24), channel_id=1, source_target_pairs={{0,24},{1,25},{2,26},{3,27},{4,28},{5,29},{6,30},{7,31},{8,16},{9,... | collective-permute-start | bytes 331784 | tf_op jit(solution)/shard_map/ppermute | solution.py:417
  5.1 0.7 %collective-permute-start.2 = (bf16[48,1152]{1,0:T(8,128)(2,1)S(1)}, bf16[48,1152]{1,0:T(8,128)(2,1)S(1)}, u32[]{:S(2)}, u32[]{:S(2)}) collective-permute-start(bf16[48,1152]{1,0:T(8,128)(2,1)S(1)} %get-tuple-element.24), channel_id=1, source_target_pairs={{0,8},{1,9},{2,10},{3,11},{4,12},{5,13},{6,14},{7,15},{8,0},{9,1},... | collective-permute-start | bytes 331784 | tf_op jit(solution)/shard_map/ppermute | solution.py:417
  5.8 0.0 collective-permute-start.3
  5.8 1.6 %collective-permute-start.5 = (bf16[48,1152]{1,0:T(8,128)(2,1)S(1)}, bf16[48,1152]{1,0:T(8,128)(2,1)S(1)}, u32[]{:S(2)}, u32[]{:S(2)}) collective-permute-start(bf16[48,1152]{1,0:T(8,128)(2,1)S(1)} %get-tuple-element.30), channel_id=1, source_target_pairs={{0,9},{1,10},{2,11},{3,12},{4,13},{5,14},{6,15},{7,8},{8,1},{9,2},... | collective-permute-start | bytes 331784 | tf_op jit(solution)/shard_map/ppermute | solution.py:417
  7.5 0.5 %collective-permute-start = (bf16[48,1152]{1,0:T(8,128)(2,1)S(1)}, bf16[48,1152]{1,0:T(8,128)(2,1)S(1)}, u32[]{:S(2)}, u32[]{:S(2)}) collective-permute-start(bf16[48,1152]{1,0:T(8,128)(2,1)S(1)} %get-tuple-element.23.refs_2_), channel_id=1, source_target_pairs={{0,16},{1,17},{2,18},{3,19},{4,20},{5,21},{6,22},{7,23},{8,24},{9,... | collective-permute-start | bytes 331784 | tf_op jit(solution)/shard_map/ppermute | solution.py:417
  8.0 2.9 %shard_map.68 = (bf16[24,144,256]{2,1,0:T(8,128)(2,1)S(1)}, bf16[24,144,256]{2,1,0:T(8,128)(2,1)S(1)}, bf16[4,288,768]{2,1,0:T(8,128)(2,1)S(1)}, bf16[192,192]{1...) custom-call(s32[2,4]{1,0:T(2,128)S(1)} %copy-done.5, ...), custom_call_target="tpu_custom_call" | custom-call | flops 3000000000 | tf_op jit(solution)/shard_map/pallas_call | solution.py:31
  11.0 0.0 copy-start.6
  11.0 0.7 %copy-done.6 = bf16[384,384]{1,0:T(8,128)(2,1)} copy-done((bf16[384,384]{1,0:T(8,128)(2,1)}, bf16[384,384]{1,0:T(8,128)(2,1)S(1)}, u32[]{:S(2)}) %copy-start.6) | copy-done | bytes 294936
  11.7 0.8 %collective-permute-done.refs_0_ = bf16[48,1152]{1,0:T(8,128)(2,1)S(1)} collective-permute-done((bf16[48,1152]{1,0:T(8,128)(2,1)S(1)}, bf16[48,1152]{1,0:T(8,128)(2,1)S(1)}, u32[]{:S(2)}, u32[]{:S(2)}) %collective-permute-start) | collective-permute-done | bytes 110624 | tf_op jit(solution)/shard_map/ppermute | solution.py:417
  12.4 1.5 %collective-permute-start.4 = (bf16[48,1152]{1,0:T(8,128)(2,1)S(1)}, bf16[48,1152]{1,0:T(8,128)(2,1)S(1)}, u32[]{:S(2)}, u32[]{:S(2)}) collective-permute-start(bf16[48,1152]{1,0:T(8,128)(2,1)S(1)} %get-tuple-element.29.b_own), channel_id=1, source_target_pairs={{0,1},{1,2},{2,3},{3,4},{4,5},{5,6},{6,7},{7,0},{8,9},{9,10},{10,1... | collective-permute-start | bytes 331784 | tf_op jit(solution)/shard_map/ppermute | solution.py:417
  13.9 0.0 collective-permute-done.1.refs_1_
  13.9 0.0 collective-permute-done.2.refs_3_
  13.9 3.9 %shard_map.70 = (bf16[1536,1152]{1,0:T(8,128)(2,1)S(1)}, bf16[2,48,1152]{2,1,0:T(8,128)(2,1)}, bf16[2,48,1152]{2,1,0:T(8,128)(2,1)}) custom-call(bf16[48,1152]{1,0:T(8,128)(2,1)S(1)} %collective-permute-done.refs_0_, bf16[48,1152]{1,0:T(8,128)(2,1)S(1)} %collective-permute-done.1.refs_1_, bf16[48,1152]{1,0:T(8,128)(2,1)S(1)} %get-tuple-element.23.refs_2_, ...), custom_call_target="tpu_custom_call" | custom-call | flops 4000000000 | tf_op jit(solution)/shard_map/pallas_call | solution.py:31
  17.8 3.5 %collective-permute-start.6 = (bf16[2,48,1152]{2,1,0:T(8,128)(2,1)}, bf16[2,48,1152]{2,1,0:T(8,128)(2,1)}, u32[]{:S(2)}, u32[]{:S(2)}) collective-permute-start(bf16[2,48,1152]{2,1,0:T(8,128)(2,1)} %get-tuple-element.34), channel_id=1, source_target_pairs={{0,0},{1,2},{2,1},{3,4},{4,3},{5,6},{6,5},{7,7},{8,8},{9,10},{10,9... | collective-permute-start | bytes 663560 | tf_op jit(solution)/shard_map/ppermute | solution.py:417
  21.3 1.5 %collective-permute-start.7 = (bf16[2,48,1152]{2,1,0:T(8,128)(2,1)}, bf16[2,48,1152]{2,1,0:T(8,128)(2,1)}, u32[]{:S(2)}, u32[]{:S(2)}) collective-permute-start(bf16[2,48,1152]{2,1,0:T(8,128)(2,1)} %get-tuple-element.35), channel_id=1, source_target_pairs={{0,1},{1,0},{2,3},{3,2},{4,5},{5,4},{6,7},{7,6},{8,9},{9,8},{10,11... | collective-permute-start | bytes 663560 | tf_op jit(solution)/shard_map/ppermute | solution.py:417
  22.8 0.0 collective-permute-done.3.b_far
  22.8 0.0 collective-permute-done.4.prev_own
  22.8 0.0 collective-permute-done.5.prev_far
  22.8 2.1 %shard_map.71 = (f32[4,8,8,128]{3,2,1,0:T(8,128)S(1)}, f32[8,128]{1,0:T(8,128)S(1)}) custom-call(bf16[48,1152]{1,0:T(8,128)(2,1)S(1)} %get-tuple-element.29.b_own, bf16[48,1152]{1,0:T(8,128)(2,1)S(1)} %collective-permute-done.3.b_far, bf16[48,1152]{1,0:T(8,128)(2,1)S(1)} %collective-permute-done.4.prev_own, ...), custom_call_target="tpu_custom_call" | custom-call | flops 3000000000 | tf_op jit(solution)/shard_map/pallas_call | solution.py:31
  24.9 0.6 %copy-done.2 = f32[4,8,8,128]{3,2,1,0:T(8,128)} copy-done((f32[4,8,8,128]{3,2,1,0:T(8,128)}, f32[4,8,8,128]{3,2,1,0:T(8,128)S(1)}, u32[]{:S(2)}) %copy-start.2) | copy-done | bytes 131096
  25.5 4.4 %all-to-all-start = ((f32[32,8,128]{2,1,0:T(8,128)}), f32[32,8,128]{2,1,0:T(8,128)}, u32[]{:S(2)}, u32[]{:S(2)}) async-start(f32[32,8,128]{2,1,0:T(8,128)} %bitcast.5), calls=%async_computation | async-start | bytes 262144 | tf_op jit(solution)/shard_map/all_to_all | solution.py:482
  29.9 1.5 %copy-done.1 = bf16[4,288,768]{2,1,0:T(8,128)(2,1)S(1)} copy-done((bf16[4,288,768]{2,1,0:T(8,128)(2,1)S(1)}, bf16[4,288,768]{2,1,0:T(8,128)(2,1)}, u32[]{:S(2)}) %copy-start.1) | copy-done | bytes 1769496
  31.4 0.9 %shard_map.72.own = f32[2,48,1152]{2,1,0:T(8,128)S(1)} custom-call(bf16[4,288,768]{2,1,0:T(8,128)(2,1)S(1)} %copy-done.1, bf16[1536,1152]{1,0:T(8,128)(2,1)S(1)} %get-tuple-element.28.terms_ref, f32[8,128]{1,0:T(8,128)S(1)} %get-tuple-element.33.after_ref), custom_call_target="tpu_custom_call" | custom-call | flops 1000000000 | tf_op jit(solution)/shard_map/pallas_call | solution.py:31
  32.3 0.0 collective-permute-done.6.after
  32.3 0.0 collective-permute-done.7.pair
  32.3 1.1 %shard_map.73 = (bf16[48,1152]{1,0:T(8,128)(2,1)S(1)}, bf16[48,1152]{1,0:T(8,128)(2,1)S(1)}) custom-call(f32[2,48,1152]{2,1,0:T(8,128)S(1)} %shard_map.72.own, bf16[2,48,1152]{2,1,0:T(8,128)(2,1)} %collective-permute-done.6.after, bf16[2,48,1152]{2,1,0:T(8,128)(2,1)} %collective-permute-done.7.pair), custom_call_target="tpu_custom_call" | custom-call | flops 100000000 | tf_op jit(solution)/shard_map/pallas_call | solution.py:31
  33.5 0.2 collective-permute-start.8
  33.7 1.2 %collective-permute-done.8.other = bf16[48,1152]{1,0:T(8,128)(2,1)S(1)} collective-permute-done((bf16[48,1152]{1,0:T(8,128)(2,1)S(1)}, bf16[48,1152]{1,0:T(8,128)(2,1)S(1)}, u32[]{:S(2)}, u32[]{:S(2)}) %collective-permute-start.8) | collective-permute-done | bytes 110624 | tf_op jit(solution)/shard_map/ppermute | solution.py:417
  34.8 1.2 %shard_map.74 = (bf16[2,24,8,288]{3,2,1,0:T(8,128)(2,1)}, f32[8,128]{1,0:T(8,128)S(1)}) custom-call(bf16[48,1152]{1,0:T(8,128)(2,1)S(1)} %get-tuple-element.36.mine, bf16[48,1152]{1,0:T(8,128)(2,1)S(1)} %collective-permute-done.8.other, bf16[384,384]{1,0:T(8,128)(2,1)S(1)} %copy-done.7), custom_call_target="tpu_custom_call" | custom-call | flops 1000000000 | tf_op jit(solution)/shard_map/pallas_call | solution.py:31
  36.0 1.6 %all-to-all-done = f32[32,8,128]{2,1,0:T(8,128)} async-done(((f32[32,8,128]{2,1,0:T(8,128)}), f32[32,8,128]{2,1,0:T(8,128)}, u32[]{:S(2)}, u32[]{:S(2)}) %all-to-all-start) | async-done | bytes 131104 | tf_op jit(solution)/shard_map/all_to_all | solution.py:482
  37.6 1.6 %shard_map.75 = f32[2,3,8,24]{3,2,1,0:T(8,128)} custom-call(f32[4,8,8,128]{3,2,1,0:T(8,128)} %bitcast.3.in_ref, f32[8,128]{1,0:T(8,128)S(1)} %get-tuple-element.41.after_ref), custom_call_target="tpu_custom_call" | custom-call | flops 500000000 | tf_op jit(solution)/shard_map/pallas_call | solution.py:31
  (12 shorter events, 0.0 us)
Async XLA Ops:
  0.6 7.4 %copy-start.4 = (f32[2,3,144]{2,0,1:T(2,128)S(1)}, f32[2,3,144]{2,0,1:T(2,128)}, u32[]{:S(2)}) copy-start(f32[2,3,144]{2,0,1:T(2,128)} %param.7) | copy-start | bytes 10372
  0.6 7.4 %copy-start.3 = (bf16[2,8,24,3,8]{2,4,3,1,0:T(8,128)(2,1)S(1)}, bf16[2,8,24,3,8]{2,4,3,1,0:T(8,128)(2,1)}, u32[]{:S(2)}) copy-start(bf16[2,8,24,3,8]{2,4,3,1,0:T(8,128)(2,1)} %param.9) | copy-start | bytes 55300
  0.7 7.3 %copy-start.5 = (s32[2,4]{1,0:T(2,128)S(1)}, s32[2,4]{1,0:T(2,128)}, u32[]{:S(2)}) copy-start(s32[2,4]{1,0:T(2,128)} %near_ref.1) | copy-start | bytes 100
  2.7 11.2 %collective-permute-start.1 = (bf16[48,1152]{1,0:T(8,128)(2,1)S(1)}, bf16[48,1152]{1,0:T(8,128)(2,1)S(1)}, u32[]{:S(2)}, u32[]{:S(2)}) collective-permute-start(bf16[48,1152]{1,0:T(8,128)(2,1)S(1)} %get-tuple-element.24), channel_id=1, source_target_pairs={{0,24},{1,25},{2,26},{3,27},{4,28},{5,29},{6,30},{7,31},{8,16},{9,... | collective-permute-start | bytes 331784 | tf_op jit(solution)/shard_map/ppermute | solution.py:417
  5.1 8.8 %collective-permute-start.2 = (bf16[48,1152]{1,0:T(8,128)(2,1)S(1)}, bf16[48,1152]{1,0:T(8,128)(2,1)S(1)}, u32[]{:S(2)}, u32[]{:S(2)}) collective-permute-start(bf16[48,1152]{1,0:T(8,128)(2,1)S(1)} %get-tuple-element.24), channel_id=1, source_target_pairs={{0,8},{1,9},{2,10},{3,11},{4,12},{5,13},{6,14},{7,15},{8,0},{9,1},... | collective-permute-start | bytes 331784 | tf_op jit(solution)/shard_map/ppermute | solution.py:417
  5.8 17.0 %collective-permute-start.3 = (bf16[48,1152]{1,0:T(8,128)(2,1)S(1)}, bf16[48,1152]{1,0:T(8,128)(2,1)S(1)}, u32[]{:S(2)}, u32[]{:S(2)}) collective-permute-start(bf16[48,1152]{1,0:T(8,128)(2,1)S(1)} %get-tuple-element.30), channel_id=1, source_target_pairs={{0,8},{1,9},{2,10},{3,11},{4,12},{5,13},{6,14},{7,15},{8,0},{9,1},... | collective-permute-start | bytes 331784 | tf_op jit(solution)/shard_map/ppermute | solution.py:417
  5.8 17.0 %collective-permute-start.5 = (bf16[48,1152]{1,0:T(8,128)(2,1)S(1)}, bf16[48,1152]{1,0:T(8,128)(2,1)S(1)}, u32[]{:S(2)}, u32[]{:S(2)}) collective-permute-start(bf16[48,1152]{1,0:T(8,128)(2,1)S(1)} %get-tuple-element.30), channel_id=1, source_target_pairs={{0,9},{1,10},{2,11},{3,12},{4,13},{5,14},{6,15},{7,8},{8,1},{9,2},... | collective-permute-start | bytes 331784 | tf_op jit(solution)/shard_map/ppermute | solution.py:417
  7.5 5.0 %collective-permute-start = (bf16[48,1152]{1,0:T(8,128)(2,1)S(1)}, bf16[48,1152]{1,0:T(8,128)(2,1)S(1)}, u32[]{:S(2)}, u32[]{:S(2)}) collective-permute-start(bf16[48,1152]{1,0:T(8,128)(2,1)S(1)} %get-tuple-element.23.refs_2_), channel_id=1, source_target_pairs={{0,16},{1,17},{2,18},{3,19},{4,20},{5,21},{6,22},{7,23},{8,24},{9,... | collective-permute-start | bytes 331784 | tf_op jit(solution)/shard_map/ppermute | solution.py:417
  11.0 0.7 %copy-start.6 = (bf16[384,384]{1,0:T(8,128)(2,1)}, bf16[384,384]{1,0:T(8,128)(2,1)S(1)}, u32[]{:S(2)}) copy-start(bf16[384,384]{1,0:T(8,128)(2,1)S(1)} %get-tuple-element.38.perm_ref) | copy-start | bytes 884740
  11.7 6.1 %copy-start = (bf16[4,288,768]{2,1,0:T(8,128)(2,1)}, bf16[4,288,768]{2,1,0:T(8,128)(2,1)S(1)}, u32[]{:S(2)}) copy-start(bf16[4,288,768]{2,1,0:T(8,128)(2,1)S(1)} %get-tuple-element.22.refs_7_.t_ref) | copy-start | bytes 5308420
  12.4 10.4 %collective-permute-start.4 = (bf16[48,1152]{1,0:T(8,128)(2,1)S(1)}, bf16[48,1152]{1,0:T(8,128)(2,1)S(1)}, u32[]{:S(2)}, u32[]{:S(2)}) collective-permute-start(bf16[48,1152]{1,0:T(8,128)(2,1)S(1)} %get-tuple-element.29.b_own), channel_id=1, source_target_pairs={{0,1},{1,2},{2,3},{3,4},{4,5},{5,6},{6,7},{7,0},{8,9},{9,10},{10,1... | collective-permute-start | bytes 331784 | tf_op jit(solution)/shard_map/ppermute | solution.py:417
  17.8 14.5 %collective-permute-start.6 = (bf16[2,48,1152]{2,1,0:T(8,128)(2,1)}, bf16[2,48,1152]{2,1,0:T(8,128)(2,1)}, u32[]{:S(2)}, u32[]{:S(2)}) collective-permute-start(bf16[2,48,1152]{2,1,0:T(8,128)(2,1)} %get-tuple-element.34), channel_id=1, source_target_pairs={{0,0},{1,2},{2,1},{3,4},{4,3},{5,6},{6,5},{7,7},{8,8},{9,10},{10,9... | collective-permute-start | bytes 663560 | tf_op jit(solution)/shard_map/ppermute | solution.py:417
  21.3 11.0 %collective-permute-start.7 = (bf16[2,48,1152]{2,1,0:T(8,128)(2,1)}, bf16[2,48,1152]{2,1,0:T(8,128)(2,1)}, u32[]{:S(2)}, u32[]{:S(2)}) collective-permute-start(bf16[2,48,1152]{2,1,0:T(8,128)(2,1)} %get-tuple-element.35), channel_id=1, source_target_pairs={{0,1},{1,0},{2,3},{3,2},{4,5},{5,4},{6,7},{7,6},{8,9},{9,8},{10,11... | collective-permute-start | bytes 663560 | tf_op jit(solution)/shard_map/ppermute | solution.py:417
  24.9 0.7 %copy-start.2 = (f32[4,8,8,128]{3,2,1,0:T(8,128)}, f32[4,8,8,128]{3,2,1,0:T(8,128)S(1)}, u32[]{:S(2)}) copy-start(f32[4,8,8,128]{3,2,1,0:T(8,128)S(1)} %get-tuple-element.40) | copy-start | bytes 393220
  25.5 12.1 %all-to-all-start = ((f32[32,8,128]{2,1,0:T(8,128)}), f32[32,8,128]{2,1,0:T(8,128)}, u32[]{:S(2)}, u32[]{:S(2)}) async-start(f32[32,8,128]{2,1,0:T(8,128)} %bitcast.5), calls=%async_computation | async-start | bytes 262144 | tf_op jit(solution)/shard_map/all_to_all | solution.py:482
  29.9 1.5 %copy-start.1 = (bf16[4,288,768]{2,1,0:T(8,128)(2,1)S(1)}, bf16[4,288,768]{2,1,0:T(8,128)(2,1)}, u32[]{:S(2)}) copy-start(bf16[4,288,768]{2,1,0:T(8,128)(2,1)} %copy-done) | copy-start | bytes 5308420
  31.4 3.5 %copy-start.7 = (bf16[384,384]{1,0:T(8,128)(2,1)S(1)}, bf16[384,384]{1,0:T(8,128)(2,1)}, u32[]{:S(2)}) copy-start(bf16[384,384]{1,0:T(8,128)(2,1)} %copy-done.6) | copy-start | bytes 884740
  33.5 1.4 %collective-permute-start.8 = (bf16[48,1152]{1,0:T(8,128)(2,1)S(1)}, bf16[48,1152]{1,0:T(8,128)(2,1)S(1)}, u32[]{:S(2)}, u32[]{:S(2)}) collective-permute-start(bf16[48,1152]{1,0:T(8,128)(2,1)S(1)} %get-tuple-element.37), channel_id=1, source_target_pairs={{0,8},{1,9},{2,10},{3,11},{4,12},{5,13},{6,14},{7,15},{8,0},{9,1},... | collective-permute-start | bytes 331784 | tf_op jit(solution)/shard_map/ppermute | solution.py:417

commit v4 on v3

--- a/solution.py
+++ b/solution.py
@@ -27,7 +27,7 @@
     return lax.dot_general(a, b, (((1,), (1,)), ((), ())), preferred_element_type=F32)
 
 
-def call(kernel, outs, ins, work, scratch=(), specs=None, limit=12):
+def call(kernel, outs, ins, work, scratch=(), specs=None, limit=24):
     return pl.pallas_call(
         kernel,
         out_shape=outs,
@@ -60,7 +60,7 @@
     return jax.ShapeDtypeStruct(dims, dtype)
 
 
-def pack_kernel(g_hbm, b_hbm, g_own, b_own, g_far, b_far, g_ref, b_ref, halves, sems):
+def pack_kernel(g_hbm, b_hbm, g_own, g_send, g_far, b_own, b_far, g_ref, b_ref, halves, sems):
     core = my_core()
     copies = []
     for i, (src, dst) in enumerate(((g_hbm, g_ref), (b_hbm, b_ref))):
@@ -81,6 +81,12 @@
             halves[h] = jnp.concatenate(parts, axis=1)
         own[...] = halves[core].astype(BF)
         far[...] = halves[1 - core].astype(BF)
+    g_send[...] = g_own[...]
+
+
+def pair_kernel(first_ref, second_ref, out_ref):
+    out_ref[0] = first_ref[...]
+    out_ref[1] = second_ref[...]
 
 
 def table_kernel(
@@ -199,7 +205,7 @@
     core = my_core()
     blocks = refs[: 2 * chips]
     perm_ref, hi_ref, lo_ref, t_ref = refs[2 * chips : 2 * chips + 4]
-    terms_ref, pair_ref, next_ref, gathered, result = refs[2 * chips + 4 :]
+    high_ref, own_ref, pair_ref, next_ref, gathered, terms_ref, result = refs[2 * chips + 5 :]
     for s in range(chips):
         n = 2 * ((s - 1) % chips)
         gathered[2 * s + core] = blocks[n][...]
@@ -233,10 +239,11 @@
                 terms_ref[at + depth : at + 2 * LANES, :] = jnp.zeros((spare, width), BF)
         for i in range(tiles):
             high = sums[m][i].astype(BF)
+            high_ref[m, :, i * LANES : (i + 1) * LANES] = high
             for n, part in enumerate((high, (sums[m][i] - high.astype(F32)).astype(BF))):
                 at = (3 * n + m) * 2 * LANES
                 terms_ref[at : at + depth, i * LANES : (i + 1) * LANES] = part
-    correlate(t_ref, 0, 4, terms_ref, result, entries)
+    correlate(t_ref, terms_ref, result, entries)
     place = lax.axis_index("en")
     odd = lax.rem(place, 2)
     below = jnp.where(place == 0, 0.0, 1.0)
@@ -246,17 +253,18 @@
     for i, c in enumerate((core, 1 - core)):
         pair_ref[i] = (result[2 - 2 * odd + c] * keep_pair).astype(BF)
         next_ref[i] = (result[2 * odd + c] * keep_next).astype(BF)
-
-
-def correlate(t_ref, begin_row, count, terms_ref, result, entries):
-    _, rows, width = result.shape
+        own_ref[i] = result[4 + c]
+
+
+def correlate(t_ref, terms_ref, result, entries):
+    count, rows, width = result.shape
     lane = index((1, LANES), 1)
     carried = None
     for p in range(width // entries):
         begin = entries * p
         first = begin // LANES
         last = (begin + entries - 1) // LANES
-        t = t_ref[p, begin_row * rows : (begin_row + count) * rows, :]
+        t = t_ref[p]
         total = dot(jnp.concatenate([t, t], axis=1), terms_ref[:, first * LANES : (last + 1) * LANES])
         for i in range(first, last + 1):
             tile = total[:, (i - first) * LANES : (i - first + 1) * LANES]
@@ -269,17 +277,12 @@
                     result[r, :, i * LANES : (i + 1) * LANES] = tile[r * rows : (r + 1) * rows]
 
 
-def own_kernel(t_ref, terms_ref, after_ref, own_ref, *, entries):
-    correlate(t_ref, 4, 2, terms_ref, own_ref, entries)
-
-
-def polar_kernel(b_own, b_far, prev_own, prev_far, turn_ref, sort_ref, terms_ref, out_ref, mark_ref, gathered, *, half, entries, momenta, local_k, local_e, scale):
+def polar_kernel(b_ref, prev_ref, turn_ref, sort_ref, high_ref, out_ref, gathered, *, half, entries, momenta, local_k, local_e, scale):
     core = my_core()
     present = jnp.where(lax.axis_index("en") == 0, 0.0, 1.0)
-    gathered[core] = (prev_own[...].astype(F32) * present).astype(BF)
-    gathered[1 - core] = (prev_far[...].astype(F32) * present).astype(BF)
-    gathered[2 + core] = b_own[...]
-    gathered[3 - core] = b_far[...]
+    for i, c in enumerate((core, 1 - core)):
+        gathered[c] = (prev_ref[i].astype(F32) * present).astype(BF)
+        gathered[2 + c] = b_ref[i]
     count, rows, width = gathered.shape
     tiles = width // LANES
     b = dot(sort_ref[...], gathered[...].reshape(count * rows, width)).astype(BF)
@@ -295,9 +298,7 @@
     group = 2 * local_e
     columns = sort_ref.shape[0]
     window = local_e
-    depth = local_e * momenta
     lane = index((1, LANES), 1)
-    mark_ref[...] = jnp.zeros(mark_ref.shape, F32)
     pieces = []
     for p in range(half):
         begin = entries * p
@@ -314,7 +315,7 @@
         rhs = jnp.concatenate(parts, axis=1)
         held = None
         for m in range(3):
-            s = dot_t(terms_ref[m * 2 * LANES : m * 2 * LANES + depth, first * LANES : (last + 1) * LANES], rhs)
+            s = dot_t(high_ref[m, :, first * LANES : (last + 1) * LANES], rhs)
             acc = None
             for e in range(local_e):
                 row = pltpu.roll(s[e * momenta : (e + 1) * momenta], columns - (local_e - e), 1)
@@ -358,9 +359,8 @@
 
 
 def sum_kernel(own, after, pair, mine, theirs):
-    core = my_core()
-    for n, i, out in ((0, core, mine), (1, 1 - core, theirs)):
-        out[...] = (own[i] + pair[n].astype(F32) + after[n].astype(F32)).astype(BF)
+    for n, out in enumerate((mine, theirs)):
+        out[...] = (own[n] + pair[n].astype(F32) + after[n].astype(F32)).astype(BF)
 
 
 def join_kernel(mine, other, perm_ref, out_ref, mark_ref, halves):
@@ -393,9 +393,9 @@
 
     deriv = derivative.transpose(1, 0, 2)
     weights = phonon.transpose(0, 1, 3, 4, 2)
-    g_own, b_own, g_far, b_far = call(
+    g_own, g_send, g_far, b_own, b_far = call(
         pack_kernel,
-        [shape((rows, width), BF)] * 4,
+        [shape((rows, width), BF)] * 5,
         [green_less, green_greater],
         1.5,
         [
@@ -405,7 +405,7 @@
             pltpu.SemaphoreType.DMA((2,)),
         ],
         [HBM] * 2,
-        limit=53.25,
+        limit=53.2,
     )
 
     def move(value, dchip, dcore, to=lambda e: e):
@@ -428,11 +428,10 @@
 
     blocks = []
     for s in range(1, chips):
-        blocks += [move(g_far, -s, 1), move(g_own, -s, 0)][::-1]
+        blocks += [move(g_far, -s, 1), move(g_send, -s, 0)][::-1]
     blocks += [g_own, move(g_far, 0, 1)]
-    b_core = move(b_far, 0, 1)
-    prev_own = move(b_own, 0, 0, onward)
-    prev_far = move(b_far, 0, 1, onward)
+    (b_both,) = call(pair_kernel, [shape((2, rows, width), BF)], [b_own, move(b_far, 0, 1)], 0.2)
+    prev_both = move(b_both, 0, 0, onward)
 
     near = neighbours.astype(jnp.int32)
     columns = -(-chip_k * 2 * local_e // LANES) * LANES
@@ -456,36 +455,37 @@
         [pl.BlockSpec(memory_space=pltpu.SMEM), VMEM, VMEM],
     )
 
-    source_terms, to_pair_rows, to_next_rows = call(
+    high, own, to_pair_rows, to_next_rows = call(
         functools.partial(product_kernel, half=half, entries=entries, chips=chips),
         [
-            shape((12 * LANES, width), BF),
+            shape((3, momenta * local_e, width), BF),
+            shape((2, rows, width), F32),
             shape((2, rows, width), BF),
             shape((2, rows, width), BF),
         ],
-        blocks + [to_energy, k_hi, k_lo, toeplitz],
+        blocks + [to_energy, k_hi, k_lo, toeplitz, prev_both],
         4,
-        [pltpu.VMEM((2 * chips, rows, width), BF), pltpu.VMEM((4, rows, width), F32)],
+        [
+            pltpu.VMEM((2 * chips, rows, width), BF),
+            pltpu.VMEM((12 * LANES, width), BF),
+            pltpu.VMEM((6, rows, width), F32),
+        ],
     )
     from_next = move(to_next_rows, 0, 0, to_next)
     from_pair = move(to_pair_rows, 0, 0, to_pair)
-    partial, done = call(
+    (partial,) = call(
         functools.partial(
             polar_kernel, half=half, entries=entries, momenta=momenta, local_k=local_k, local_e=local_e,
             scale=1.0 / (NO * float(np.sqrt(momenta * total_e))),
         ),
-        [shape((mom, en, local_k * half, LANES), F32), shape((8, LANES), F32)],
-        [b_own, b_core, prev_own, prev_far, turn, sort_e, source_terms],
+        [shape((mom, en, local_k * half, LANES), F32)],
+        [b_both, prev_both, turn, sort_e, high],
         3,
         [pltpu.VMEM((4, rows, width), BF)],
     )
     terms = lax.all_to_all(
         partial.reshape(mom * en, local_k * half, LANES), ("mom", "en"), split_axis=0, concat_axis=0, tiled=True
     )
-    (own,) = call(
-        functools.partial(own_kernel, entries=entries), [shape((2, rows, width), F32)], [toeplitz, source_terms, done], 1
-    )
-
     mine, theirs = call(
         sum_kernel, [shape((rows, width), BF)] * 2, [own, from_next, from_pair], 0.1
     )

time: 39.6 us -> 38.9 us (0.982)
  waiting for transfers between devices: 3.53 us -> 12.2 us
  starting transfers between devices: 16.4 us -> 12.4 us
  local copies, waits for them, and re-layouts: 2.84 us -> 0.01 us
  Pallas kernels: 15.7 us -> 13.4 us
    ppermute x9 -> x8, waiting for transfers between devices: 1.92 us -> 7.85 us  [move(): return lax.ppermute(value, ('mom', 'en'), links)]
    ppermute x9 -> x8, starting transfers between devices: 12 us -> 8.48 us  [move(): return lax.ppermute(value, ('mom', 'en'), links)]
    unnamed x16 -> x6, local copies, waits for them, and re-layouts: 2.84 us -> 0.01 us
    all_to_all x1, waiting for transfers between devices: 1.6 us -> 4.37 us  [body(): lax.all_to_all(partial.reshape(mom * en, local_k * half, LANES), ('mom',...]
    pallas_call x8, Pallas kernels: 15.7 us -> 13.4 us  [call(): pl.pallas_call(kernel, out_shape=outs, in_specs=specs or [VMEM] * len(ins...]
    all_to_all x1, starting transfers between devices: 4.37 us -> 3.88 us  [body(): lax.all_to_all(partial.reshape(mom * en, local_k * half, LANES), ('mom',...]
  transfers between devices with their start and end apart: 10 -> 9, of which waited for: 3 -> 5; matrix products, arithmetic and copies ran while one was open for 0% -> 0% of each run, Pallas kernels for 31% -> 18%
where the time goes in v4:
time: 38.9 us; the launch traced here: 38.7 us
  Pallas kernels  13.4 us (34%)
  starting transfers between devices  12.4 us (32%)
  waiting for transfers between devices  12.2 us (31%)
  between operations  0.72 us (2%)
    pallas_call x8, Pallas kernels, call(): pl.pallas_call(kernel, out_shape=outs, in_specs=specs or [VMEM] * len(ins...  13.4 us
    ppermute x8, starting transfers between devices, move(): return lax.ppermute(value, ('mom', 'en'), links)  8.48 us
    ppermute x8, waiting for transfers between devices, move(): return lax.ppermute(value, ('mom', 'en'), links)  7.85 us
    all_to_all x1, waiting for transfers between devices, body(): lax.all_to_all(partial.reshape(mom * en, local_k * half, LANES), ('mom',...  4.37 us
    all_to_all x1, starting transfers between devices, body(): lax.all_to_all(partial.reshape(mom * en, local_k * half, LANES), ('mom',...  3.88 us
  transfers between devices with their start and end apart: 9, of which 5 were waited for; matrix products, arithmetic and copies ran while one was open for 0% of the time, Pallas kernels for 18%

profile of v4, /device:TPU:0, one launch (start us, length us, event | category | flops | bytes accessed | tf_op | source)
XLA Modules:
  0.0 38.7 jit_solution(4361318173963131015)
XLA Ops:
  0.6 0.0 copy-start
  0.6 0.0 copy-start.2
  0.7 0.0 copy-start.1
  0.7 2.0 %shard_map.68 = (bf16[48,1152]{1,0:T(8,128)(2,1)S(1)}, bf16[48,1152]{1,0:T(8,128)(2,1)S(1)}, bf16[48,1152]{1,0:T(8,128)(2,1)S(1)}, bf16[48,1152]{1,0:T(8,128)(2,1)S(1)}, bf16[48,1152]{1,0:T(8,128)(2,1)S(1)}) custom-call(bf16[2,24,8,288]{3,2,1,0:T(8,128)(2,1)} %g_hbm.1, bf16[2,24,8,288]{3,2,1,0:T(8,128)(2,1)} %b_hbm.1), custom_call_target="tpu_custom_call" | custom-call | flops 1500000000 | tf_op jit(solution)/shard_map/pallas_call | solution.py:31
  2.7 0.5 %collective-permute-start.3 = (bf16[48,1152]{1,0:T(8,128)(2,1)S(1)}, bf16[48,1152]{1,0:T(8,128)(2,1)S(1)}, u32[]{:S(2)}, u32[]{:S(2)}) collective-permute-start(bf16[48,1152]{1,0:T(8,128)(2,1)S(1)} %get-tuple-element.30), channel_id=1, source_target_pairs={{0,8},{1,9},{2,10},{3,11},{4,12},{5,13},{6,14},{7,15},{8,0},{9,1},... | collective-permute-start | bytes 331784 | tf_op jit(solution)/shard_map/ppermute | solution.py:417
  3.2 0.1 collective-permute-start.2
  3.3 2.6 %collective-permute-start.1 = (bf16[48,1152]{1,0:T(8,128)(2,1)S(1)}, bf16[48,1152]{1,0:T(8,128)(2,1)S(1)}, u32[]{:S(2)}, u32[]{:S(2)}) collective-permute-start(bf16[48,1152]{1,0:T(8,128)(2,1)S(1)} %get-tuple-element.23), channel_id=1, source_target_pairs={{0,24},{1,25},{2,26},{3,27},{4,28},{5,29},{6,30},{7,31},{8,16},{9,... | collective-permute-start | bytes 331784 | tf_op jit(solution)/shard_map/ppermute | solution.py:417
  5.9 0.3 collective-permute-start
  6.3 0.0 collective-permute-done.3.second_ref
  6.3 1.8 %collective-permute-start.4 = (bf16[2,48,1152]{2,1,0:T(8,128)(2,1)S(1)}, bf16[2,48,1152]{2,1,0:T(8,128)(2,1)S(1)}, u32[]{:S(2)}, u32[]{:S(2)}) collective-permute-start(bf16[2,48,1152]{2,1,0:T(8,128)(2,1)S(1)} %shard_map.70.b_ref), channel_id=1, source_target_pairs={{0,1},{1,2},{2,3},{3,4},{4,5},{5,6},{6,7},{7,0},{8,9},{9,10},{10,1... | collective-permute-start | bytes 663560 | tf_op jit(solution)/shard_map/ppermute | solution.py:417
  8.0 0.0 copy-done
  8.0 0.0 copy-done.2
  8.0 0.0 copy-done.1
  8.0 2.9 %shard_map.69 = (bf16[24,144,256]{2,1,0:T(8,128)(2,1)S(1)}, bf16[24,144,256]{2,1,0:T(8,128)(2,1)S(1)}, bf16[4,288,768]{2,1,0:T(8,128)(2,1)S(1)}, bf16[192,192]{1...) custom-call(s32[2,4]{1,0:T(2,128)S(1)} %copy-done.2, ...), custom_call_target="tpu_custom_call" | custom-call | flops 3000000000 | tf_op jit(solution)/shard_map/pallas_call | solution.py:31
  11.0 0.9 %collective-permute-done.refs_0_ = bf16[48,1152]{1,0:T(8,128)(2,1)S(1)} collective-permute-done((bf16[48,1152]{1,0:T(8,128)(2,1)S(1)}, bf16[48,1152]{1,0:T(8,128)(2,1)S(1)}, u32[]{:S(2)}, u32[]{:S(2)}) %collective-permute-start) | collective-permute-done | bytes 110624 | tf_op jit(solution)/shard_map/ppermute | solution.py:417
  11.9 0.0 collective-permute-done.2.refs_3_
  11.9 0.0 collective-permute-done.1.refs_1_
  11.9 4.9 %collective-permute-done.4.refs_8_.prev_ref = bf16[2,48,1152]{2,1,0:T(8,128)(2,1)S(1)} collective-permute-done((bf16[2,48,1152]{2,1,0:T(8,128)(2,1)S(1)}, bf16[2,48,1152]{2,1,0:T(8,128)(2,1)S(1)}, u32[]{:S(2)}, u32[]{:S(2)}) %collective-permute-start.4) | collective-permute-done | bytes 221216 | tf_op jit(solution)/shard_map/ppermute | solution.py:417
  16.8 3.7 %shard_map.71 = (bf16[3,192,1152]{2,1,0:T(8,128)(2,1)S(1)}, f32[2,48,1152]{2,1,0:T(8,128)S(1)}, bf16[2,48,1152]{2,1,0:T(8,128)(2,1)S(1)}, bf16[2,48,1152]{2,1,0:T(8,128)(2,1)S(1)}) custom-call(bf16[48,1152]{1,0:T(8,128)(2,1)S(1)} %collective-permute-done.refs_0_, bf16[48,1152]{1,0:T(8,128)(2,1)S(1)} %collective-permute-done.1.refs_1_, ...), custom_call_target="tpu_custom_call" | custom-call | flops 4000000000 | tf_op jit(solution)/shard_map/pallas_call | solution.py:31
  20.5 0.7 %collective-permute-start.5 = (bf16[2,48,1152]{2,1,0:T(8,128)(2,1)S(1)}, bf16[2,48,1152]{2,1,0:T(8,128)(2,1)S(1)}, u32[]{:S(2)}, u32[]{:S(2)}) collective-permute-start(bf16[2,48,1152]{2,1,0:T(8,128)(2,1)S(1)} %get-tuple-element.32), channel_id=1, source_target_pairs={{0,0},{1,2},{2,1},{3,4},{4,3},{5,6},{6,5},{7,7},{8,8},{9,10},{10,9... | collective-permute-start | bytes 663560 | tf_op jit(solution)/shard_map/ppermute | solution.py:417
  21.2 2.4 %collective-permute-start.6 = (bf16[2,48,1152]{2,1,0:T(8,128)(2,1)S(1)}, bf16[2,48,1152]{2,1,0:T(8,128)(2,1)S(1)}, u32[]{:S(2)}, u32[]{:S(2)}) collective-permute-start(bf16[2,48,1152]{2,1,0:T(8,128)(2,1)S(1)} %get-tuple-element.33), channel_id=1, source_target_pairs={{0,1},{1,0},{2,3},{3,2},{4,5},{5,4},{6,7},{7,6},{8,9},{9,8},{10,11... | collective-permute-start | bytes 663560 | tf_op jit(solution)/shard_map/ppermute | solution.py:417
  23.6 2.7 %shard_map.74 = f32[4,8,8,128]{3,2,1,0:T(8,128)} custom-call(bf16[2,48,1152]{2,1,0:T(8,128)(2,1)S(1)} %shard_map.70.b_ref, bf16[2,48,1152]{2,1,0:T(8,128)(2,1)S(1)} %collective-permute-done.4.refs_8_.prev_ref, bf16[8,256,256]{2,1,0:T(8,128)(2,1)S(1)} %get-tuple-element.38.turn_ref, bf16[256,192]{1,0:T(8,128)(2,1)S(1)} %get-tuple-element.39.sort_ref, ...), custom_call_target="tpu_custom_call" | custom-call | flops 3000000000 | tf_op jit(solution)/shard_map/pallas_call | solution.py:31
  26.4 3.9 %all-to-all-start = ((f32[32,8,128]{2,1,0:T(8,128)}), f32[32,8,128]{2,1,0:T(8,128)S(1)}, u32[]{:S(2)}, u32[]{:S(2)}) async-start(f32[32,8,128]{2,1,0:T(8,128)} %bitcast.2), calls=%async_computation | async-start | bytes 262144 | tf_op jit(solution)/shard_map/all_to_all | solution.py:486
  30.2 0.0 collective-permute-done.5.after
  30.3 0.7 %collective-permute-done.6.pair = bf16[2,48,1152]{2,1,0:T(8,128)(2,1)S(1)} collective-permute-done((bf16[2,48,1152]{2,1,0:T(8,128)(2,1)S(1)}, bf16[2,48,1152]{2,1,0:T(8,128)(2,1)S(1)}, u32[]{:S(2)}, u32[]{:S(2)}) %collective-permute-start.6) | collective-permute-done | bytes 221216 | tf_op jit(solution)/shard_map/ppermute | solution.py:417
  31.0 0.1 shard_map.72
  31.0 0.1 collective-permute-start.7
  31.1 1.3 %collective-permute-done.7.other = bf16[48,1152]{1,0:T(8,128)(2,1)S(1)} collective-permute-done((bf16[48,1152]{1,0:T(8,128)(2,1)S(1)}, bf16[48,1152]{1,0:T(8,128)(2,1)S(1)}, u32[]{:S(2)}, u32[]{:S(2)}) %collective-permute-start.7) | collective-permute-done | bytes 110624 | tf_op jit(solution)/shard_map/ppermute | solution.py:417
  32.4 1.2 %shard_map.73 = (bf16[2,24,8,288]{3,2,1,0:T(8,128)(2,1)}, f32[8,128]{1,0:T(8,128)S(1)}) custom-call(bf16[48,1152]{1,0:T(8,128)(2,1)S(1)} %get-tuple-element.34.mine, bf16[48,1152]{1,0:T(8,128)(2,1)S(1)} %collective-permute-done.7.other, bf16[384,384]{1,0:T(8,128)(2,1)S(1)} %get-tuple-element.36.perm_ref), custom_call_target="tpu_custom_call" | custom-call | flops 1000000000 | tf_op jit(solution)/shard_map/pallas_call | solution.py:31
  33.6 4.4 %all-to-all-done = f32[32,8,128]{2,1,0:T(8,128)S(1)} async-done(((f32[32,8,128]{2,1,0:T(8,128)}), f32[32,8,128]{2,1,0:T(8,128)S(1)}, u32[]{:S(2)}, u32[]{:S(2)}) %all-to-all-start) | async-done | bytes 131104 | tf_op jit(solution)/shard_map/all_to_all | solution.py:486
  38.0 0.7 %shard_map.75 = f32[2,3,8,24]{3,2,1,0:T(8,128)} custom-call(f32[4,8,8,128]{3,2,1,0:T(8,128)S(1)} %bitcast.5, f32[8,128]{1,0:T(8,128)S(1)} %get-tuple-element.41.after_ref), custom_call_target="tpu_custom_call" | custom-call | flops 500000000 | tf_op jit(solution)/shard_map/pallas_call | solution.py:31
  (1 shorter events, 0.0 us)
Async XLA Ops:
  0.6 7.4 %copy-start = (bf16[2,8,24,3,8]{2,4,3,1,0:T(8,128)(2,1)S(1)}, bf16[2,8,24,3,8]{2,4,3,1,0:T(8,128)(2,1)}, u32[]{:S(2)}) copy-start(bf16[2,8,24,3,8]{2,4,3,1,0:T(8,128)(2,1)} %param.9) | copy-start | bytes 55300
  0.6 7.4 %copy-start.2 = (s32[2,4]{1,0:T(2,128)S(1)}, s32[2,4]{1,0:T(2,128)}, u32[]{:S(2)}) copy-start(s32[2,4]{1,0:T(2,128)} %near_ref.1) | copy-start | bytes 100
  0.7 7.4 %copy-start.1 = (f32[2,3,144]{2,0,1:T(2,128)S(1)}, f32[2,3,144]{2,0,1:T(2,128)}, u32[]{:S(2)}) copy-start(f32[2,3,144]{2,0,1:T(2,128)} %param.7) | copy-start | bytes 10372
  2.7 3.6 %collective-permute-start.3 = (bf16[48,1152]{1,0:T(8,128)(2,1)S(1)}, bf16[48,1152]{1,0:T(8,128)(2,1)S(1)}, u32[]{:S(2)}, u32[]{:S(2)}) collective-permute-start(bf16[48,1152]{1,0:T(8,128)(2,1)S(1)} %get-tuple-element.30), channel_id=1, source_target_pairs={{0,8},{1,9},{2,10},{3,11},{4,12},{5,13},{6,14},{7,15},{8,0},{9,1},... | collective-permute-start | bytes 331784 | tf_op jit(solution)/shard_map/ppermute | solution.py:417
  3.2 8.7 %collective-permute-start.2 = (bf16[48,1152]{1,0:T(8,128)(2,1)S(1)}, bf16[48,1152]{1,0:T(8,128)(2,1)S(1)}, u32[]{:S(2)}, u32[]{:S(2)}) collective-permute-start(bf16[48,1152]{1,0:T(8,128)(2,1)S(1)} %get-tuple-element.23), channel_id=1, source_target_pairs={{0,8},{1,9},{2,10},{3,11},{4,12},{5,13},{6,14},{7,15},{8,0},{9,1},... | collective-permute-start | bytes 331784 | tf_op jit(solution)/shard_map/ppermute | solution.py:417
  3.3 8.6 %collective-permute-start.1 = (bf16[48,1152]{1,0:T(8,128)(2,1)S(1)}, bf16[48,1152]{1,0:T(8,128)(2,1)S(1)}, u32[]{:S(2)}, u32[]{:S(2)}) collective-permute-start(bf16[48,1152]{1,0:T(8,128)(2,1)S(1)} %get-tuple-element.23), channel_id=1, source_target_pairs={{0,24},{1,25},{2,26},{3,27},{4,28},{5,29},{6,30},{7,31},{8,16},{9,... | collective-permute-start | bytes 331784 | tf_op jit(solution)/shard_map/ppermute | solution.py:417
  5.9 6.0 %collective-permute-start = (bf16[48,1152]{1,0:T(8,128)(2,1)S(1)}, bf16[48,1152]{1,0:T(8,128)(2,1)S(1)}, u32[]{:S(2)}, u32[]{:S(2)}) collective-permute-start(bf16[48,1152]{1,0:T(8,128)(2,1)S(1)} %get-tuple-element.22), channel_id=1, source_target_pairs={{0,16},{1,17},{2,18},{3,19},{4,20},{5,21},{6,22},{7,23},{8,24},{9,... | collective-permute-start | bytes 331784 | tf_op jit(solution)/shard_map/ppermute | solution.py:417
  6.3 10.6 %collective-permute-start.4 = (bf16[2,48,1152]{2,1,0:T(8,128)(2,1)S(1)}, bf16[2,48,1152]{2,1,0:T(8,128)(2,1)S(1)}, u32[]{:S(2)}, u32[]{:S(2)}) collective-permute-start(bf16[2,48,1152]{2,1,0:T(8,128)(2,1)S(1)} %shard_map.70.b_ref), channel_id=1, source_target_pairs={{0,1},{1,2},{2,3},{3,4},{4,5},{5,6},{6,7},{7,0},{8,9},{9,10},{10,1... | collective-permute-start | bytes 663560 | tf_op jit(solution)/shard_map/ppermute | solution.py:417
  20.5 9.7 %collective-permute-start.5 = (bf16[2,48,1152]{2,1,0:T(8,128)(2,1)S(1)}, bf16[2,48,1152]{2,1,0:T(8,128)(2,1)S(1)}, u32[]{:S(2)}, u32[]{:S(2)}) collective-permute-start(bf16[2,48,1152]{2,1,0:T(8,128)(2,1)S(1)} %get-tuple-element.32), channel_id=1, source_target_pairs={{0,0},{1,2},{2,1},{3,4},{4,3},{5,6},{6,5},{7,7},{8,8},{9,10},{10,9... | collective-permute-start | bytes 663560 | tf_op jit(solution)/shard_map/ppermute | solution.py:417
  21.2 9.7 %collective-permute-start.6 = (bf16[2,48,1152]{2,1,0:T(8,128)(2,1)S(1)}, bf16[2,48,1152]{2,1,0:T(8,128)(2,1)S(1)}, u32[]{:S(2)}, u32[]{:S(2)}) collective-permute-start(bf16[2,48,1152]{2,1,0:T(8,128)(2,1)S(1)} %get-tuple-element.33), channel_id=1, source_target_pairs={{0,1},{1,0},{2,3},{3,2},{4,5},{5,4},{6,7},{7,6},{8,9},{9,8},{10,11... | collective-permute-start | bytes 663560 | tf_op jit(solution)/shard_map/ppermute | solution.py:417
  26.4 11.6 %all-to-all-start = ((f32[32,8,128]{2,1,0:T(8,128)}), f32[32,8,128]{2,1,0:T(8,128)S(1)}, u32[]{:S(2)}, u32[]{:S(2)}) async-start(f32[32,8,128]{2,1,0:T(8,128)} %bitcast.2), calls=%async_computation | async-start | bytes 262144 | tf_op jit(solution)/shard_map/all_to_all | solution.py:486
  31.0 1.4 %collective-permute-start.7 = (bf16[48,1152]{1,0:T(8,128)(2,1)S(1)}, bf16[48,1152]{1,0:T(8,128)(2,1)S(1)}, u32[]{:S(2)}, u32[]{:S(2)}) collective-permute-start(bf16[48,1152]{1,0:T(8,128)(2,1)S(1)} %get-tuple-element.35), channel_id=1, source_target_pairs={{0,8},{1,9},{2,10},{3,11},{4,12},{5,13},{6,14},{7,15},{8,0},{9,1},... | collective-permute-start | bytes 331784 | tf_op jit(solution)/shard_map/ppermute | solution.py:417

commit v5 on v4

--- a/solution.py
+++ b/solution.py
@@ -60,7 +60,7 @@
     return jax.ShapeDtypeStruct(dims, dtype)
 
 
-def pack_kernel(g_hbm, b_hbm, g_own, g_send, g_far, b_own, b_far, g_ref, b_ref, halves, sems):
+def pack_kernel(g_hbm, b_hbm, g_own, g_far, b_own, b_far, both_far, g_ref, b_ref, halves, sems):
     core = my_core()
     copies = []
     for i, (src, dst) in enumerate(((g_hbm, g_ref), (b_hbm, b_ref))):
@@ -81,12 +81,8 @@
             halves[h] = jnp.concatenate(parts, axis=1)
         own[...] = halves[core].astype(BF)
         far[...] = halves[1 - core].astype(BF)
-    g_send[...] = g_own[...]
-
-
-def pair_kernel(first_ref, second_ref, out_ref):
-    out_ref[0] = first_ref[...]
-    out_ref[1] = second_ref[...]
+    both_far[0] = g_far[...]
+    both_far[1] = b_far[...]
 
 
 def table_kernel(
@@ -205,11 +201,11 @@
     core = my_core()
     blocks = refs[: 2 * chips]
     perm_ref, hi_ref, lo_ref, t_ref = refs[2 * chips : 2 * chips + 4]
-    high_ref, own_ref, pair_ref, next_ref, gathered, terms_ref, result = refs[2 * chips + 5 :]
+    high_ref, own_ref, low_ref, up_ref, gathered, terms_ref, result = refs[2 * chips + 4 :]
     for s in range(chips):
         n = 2 * ((s - 1) % chips)
         gathered[2 * s + core] = blocks[n][...]
-        gathered[2 * s + 1 - core] = blocks[n + 1][...]
+        gathered[2 * s + 1 - core] = blocks[n + 1][...] if s else blocks[n + 1][0]
     count, rows, width = gathered.shape
     depth = count * rows
     tiles = width // LANES
@@ -245,14 +241,11 @@
                 terms_ref[at : at + depth, i * LANES : (i + 1) * LANES] = part
     correlate(t_ref, terms_ref, result, entries)
     place = lax.axis_index("en")
-    odd = lax.rem(place, 2)
     below = jnp.where(place == 0, 0.0, 1.0)
     above = jnp.where(place == lax.axis_size("en") - 1, 0.0, 1.0)
-    keep_pair = jnp.where(odd == 1, below, above)
-    keep_next = jnp.where(odd == 1, above, below)
     for i, c in enumerate((core, 1 - core)):
-        pair_ref[i] = (result[2 - 2 * odd + c] * keep_pair).astype(BF)
-        next_ref[i] = (result[2 * odd + c] * keep_next).astype(BF)
+        low_ref[i] = (result[c] * below).astype(BF)
+        up_ref[i] = (result[2 + c] * above).astype(BF)
         own_ref[i] = result[4 + c]
 
 
@@ -277,12 +270,13 @@
                     result[r, :, i * LANES : (i + 1) * LANES] = tile[r * rows : (r + 1) * rows]
 
 
-def polar_kernel(b_ref, prev_ref, turn_ref, sort_ref, high_ref, out_ref, gathered, *, half, entries, momenta, local_k, local_e, scale):
+def polar_kernel(b_own, both_core, prev_own, prev_far, turn_ref, sort_ref, high_ref, out_ref, gathered, *, half, entries, momenta, local_k, local_e, scale):
     core = my_core()
     present = jnp.where(lax.axis_index("en") == 0, 0.0, 1.0)
-    for i, c in enumerate((core, 1 - core)):
-        gathered[c] = (prev_ref[i].astype(F32) * present).astype(BF)
-        gathered[2 + c] = b_ref[i]
+    gathered[core] = (prev_own[...].astype(F32) * present).astype(BF)
+    gathered[1 - core] = (prev_far[...].astype(F32) * present).astype(BF)
+    gathered[2 + core] = b_own[...]
+    gathered[3 - core] = both_core[1]
     count, rows, width = gathered.shape
     tiles = width // LANES
     b = dot(sort_ref[...], gathered[...].reshape(count * rows, width)).astype(BF)
@@ -358,9 +352,9 @@
             out_ref[i, m] = moved[:, :window]
 
 
-def sum_kernel(own, after, pair, mine, theirs):
+def sum_kernel(own, below, above, mine, theirs):
     for n, out in enumerate((mine, theirs)):
-        out[...] = (own[n] + pair[n].astype(F32) + after[n].astype(F32)).astype(BF)
+        out[...] = (own[n] + below[n].astype(F32) + above[n].astype(F32)).astype(BF)
 
 
 def join_kernel(mine, other, perm_ref, out_ref, mark_ref, halves):
@@ -393,9 +387,9 @@
 
     deriv = derivative.transpose(1, 0, 2)
     weights = phonon.transpose(0, 1, 3, 4, 2)
-    g_own, g_send, g_far, b_own, b_far = call(
+    g_own, g_far, b_own, b_far, both_far = call(
         pack_kernel,
-        [shape((rows, width), BF)] * 5,
+        [shape((rows, width), BF)] * 4 + [shape((2, rows, width), BF)],
         [green_less, green_greater],
         1.5,
         [
@@ -405,7 +399,7 @@
             pltpu.SemaphoreType.DMA((2,)),
         ],
         [HBM] * 2,
-        limit=53.2,
+        limit=53.12,
     )
 
     def move(value, dchip, dcore, to=lambda e: e):
@@ -419,19 +413,16 @@
     def onward(e):
         return (e + 1) % en
 
-    def to_pair(e):
-        return e ^ 1 if e ^ 1 < en else e
-
-    def to_next(e):
-        other = e + 1 if e % 2 else e - 1
-        return other if 0 <= other < en else e
+    def back(e):
+        return (e - 1) % en
 
     blocks = []
     for s in range(1, chips):
-        blocks += [move(g_far, -s, 1), move(g_send, -s, 0)][::-1]
-    blocks += [g_own, move(g_far, 0, 1)]
-    (b_both,) = call(pair_kernel, [shape((2, rows, width), BF)], [b_own, move(b_far, 0, 1)], 0.2)
-    prev_both = move(b_both, 0, 0, onward)
+        blocks += [move(g_far, -s, 1), move(g_own, -s, 0)][::-1]
+    both_core = move(both_far, 0, 1)
+    blocks += [g_own, both_core]
+    prev_far = move(b_far, 0, 1, onward)
+    prev_own = move(b_own, 0, 0, onward)
 
     near = neighbours.astype(jnp.int32)
     columns = -(-chip_k * 2 * local_e // LANES) * LANES
@@ -455,7 +446,7 @@
         [pl.BlockSpec(memory_space=pltpu.SMEM), VMEM, VMEM],
     )
 
-    high, own, to_pair_rows, to_next_rows = call(
+    high, own, low, up = call(
         functools.partial(product_kernel, half=half, entries=entries, chips=chips),
         [
             shape((3, momenta * local_e, width), BF),
@@ -463,7 +454,7 @@
             shape((2, rows, width), BF),
             shape((2, rows, width), BF),
         ],
-        blocks + [to_energy, k_hi, k_lo, toeplitz, prev_both],
+        blocks + [to_energy, k_hi, k_lo, toeplitz],
         4,
         [
             pltpu.VMEM((2 * chips, rows, width), BF),
@@ -471,15 +462,15 @@
             pltpu.VMEM((6, rows, width), F32),
         ],
     )
-    from_next = move(to_next_rows, 0, 0, to_next)
-    from_pair = move(to_pair_rows, 0, 0, to_pair)
+    from_below = move(up, 0, 0, onward)
+    from_above = move(low, 0, 0, back)
     (partial,) = call(
         functools.partial(
             polar_kernel, half=half, entries=entries, momenta=momenta, local_k=local_k, local_e=local_e,
             scale=1.0 / (NO * float(np.sqrt(momenta * total_e))),
         ),
         [shape((mom, en, local_k * half, LANES), F32)],
-        [b_both, prev_both, turn, sort_e, high],
+        [b_own, both_core, prev_own, prev_far, turn, sort_e, high],
         3,
         [pltpu.VMEM((4, rows, width), BF)],
     )
@@ -487,7 +478,7 @@
         partial.reshape(mom * en, local_k * half, LANES), ("mom", "en"), split_axis=0, concat_axis=0, tiled=True
     )
     mine, theirs = call(
-        sum_kernel, [shape((rows, width), BF)] * 2, [own, from_next, from_pair], 0.1
+        sum_kernel, [shape((rows, width), BF)] * 2, [own, from_below, from_above], 0.1
     )
     other = move(theirs, 0, 1)
     self_energy, mark = call(

time: 38.9 us -> 34.7 us (0.89)
  waiting for transfers between devices: 12.2 us -> 6.4 us
  starting transfers between devices: 12.4 us -> 13.9 us
    ppermute x8, waiting for transfers between devices: 7.85 us -> 4.72 us  [move(): return lax.ppermute(value, ('mom', 'en'), links)]
    all_to_all x1, waiting for transfers between devices: 4.37 us -> 1.68 us  [body(): lax.all_to_all(partial.reshape(mom * en, local_k * half, LANES), ('mom',...]
    ppermute x8, starting transfers between devices: 8.48 us -> 10.9 us  [move(): return lax.ppermute(value, ('mom', 'en'), links)]
    all_to_all x1, starting transfers between devices: 3.88 us -> 2.99 us  [body(): lax.all_to_all(partial.reshape(mom * en, local_k * half, LANES), ('mom',...]
    pallas_call x8 -> x7, Pallas kernels: 13.4 us -> 13.4 us  [call(): pl.pallas_call(kernel, out_shape=outs, in_specs=specs or [VMEM] * len(ins...]
  transfers between devices with their start and end apart: 9 -> 9, of which waited for: 5 -> 4; matrix products, arithmetic and copies ran while one was open for 0% -> 0% of each run, Pallas kernels for 18% -> 31%
where the time goes in v5:
time: 34.7 us; the launch traced here: 34.5 us
  starting transfers between devices  13.9 us (40%)
  Pallas kernels  13.4 us (39%)
  waiting for transfers between devices  6.4 us (18%)
  between operations  0.73 us (2%)
    pallas_call x7, Pallas kernels, call(): pl.pallas_call(kernel, out_shape=outs, in_specs=specs or [VMEM] * len(ins...  13.4 us
    ppermute x8, starting transfers between devices, move(): return lax.ppermute(value, ('mom', 'en'), links)  10.9 us
    ppermute x8, waiting for transfers between devices, move(): return lax.ppermute(value, ('mom', 'en'), links)  4.72 us
    all_to_all x1, starting transfers between devices, body(): lax.all_to_all(partial.reshape(mom * en, local_k * half, LANES), ('mom',...  2.99 us
    all_to_all x1, waiting for transfers between devices, body(): lax.all_to_all(partial.reshape(mom * en, local_k * half, LANES), ('mom',...  1.68 us
  transfers between devices with their start and end apart: 9, of which 4 were waited for; matrix products, arithmetic and copies ran while one was open for 0% of the time, Pallas kernels for 31%

profile of v5, /device:TPU:0, one launch (start us, length us, event | category | flops | bytes accessed | tf_op | source)
XLA Modules:
  0.0 34.5 jit_solution(12165166305459265777)
XLA Ops:
  0.6 0.0 copy-start.1
  0.6 0.0 copy-start
  0.7 0.0 copy-start.2
  0.7 2.1 %shard_map.68 = (bf16[48,1152]{1,0:T(8,128)(2,1)S(1)}, bf16[48,1152]{1,0:T(8,128)(2,1)S(1)}, bf16[48,1152]{1,0:T(8,128)(2,1)S(1)}, bf16[48,1152]{1,0:T(8,128)(2,1)S(1)}, bf16[2,48,1152]{2,1,0:T(8,128)(2,1)S(1)}) custom-call(bf16[2,24,8,288]{3,2,1,0:T(8,128)(2,1)} %g_hbm.1, bf16[2,24,8,288]{3,2,1,0:T(8,128)(2,1)} %b_hbm.1), custom_call_target="tpu_custom_call" | custom-call | flops 1500000000 | tf_op jit(solution)/shard_map/pallas_call | solution.py:31
  2.7 0.5 %collective-permute-start.2 = (bf16[2,48,1152]{2,1,0:T(8,128)(2,1)S(1)}, bf16[2,48,1152]{2,1,0:T(8,128)(2,1)S(1)}, u32[]{:S(2)}, u32[]{:S(2)}) collective-permute-start(bf16[2,48,1152]{2,1,0:T(8,128)(2,1)S(1)} %get-tuple-element.24), channel_id=1, source_target_pairs={{0,8},{1,9},{2,10},{3,11},{4,12},{5,13},{6,14},{7,15},{8,0},{9,1},... | collective-permute-start | bytes 663560 | tf_op jit(solution)/shard_map/ppermute | solution.py:411
  3.3 2.6 %collective-permute-start = (bf16[48,1152]{1,0:T(8,128)(2,1)S(1)}, bf16[48,1152]{1,0:T(8,128)(2,1)S(1)}, u32[]{:S(2)}, u32[]{:S(2)}) collective-permute-start(bf16[48,1152]{1,0:T(8,128)(2,1)S(1)} %get-tuple-element.22.refs_2_), channel_id=1, source_target_pairs={{0,16},{1,17},{2,18},{3,19},{4,20},{5,21},{6,22},{7,23},{8,24},{9,... | collective-permute-start | bytes 331784 | tf_op jit(solution)/shard_map/ppermute | solution.py:411
  5.8 0.1 collective-permute-start.1
  5.9 1.8 %collective-permute-start.6 = (bf16[48,1152]{1,0:T(8,128)(2,1)S(1)}, bf16[48,1152]{1,0:T(8,128)(2,1)S(1)}, u32[]{:S(2)}, u32[]{:S(2)}) collective-permute-start(bf16[48,1152]{1,0:T(8,128)(2,1)S(1)} %get-tuple-element.36.b_own), channel_id=1, source_target_pairs={{0,1},{1,2},{2,3},{3,4},{4,5},{5,6},{6,7},{7,0},{8,9},{9,10},{10,1... | collective-permute-start | bytes 331784 | tf_op jit(solution)/shard_map/ppermute | solution.py:411
  7.6 1.2 %collective-permute-start.7 = (bf16[48,1152]{1,0:T(8,128)(2,1)S(1)}, bf16[48,1152]{1,0:T(8,128)(2,1)S(1)}, u32[]{:S(2)}, u32[]{:S(2)}) collective-permute-start(bf16[48,1152]{1,0:T(8,128)(2,1)S(1)} %get-tuple-element.37), channel_id=1, source_target_pairs={{0,9},{1,10},{2,11},{3,12},{4,13},{5,14},{6,15},{7,8},{8,1},{9,2},... | collective-permute-start | bytes 331784 | tf_op jit(solution)/shard_map/ppermute | solution.py:411
  8.8 0.0 copy-done.1
  8.8 0.0 copy-done
  8.8 0.0 copy-done.2
  8.8 2.9 %shard_map.69 = (bf16[24,144,256]{2,1,0:T(8,128)(2,1)S(1)}, bf16[24,144,256]{2,1,0:T(8,128)(2,1)S(1)}, bf16[4,288,768]{2,1,0:T(8,128)(2,1)S(1)}, bf16[192,192]{1...) custom-call(s32[2,4]{1,0:T(2,128)S(1)} %copy-done.2, ...), custom_call_target="tpu_custom_call" | custom-call | flops 3000000000 | tf_op jit(solution)/shard_map/pallas_call | solution.py:31
  11.8 0.0 collective-permute-done.refs_0_
  11.8 0.0 collective-permute-done.1.refs_1_
  11.8 0.0 collective-permute-done.2.refs_3_.both_core
  11.8 3.7 %shard_map.70 = (bf16[3,192,1152]{2,1,0:T(8,128)(2,1)S(1)}, f32[2,48,1152]{2,1,0:T(8,128)S(1)}, bf16[2,48,1152]{2,1,0:T(8,128)(2,1)S(1)}, bf16[2,48,1152]{2,1,0:T(8,128)(2,1)S(1)}) custom-call(bf16[48,1152]{1,0:T(8,128)(2,1)S(1)} %collective-permute-done.refs_0_, bf16[48,1152]{1,0:T(8,128)(2,1)S(1)} %collective-permute-done.1.refs_1_, ...), custom_call_target="tpu_custom_call" | custom-call | flops 4000000000 | tf_op jit(solution)/shard_map/pallas_call | solution.py:31
  15.5 1.6 %collective-permute-start.3 = (bf16[2,48,1152]{2,1,0:T(8,128)(2,1)S(1)}, bf16[2,48,1152]{2,1,0:T(8,128)(2,1)S(1)}, u32[]{:S(2)}, u32[]{:S(2)}) collective-permute-start(bf16[2,48,1152]{2,1,0:T(8,128)(2,1)S(1)} %get-tuple-element.30), channel_id=1, source_target_pairs={{0,1},{1,2},{2,3},{3,4},{4,5},{5,6},{6,7},{7,0},{8,9},{9,10},{10,1... | collective-permute-start | bytes 663560 | tf_op jit(solution)/shard_map/ppermute | solution.py:411
  17.1 3.2 %collective-permute-start.4 = (bf16[2,48,1152]{2,1,0:T(8,128)(2,1)S(1)}, bf16[2,48,1152]{2,1,0:T(8,128)(2,1)S(1)}, u32[]{:S(2)}, u32[]{:S(2)}) collective-permute-start(bf16[2,48,1152]{2,1,0:T(8,128)(2,1)S(1)} %get-tuple-element.31), channel_id=1, source_target_pairs={{0,7},{1,0},{2,1},{3,2},{4,3},{5,4},{6,5},{7,6},{8,15},{9,8},{10,9... | collective-permute-start | bytes 663560 | tf_op jit(solution)/shard_map/ppermute | solution.py:411
  20.3 0.0 collective-permute-done.6.prev_own
  20.3 0.0 collective-permute-done.7.prev_far
  20.3 2.7 %shard_map.73 = f32[4,8,8,128]{3,2,1,0:T(8,128)} custom-call(bf16[48,1152]{1,0:T(8,128)(2,1)S(1)} %get-tuple-element.36.b_own, bf16[2,48,1152]{2,1,0:T(8,128)(2,1)S(1)} %collective-permute-done.2.refs_3_.both_core, bf16[48,1152]{1,0:T(8,128)(2,1)S(1)} %collective-permute-done.6.prev_own, bf16[48,1152]{1,0:T(8,128)(2,1)S(1)} %collective-permute-done.7.prev_far, ...), custom_call_target="tpu_custom_call" | custom-call | flops 3000000000 | tf_op jit(solution)/shard_map/pallas_call | solution.py:31
  23.0 3.0 %all-to-all-start = ((f32[32,8,128]{2,1,0:T(8,128)}), f32[32,8,128]{2,1,0:T(8,128)S(1)}, u32[]{:S(2)}, u32[]{:S(2)}) async-start(f32[32,8,128]{2,1,0:T(8,128)} %bitcast.2), calls=%async_computation | async-start | bytes 262144 | tf_op jit(solution)/shard_map/all_to_all | solution.py:477
  26.0 1.2 %collective-permute-done.3.below = bf16[2,48,1152]{2,1,0:T(8,128)(2,1)S(1)} collective-permute-done((bf16[2,48,1152]{2,1,0:T(8,128)(2,1)S(1)}, bf16[2,48,1152]{2,1,0:T(8,128)(2,1)S(1)}, u32[]{:S(2)}, u32[]{:S(2)}) %collective-permute-start.3) | collective-permute-done | bytes 221216 | tf_op jit(solution)/shard_map/ppermute | solution.py:411
  27.2 2.2 %collective-permute-done.4.above = bf16[2,48,1152]{2,1,0:T(8,128)(2,1)S(1)} collective-permute-done((bf16[2,48,1152]{2,1,0:T(8,128)(2,1)S(1)}, bf16[2,48,1152]{2,1,0:T(8,128)(2,1)S(1)}, u32[]{:S(2)}, u32[]{:S(2)}) %collective-permute-start.4) | collective-permute-done | bytes 221216 | tf_op jit(solution)/shard_map/ppermute | solution.py:411
  29.4 0.1 shard_map.71
  29.5 0.1 collective-permute-start.5
  29.6 1.3 %collective-permute-done.5.other = bf16[48,1152]{1,0:T(8,128)(2,1)S(1)} collective-permute-done((bf16[48,1152]{1,0:T(8,128)(2,1)S(1)}, bf16[48,1152]{1,0:T(8,128)(2,1)S(1)}, u32[]{:S(2)}, u32[]{:S(2)}) %collective-permute-start.5) | collective-permute-done | bytes 110624 | tf_op jit(solution)/shard_map/ppermute | solution.py:411
  30.9 1.2 %shard_map.72 = (bf16[2,24,8,288]{3,2,1,0:T(8,128)(2,1)}, f32[8,128]{1,0:T(8,128)S(1)}) custom-call(bf16[48,1152]{1,0:T(8,128)(2,1)S(1)} %get-tuple-element.32.mine, bf16[48,1152]{1,0:T(8,128)(2,1)S(1)} %collective-permute-done.5.other, bf16[384,384]{1,0:T(8,128)(2,1)S(1)} %get-tuple-element.34.perm_ref), custom_call_target="tpu_custom_call" | custom-call | flops 1000000000 | tf_op jit(solution)/shard_map/pallas_call | solution.py:31
  32.1 1.7 %all-to-all-done = f32[32,8,128]{2,1,0:T(8,128)S(1)} async-done(((f32[32,8,128]{2,1,0:T(8,128)}), f32[32,8,128]{2,1,0:T(8,128)S(1)}, u32[]{:S(2)}, u32[]{:S(2)}) %all-to-all-start) | async-done | bytes 131104 | tf_op jit(solution)/shard_map/all_to_all | solution.py:477
  33.8 0.7 %shard_map.74 = f32[2,3,8,24]{3,2,1,0:T(8,128)} custom-call(f32[4,8,8,128]{3,2,1,0:T(8,128)S(1)} %bitcast.5, f32[8,128]{1,0:T(8,128)S(1)} %get-tuple-element.41.after_ref), custom_call_target="tpu_custom_call" | custom-call | flops 500000000 | tf_op jit(solution)/shard_map/pallas_call | solution.py:31
Async XLA Ops:
  0.6 8.2 %copy-start.1 = (f32[2,3,144]{2,0,1:T(2,128)S(1)}, f32[2,3,144]{2,0,1:T(2,128)}, u32[]{:S(2)}) copy-start(f32[2,3,144]{2,0,1:T(2,128)} %param.7) | copy-start | bytes 10372
  0.6 8.2 %copy-start = (bf16[2,8,24,3,8]{2,4,3,1,0:T(8,128)(2,1)S(1)}, bf16[2,8,24,3,8]{2,4,3,1,0:T(8,128)(2,1)}, u32[]{:S(2)}) copy-start(bf16[2,8,24,3,8]{2,4,3,1,0:T(8,128)(2,1)} %param.9) | copy-start | bytes 55300
  0.7 8.2 %copy-start.2 = (s32[2,4]{1,0:T(2,128)S(1)}, s32[2,4]{1,0:T(2,128)}, u32[]{:S(2)}) copy-start(s32[2,4]{1,0:T(2,128)} %near_ref.1) | copy-start | bytes 100
  2.7 9.1 %collective-permute-start.2 = (bf16[2,48,1152]{2,1,0:T(8,128)(2,1)S(1)}, bf16[2,48,1152]{2,1,0:T(8,128)(2,1)S(1)}, u32[]{:S(2)}, u32[]{:S(2)}) collective-permute-start(bf16[2,48,1152]{2,1,0:T(8,128)(2,1)S(1)} %get-tuple-element.24), channel_id=1, source_target_pairs={{0,8},{1,9},{2,10},{3,11},{4,12},{5,13},{6,14},{7,15},{8,0},{9,1},... | collective-permute-start | bytes 663560 | tf_op jit(solution)/shard_map/ppermute | solution.py:411
  3.3 8.5 %collective-permute-start = (bf16[48,1152]{1,0:T(8,128)(2,1)S(1)}, bf16[48,1152]{1,0:T(8,128)(2,1)S(1)}, u32[]{:S(2)}, u32[]{:S(2)}) collective-permute-start(bf16[48,1152]{1,0:T(8,128)(2,1)S(1)} %get-tuple-element.22.refs_2_), channel_id=1, source_target_pairs={{0,16},{1,17},{2,18},{3,19},{4,20},{5,21},{6,22},{7,23},{8,24},{9,... | collective-permute-start | bytes 331784 | tf_op jit(solution)/shard_map/ppermute | solution.py:411
  5.8 6.0 %collective-permute-start.1 = (bf16[48,1152]{1,0:T(8,128)(2,1)S(1)}, bf16[48,1152]{1,0:T(8,128)(2,1)S(1)}, u32[]{:S(2)}, u32[]{:S(2)}) collective-permute-start(bf16[48,1152]{1,0:T(8,128)(2,1)S(1)} %get-tuple-element.23), channel_id=1, source_target_pairs={{0,24},{1,25},{2,26},{3,27},{4,28},{5,29},{6,30},{7,31},{8,16},{9,... | collective-permute-start | bytes 331784 | tf_op jit(solution)/shard_map/ppermute | solution.py:411
  5.9 14.4 %collective-permute-start.6 = (bf16[48,1152]{1,0:T(8,128)(2,1)S(1)}, bf16[48,1152]{1,0:T(8,128)(2,1)S(1)}, u32[]{:S(2)}, u32[]{:S(2)}) collective-permute-start(bf16[48,1152]{1,0:T(8,128)(2,1)S(1)} %get-tuple-element.36.b_own), channel_id=1, source_target_pairs={{0,1},{1,2},{2,3},{3,4},{4,5},{5,6},{6,7},{7,0},{8,9},{9,10},{10,1... | collective-permute-start | bytes 331784 | tf_op jit(solution)/shard_map/ppermute | solution.py:411
  7.6 12.7 %collective-permute-start.7 = (bf16[48,1152]{1,0:T(8,128)(2,1)S(1)}, bf16[48,1152]{1,0:T(8,128)(2,1)S(1)}, u32[]{:S(2)}, u32[]{:S(2)}) collective-permute-start(bf16[48,1152]{1,0:T(8,128)(2,1)S(1)} %get-tuple-element.37), channel_id=1, source_target_pairs={{0,9},{1,10},{2,11},{3,12},{4,13},{5,14},{6,15},{7,8},{8,1},{9,2},... | collective-permute-start | bytes 331784 | tf_op jit(solution)/shard_map/ppermute | solution.py:411
  15.5 11.7 %collective-permute-start.3 = (bf16[2,48,1152]{2,1,0:T(8,128)(2,1)S(1)}, bf16[2,48,1152]{2,1,0:T(8,128)(2,1)S(1)}, u32[]{:S(2)}, u32[]{:S(2)}) collective-permute-start(bf16[2,48,1152]{2,1,0:T(8,128)(2,1)S(1)} %get-tuple-element.30), channel_id=1, source_target_pairs={{0,1},{1,2},{2,3},{3,4},{4,5},{5,6},{6,7},{7,0},{8,9},{9,10},{10,1... | collective-permute-start | bytes 663560 | tf_op jit(solution)/shard_map/ppermute | solution.py:411
  17.1 12.3 %collective-permute-start.4 = (bf16[2,48,1152]{2,1,0:T(8,128)(2,1)S(1)}, bf16[2,48,1152]{2,1,0:T(8,128)(2,1)S(1)}, u32[]{:S(2)}, u32[]{:S(2)}) collective-permute-start(bf16[2,48,1152]{2,1,0:T(8,128)(2,1)S(1)} %get-tuple-element.31), channel_id=1, source_target_pairs={{0,7},{1,0},{2,1},{3,2},{4,3},{5,4},{6,5},{7,6},{8,15},{9,8},{10,9... | collective-permute-start | bytes 663560 | tf_op jit(solution)/shard_map/ppermute | solution.py:411
  23.0 10.7 %all-to-all-start = ((f32[32,8,128]{2,1,0:T(8,128)}), f32[32,8,128]{2,1,0:T(8,128)S(1)}, u32[]{:S(2)}, u32[]{:S(2)}) async-start(f32[32,8,128]{2,1,0:T(8,128)} %bitcast.2), calls=%async_computation | async-start | bytes 262144 | tf_op jit(solution)/shard_map/all_to_all | solution.py:477
  29.5 1.4 %collective-permute-start.5 = (bf16[48,1152]{1,0:T(8,128)(2,1)S(1)}, bf16[48,1152]{1,0:T(8,128)(2,1)S(1)}, u32[]{:S(2)}, u32[]{:S(2)}) collective-permute-start(bf16[48,1152]{1,0:T(8,128)(2,1)S(1)} %get-tuple-element.33), channel_id=1, source_target_pairs={{0,8},{1,9},{2,10},{3,11},{4,12},{5,13},{6,14},{7,15},{8,0},{9,1},... | collective-permute-start | bytes 331784 | tf_op jit(solution)/shard_map/ppermute | solution.py:411

commit v6 on v5

--- a/solution.py
+++ b/solution.py
@@ -270,7 +270,8 @@
                     result[r, :, i * LANES : (i + 1) * LANES] = tile[r * rows : (r + 1) * rows]
 
 
-def polar_kernel(b_own, both_core, prev_own, prev_far, turn_ref, sort_ref, high_ref, out_ref, gathered, *, half, entries, momenta, local_k, local_e, scale):
+def polar_kernel(b_own, both_core, prev_own, prev_far, turn_ref, sort_ref, high_ref, out_ref, mark_ref, gathered, *, half, entries, momenta, local_k, local_e, scale):
+    mark_ref[...] = jnp.zeros(mark_ref.shape, F32)
     core = my_core()
     present = jnp.where(lax.axis_index("en") == 0, 0.0, 1.0)
     gathered[core] = (prev_own[...].astype(F32) * present).astype(BF)
@@ -335,7 +336,7 @@
             out_ref[t, e] = tile
 
 
-def total_kernel(in_ref, after_ref, out_ref, *, half):
+def total_kernel(in_ref, out_ref, *, half):
     targets, en = in_ref.shape[:2]
     local_k, _, _, window = out_ref.shape
     sums = []
@@ -352,12 +353,17 @@
             out_ref[i, m] = moved[:, :window]
 
 
-def sum_kernel(own, below, above, mine, theirs):
+def first_kernel(own, below, low, mark_ref, sum_ref, low_ref):
+    sum_ref[...] = own[...] + below[...].astype(F32)
+    low_ref[...] = low[...]
+
+
+def sum_kernel(own, above, mine, theirs):
     for n, out in enumerate((mine, theirs)):
-        out[...] = (own[n] + below[n].astype(F32) + above[n].astype(F32)).astype(BF)
-
-
-def join_kernel(mine, other, perm_ref, out_ref, mark_ref, halves):
+        out[...] = (own[n] + above[n].astype(F32)).astype(BF)
+
+
+def join_kernel(mine, other, perm_ref, out_ref, halves):
     core = my_core()
     pairs = out_ref.shape[2]
     entries = out_ref.shape[3]
@@ -369,7 +375,6 @@
         begin = entries * (p % half)
         parts.append(halves[p // half][:, begin : begin + entries])
     stacked = jnp.concatenate(parts, axis=0).astype(BF)
-    mark_ref[...] = jnp.zeros(mark_ref.shape, F32)
     out_ref[...] = dot(perm_ref[...], stacked).astype(BF).reshape(out_ref.shape)
 
 
@@ -463,13 +468,12 @@
         ],
     )
     from_below = move(up, 0, 0, onward)
-    from_above = move(low, 0, 0, back)
-    (partial,) = call(
+    partial, done = call(
         functools.partial(
             polar_kernel, half=half, entries=entries, momenta=momenta, local_k=local_k, local_e=local_e,
             scale=1.0 / (NO * float(np.sqrt(momenta * total_e))),
         ),
-        [shape((mom, en, local_k * half, LANES), F32)],
+        [shape((mom, en, local_k * half, LANES), F32), shape((8, LANES), F32)],
         [b_own, both_core, prev_own, prev_far, turn, sort_e, high],
         3,
         [pltpu.VMEM((4, rows, width), BF)],
@@ -477,13 +481,17 @@
     terms = lax.all_to_all(
         partial.reshape(mom * en, local_k * half, LANES), ("mom", "en"), split_axis=0, concat_axis=0, tiled=True
     )
+    own, low = call(
+        first_kernel, [shape((2, rows, width), F32), shape(low.shape, BF)], [own, from_below, low, done], 0.2
+    )
+    from_above = move(low, 0, 0, back)
     mine, theirs = call(
-        sum_kernel, [shape((rows, width), BF)] * 2, [own, from_below, from_above], 0.1
+        sum_kernel, [shape((rows, width), BF)] * 2, [own, from_above], 0.1
     )
     other = move(theirs, 0, 1)
-    self_energy, mark = call(
+    (self_energy,) = call(
         join_kernel,
-        [shape(green_less.shape, BF), shape((8, LANES), F32)],
+        [shape(green_less.shape, BF)],
         [mine, other, to_rows],
         1,
         [pltpu.VMEM((2, rows, width), F32)],
@@ -491,7 +499,7 @@
     (polar,) = call(
         functools.partial(total_kernel, half=half),
         [shape((local_k, 3, pairs, window), F32)],
-        [terms.reshape(mom, en, local_k * half, LANES), mark],
+        [terms.reshape(mom, en, local_k * half, LANES)],
         0.5,
     )
     polar = polar.transpose(0, 3, 1, 2)

time: 34.7 us -> 40.5 us (1.17)
  waiting for transfers between devices: 6.4 us -> 13.9 us
  starting transfers between devices: 13.9 us -> 12.2 us
    ppermute x8, waiting for transfers between devices: 4.72 us -> 9.34 us  [move(): return lax.ppermute(value, ('mom', 'en'), links)]
    all_to_all x1, waiting for transfers between devices: 1.68 us -> 4.6 us  [body(): lax.all_to_all(partial.reshape(mom * en, local_k * half, LANES), ('mom',...]
    ppermute x8, starting transfers between devices: 10.9 us -> 9.54 us  [move(): return lax.ppermute(value, ('mom', 'en'), links)]
    pallas_call x7 -> x8, Pallas kernels: 13.4 us -> 13.4 us  [call(): pl.pallas_call(kernel, out_shape=outs, in_specs=specs or [VMEM] * len(ins...]
  transfers between devices with their start and end apart: 9 -> 9, of which waited for: 4 -> 3; matrix products, arithmetic and copies ran while one was open for 0% -> 0% of each run, Pallas kernels for 31% -> 25%
where the time goes in v6:
time: 40.5 us; the launch traced here: 40.3 us
  waiting for transfers between devices  13.9 us (34%)
  Pallas kernels  13.4 us (33%)
  starting transfers between devices  12.2 us (30%)
  between operations  0.73 us (2%)
    pallas_call x8, Pallas kernels, call(): pl.pallas_call(kernel, out_shape=outs, in_specs=specs or [VMEM] * len(ins...  13.4 us
    ppermute x8, starting transfers between devices, move(): return lax.ppermute(value, ('mom', 'en'), links)  9.54 us
    ppermute x8, waiting for transfers between devices, move(): return lax.ppermute(value, ('mom', 'en'), links)  9.34 us
    all_to_all x1, waiting for transfers between devices, body(): lax.all_to_all(partial.reshape(mom * en, local_k * half, LANES), ('mom',...  4.6 us
    all_to_all x1, starting transfers between devices, body(): lax.all_to_all(partial.reshape(mom * en, local_k * half, LANES), ('mom',...  2.69 us
  transfers between devices with their start and end apart: 9, of which 3 were waited for; matrix products, arithmetic and copies ran while one was open for 0% of the time, Pallas kernels for 25%

profile of v6, /device:TPU:0, one launch (start us, length us, event | category | flops | bytes accessed | tf_op | source)
XLA Modules:
  0.0 40.3 jit_solution(1055064055920185692)
XLA Ops:
  0.6 0.0 copy-start.1
  0.6 0.0 copy-start
  0.7 0.0 copy-start.2
  0.7 2.1 %shard_map.68 = (bf16[48,1152]{1,0:T(8,128)(2,1)S(1)}, bf16[48,1152]{1,0:T(8,128)(2,1)S(1)}, bf16[48,1152]{1,0:T(8,128)(2,1)S(1)}, bf16[48,1152]{1,0:T(8,128)(2,1)S(1)}, bf16[2,48,1152]{2,1,0:T(8,128)(2,1)S(1)}) custom-call(bf16[2,24,8,288]{3,2,1,0:T(8,128)(2,1)} %g_hbm.1, bf16[2,24,8,288]{3,2,1,0:T(8,128)(2,1)} %b_hbm.1), custom_call_target="tpu_custom_call" | custom-call | flops 1500000000 | tf_op jit(solution)/shard_map/pallas_call | solution.py:31
  2.7 0.5 %collective-permute-start.2 = (bf16[2,48,1152]{2,1,0:T(8,128)(2,1)S(1)}, bf16[2,48,1152]{2,1,0:T(8,128)(2,1)S(1)}, u32[]{:S(2)}, u32[]{:S(2)}) collective-permute-start(bf16[2,48,1152]{2,1,0:T(8,128)(2,1)S(1)} %get-tuple-element.26), channel_id=1, source_target_pairs={{0,8},{1,9},{2,10},{3,11},{4,12},{5,13},{6,14},{7,15},{8,0},{9,1},... | collective-permute-start | bytes 663560 | tf_op jit(solution)/shard_map/ppermute | solution.py:416
  3.3 2.6 %collective-permute-start = (bf16[48,1152]{1,0:T(8,128)(2,1)S(1)}, bf16[48,1152]{1,0:T(8,128)(2,1)S(1)}, u32[]{:S(2)}, u32[]{:S(2)}) collective-permute-start(bf16[48,1152]{1,0:T(8,128)(2,1)S(1)} %get-tuple-element.24.refs_2_), channel_id=1, source_target_pairs={{0,16},{1,17},{2,18},{3,19},{4,20},{5,21},{6,22},{7,23},{8,24},{9,... | collective-permute-start | bytes 331784 | tf_op jit(solution)/shard_map/ppermute | solution.py:416
  5.8 0.1 collective-permute-start.1
  5.9 1.8 %collective-permute-start.4 = (bf16[48,1152]{1,0:T(8,128)(2,1)S(1)}, bf16[48,1152]{1,0:T(8,128)(2,1)S(1)}, u32[]{:S(2)}, u32[]{:S(2)}) collective-permute-start(bf16[48,1152]{1,0:T(8,128)(2,1)S(1)} %get-tuple-element.34.b_own), channel_id=1, source_target_pairs={{0,1},{1,2},{2,3},{3,4},{4,5},{5,6},{6,7},{7,0},{8,9},{9,10},{10,1... | collective-permute-start | bytes 331784 | tf_op jit(solution)/shard_map/ppermute | solution.py:416
  7.6 1.2 %collective-permute-start.5 = (bf16[48,1152]{1,0:T(8,128)(2,1)S(1)}, bf16[48,1152]{1,0:T(8,128)(2,1)S(1)}, u32[]{:S(2)}, u32[]{:S(2)}) collective-permute-start(bf16[48,1152]{1,0:T(8,128)(2,1)S(1)} %get-tuple-element.35), channel_id=1, source_target_pairs={{0,9},{1,10},{2,11},{3,12},{4,13},{5,14},{6,15},{7,8},{8,1},{9,2},... | collective-permute-start | bytes 331784 | tf_op jit(solution)/shard_map/ppermute | solution.py:416
  8.8 0.0 copy-done.1
  8.8 0.0 copy-done
  8.8 0.0 copy-done.2
  8.8 2.9 %shard_map.69 = (bf16[24,144,256]{2,1,0:T(8,128)(2,1)S(1)}, bf16[24,144,256]{2,1,0:T(8,128)(2,1)S(1)}, bf16[4,288,768]{2,1,0:T(8,128)(2,1)S(1)}, bf16[192,192]{1...) custom-call(s32[2,4]{1,0:T(2,128)S(1)} %copy-done.2, ...), custom_call_target="tpu_custom_call" | custom-call | flops 3000000000 | tf_op jit(solution)/shard_map/pallas_call | solution.py:31
  11.8 0.0 collective-permute-done.refs_0_
  11.8 0.0 collective-permute-done.1.refs_1_
  11.8 0.0 collective-permute-done.2.refs_3_.both_core
  11.8 3.7 %shard_map.70 = (bf16[3,192,1152]{2,1,0:T(8,128)(2,1)S(1)}, f32[2,48,1152]{2,1,0:T(8,128)S(1)}, bf16[2,48,1152]{2,1,0:T(8,128)(2,1)S(1)}, bf16[2,48,1152]{2,1,0:T(8,128)(2,1)S(1)}) custom-call(bf16[48,1152]{1,0:T(8,128)(2,1)S(1)} %collective-permute-done.refs_0_, bf16[48,1152]{1,0:T(8,128)(2,1)S(1)} %collective-permute-done.1.refs_1_, ...), custom_call_target="tpu_custom_call" | custom-call | flops 4000000000 | tf_op jit(solution)/shard_map/pallas_call | solution.py:31
  15.5 1.6 %collective-permute-start.3 = (bf16[2,48,1152]{2,1,0:T(8,128)(2,1)S(1)}, bf16[2,48,1152]{2,1,0:T(8,128)(2,1)S(1)}, u32[]{:S(2)}, u32[]{:S(2)}) collective-permute-start(bf16[2,48,1152]{2,1,0:T(8,128)(2,1)S(1)} %get-tuple-element.32), channel_id=1, source_target_pairs={{0,1},{1,2},{2,3},{3,4},{4,5},{5,6},{6,7},{7,0},{8,9},{9,10},{10,1... | collective-permute-start | bytes 663560 | tf_op jit(solution)/shard_map/ppermute | solution.py:416
  17.1 0.0 collective-permute-done.4.prev_own
  17.1 0.0 collective-permute-done.5.prev_far
  17.1 2.7 %shard_map.71 = (f32[4,8,8,128]{3,2,1,0:T(8,128)}, f32[8,128]{1,0:T(8,128)S(1)}) custom-call(bf16[48,1152]{1,0:T(8,128)(2,1)S(1)} %get-tuple-element.34.b_own, bf16[2,48,1152]{2,1,0:T(8,128)(2,1)S(1)} %collective-permute-done.2.refs_3_.both_core, bf16[48,1152]{1,0:T(8,128)(2,1)S(1)} %collective-permute-done.4.prev_own, ...), custom_call_target="tpu_custom_call" | custom-call | flops 3000000000 | tf_op jit(solution)/shard_map/pallas_call | solution.py:31
  19.8 6.3 %collective-permute-done.3.below = bf16[2,48,1152]{2,1,0:T(8,128)(2,1)S(1)} collective-permute-done((bf16[2,48,1152]{2,1,0:T(8,128)(2,1)S(1)}, bf16[2,48,1152]{2,1,0:T(8,128)(2,1)S(1)}, u32[]{:S(2)}, u32[]{:S(2)}) %collective-permute-start.3) | collective-permute-done | bytes 221216 | tf_op jit(solution)/shard_map/ppermute | solution.py:416
  26.1 0.1 shard_map.72
  26.2 1.8 %collective-permute-start.6 = (bf16[2,48,1152]{2,1,0:T(8,128)(2,1)S(1)}, bf16[2,48,1152]{2,1,0:T(8,128)(2,1)S(1)}, u32[]{:S(2)}, u32[]{:S(2)}) collective-permute-start(bf16[2,48,1152]{2,1,0:T(8,128)(2,1)S(1)} %get-tuple-element.41), channel_id=1, source_target_pairs={{0,7},{1,0},{2,1},{3,2},{4,3},{5,4},{6,5},{7,6},{8,15},{9,8},{10,9... | collective-permute-start | bytes 663560 | tf_op jit(solution)/shard_map/ppermute | solution.py:416
  28.0 2.7 %all-to-all-start = ((f32[32,8,128]{2,1,0:T(8,128)}), f32[32,8,128]{2,1,0:T(8,128)S(1)}, u32[]{:S(2)}, u32[]{:S(2)}) async-start(f32[32,8,128]{2,1,0:T(8,128)} %bitcast.2), calls=%async_computation | async-start | bytes 262144 | tf_op jit(solution)/shard_map/all_to_all | solution.py:481
  30.7 3.0 %collective-permute-done.6.above = bf16[2,48,1152]{2,1,0:T(8,128)(2,1)S(1)} collective-permute-done((bf16[2,48,1152]{2,1,0:T(8,128)(2,1)S(1)}, bf16[2,48,1152]{2,1,0:T(8,128)(2,1)S(1)}, u32[]{:S(2)}, u32[]{:S(2)}) %collective-permute-start.6) | collective-permute-done | bytes 221216 | tf_op jit(solution)/shard_map/ppermute | solution.py:416
  33.8 0.1 collective-permute-start.7
  33.8 4.6 %all-to-all-done = f32[32,8,128]{2,1,0:T(8,128)S(1)} async-done(((f32[32,8,128]{2,1,0:T(8,128)}), f32[32,8,128]{2,1,0:T(8,128)S(1)}, u32[]{:S(2)}, u32[]{:S(2)}) %all-to-all-start) | async-done | bytes 131104 | tf_op jit(solution)/shard_map/all_to_all | solution.py:481
  38.4 0.7 %shard_map.75 = f32[2,3,8,24]{3,2,1,0:T(8,128)} custom-call(f32[4,8,8,128]{3,2,1,0:T(8,128)S(1)} %bitcast.5), custom_call_target="tpu_custom_call" | custom-call | flops 500000000 | tf_op jit(solution)/shard_map/pallas_call | solution.py:31
  39.1 0.0 collective-permute-done.7.other
  39.1 1.2 %shard_map.74 = bf16[2,24,8,288]{3,2,1,0:T(8,128)(2,1)} custom-call(bf16[48,1152]{1,0:T(8,128)(2,1)S(1)} %get-tuple-element.42.mine, bf16[48,1152]{1,0:T(8,128)(2,1)S(1)} %collective-permute-done.7.other, bf16[384,384]{1,0:T(8,128)(2,1)S(1)} %get-tuple-element.44.perm_ref), custom_call_target="tpu_custom_call" | custom-call | flops 1000000000 | tf_op jit(solution)/shard_map/pallas_call | solution.py:31
  (1 shorter events, 0.0 us)
Async XLA Ops:
  0.6 8.2 %copy-start.1 = (f32[2,3,144]{2,0,1:T(2,128)S(1)}, f32[2,3,144]{2,0,1:T(2,128)}, u32[]{:S(2)}) copy-start(f32[2,3,144]{2,0,1:T(2,128)} %param.7) | copy-start | bytes 10372
  0.6 8.2 %copy-start = (bf16[2,8,24,3,8]{2,4,3,1,0:T(8,128)(2,1)S(1)}, bf16[2,8,24,3,8]{2,4,3,1,0:T(8,128)(2,1)}, u32[]{:S(2)}) copy-start(bf16[2,8,24,3,8]{2,4,3,1,0:T(8,128)(2,1)} %param.9) | copy-start | bytes 55300
  0.7 8.2 %copy-start.2 = (s32[2,4]{1,0:T(2,128)S(1)}, s32[2,4]{1,0:T(2,128)}, u32[]{:S(2)}) copy-start(s32[2,4]{1,0:T(2,128)} %near_ref.1) | copy-start | bytes 100
  2.7 9.1 %collective-permute-start.2 = (bf16[2,48,1152]{2,1,0:T(8,128)(2,1)S(1)}, bf16[2,48,1152]{2,1,0:T(8,128)(2,1)S(1)}, u32[]{:S(2)}, u32[]{:S(2)}) collective-permute-start(bf16[2,48,1152]{2,1,0:T(8,128)(2,1)S(1)} %get-tuple-element.26), channel_id=1, source_target_pairs={{0,8},{1,9},{2,10},{3,11},{4,12},{5,13},{6,14},{7,15},{8,0},{9,1},... | collective-permute-start | bytes 663560 | tf_op jit(solution)/shard_map/ppermute | solution.py:416
  3.3 8.5 %collective-permute-start = (bf16[48,1152]{1,0:T(8,128)(2,1)S(1)}, bf16[48,1152]{1,0:T(8,128)(2,1)S(1)}, u32[]{:S(2)}, u32[]{:S(2)}) collective-permute-start(bf16[48,1152]{1,0:T(8,128)(2,1)S(1)} %get-tuple-element.24.refs_2_), channel_id=1, source_target_pairs={{0,16},{1,17},{2,18},{3,19},{4,20},{5,21},{6,22},{7,23},{8,24},{9,... | collective-permute-start | bytes 331784 | tf_op jit(solution)/shard_map/ppermute | solution.py:416
  5.8 6.0 %collective-permute-start.1 = (bf16[48,1152]{1,0:T(8,128)(2,1)S(1)}, bf16[48,1152]{1,0:T(8,128)(2,1)S(1)}, u32[]{:S(2)}, u32[]{:S(2)}) collective-permute-start(bf16[48,1152]{1,0:T(8,128)(2,1)S(1)} %get-tuple-element.25), channel_id=1, source_target_pairs={{0,24},{1,25},{2,26},{3,27},{4,28},{5,29},{6,30},{7,31},{8,16},{9,... | collective-permute-start | bytes 331784 | tf_op jit(solution)/shard_map/ppermute | solution.py:416
  5.9 11.2 %collective-permute-start.4 = (bf16[48,1152]{1,0:T(8,128)(2,1)S(1)}, bf16[48,1152]{1,0:T(8,128)(2,1)S(1)}, u32[]{:S(2)}, u32[]{:S(2)}) collective-permute-start(bf16[48,1152]{1,0:T(8,128)(2,1)S(1)} %get-tuple-element.34.b_own), channel_id=1, source_target_pairs={{0,1},{1,2},{2,3},{3,4},{4,5},{5,6},{6,7},{7,0},{8,9},{9,10},{10,1... | collective-permute-start | bytes 331784 | tf_op jit(solution)/shard_map/ppermute | solution.py:416
  7.6 9.5 %collective-permute-start.5 = (bf16[48,1152]{1,0:T(8,128)(2,1)S(1)}, bf16[48,1152]{1,0:T(8,128)(2,1)S(1)}, u32[]{:S(2)}, u32[]{:S(2)}) collective-permute-start(bf16[48,1152]{1,0:T(8,128)(2,1)S(1)} %get-tuple-element.35), channel_id=1, source_target_pairs={{0,9},{1,10},{2,11},{3,12},{4,13},{5,14},{6,15},{7,8},{8,1},{9,2},... | collective-permute-start | bytes 331784 | tf_op jit(solution)/shard_map/ppermute | solution.py:416
  15.5 10.6 %collective-permute-start.3 = (bf16[2,48,1152]{2,1,0:T(8,128)(2,1)S(1)}, bf16[2,48,1152]{2,1,0:T(8,128)(2,1)S(1)}, u32[]{:S(2)}, u32[]{:S(2)}) collective-permute-start(bf16[2,48,1152]{2,1,0:T(8,128)(2,1)S(1)} %get-tuple-element.32), channel_id=1, source_target_pairs={{0,1},{1,2},{2,3},{3,4},{4,5},{5,6},{6,7},{7,0},{8,9},{9,10},{10,1... | collective-permute-start | bytes 663560 | tf_op jit(solution)/shard_map/ppermute | solution.py:416
  26.2 7.5 %collective-permute-start.6 = (bf16[2,48,1152]{2,1,0:T(8,128)(2,1)S(1)}, bf16[2,48,1152]{2,1,0:T(8,128)(2,1)S(1)}, u32[]{:S(2)}, u32[]{:S(2)}) collective-permute-start(bf16[2,48,1152]{2,1,0:T(8,128)(2,1)S(1)} %get-tuple-element.41), channel_id=1, source_target_pairs={{0,7},{1,0},{2,1},{3,2},{4,3},{5,4},{6,5},{7,6},{8,15},{9,8},{10,9... | collective-permute-start | bytes 663560 | tf_op jit(solution)/shard_map/ppermute | solution.py:416
  28.0 10.4 %all-to-all-start = ((f32[32,8,128]{2,1,0:T(8,128)}), f32[32,8,128]{2,1,0:T(8,128)S(1)}, u32[]{:S(2)}, u32[]{:S(2)}) async-start(f32[32,8,128]{2,1,0:T(8,128)} %bitcast.2), calls=%async_computation | async-start | bytes 262144 | tf_op jit(solution)/shard_map/all_to_all | solution.py:481
  33.8 5.4 %collective-permute-start.7 = (bf16[48,1152]{1,0:T(8,128)(2,1)S(1)}, bf16[48,1152]{1,0:T(8,128)(2,1)S(1)}, u32[]{:S(2)}, u32[]{:S(2)}) collective-permute-start(bf16[48,1152]{1,0:T(8,128)(2,1)S(1)} %get-tuple-element.43), channel_id=1, source_target_pairs={{0,8},{1,9},{2,10},{3,11},{4,12},{5,13},{6,14},{7,15},{8,0},{9,1},... | collective-permute-start | bytes 331784 | tf_op jit(solution)/shard_map/ppermute | solution.py:416

commit v7 on v5

--- a/solution.py
+++ b/solution.py
@@ -201,7 +201,7 @@
     core = my_core()
     blocks = refs[: 2 * chips]
     perm_ref, hi_ref, lo_ref, t_ref = refs[2 * chips : 2 * chips + 4]
-    high_ref, own_ref, low_ref, up_ref, gathered, terms_ref, result = refs[2 * chips + 4 :]
+    high_ref, own_ref, far_ref, pair_ref, gathered, terms_ref, result = refs[2 * chips + 4 :]
     for s in range(chips):
         n = 2 * ((s - 1) % chips)
         gathered[2 * s + core] = blocks[n][...]
@@ -243,9 +243,12 @@
     place = lax.axis_index("en")
     below = jnp.where(place == 0, 0.0, 1.0)
     above = jnp.where(place == lax.axis_size("en") - 1, 0.0, 1.0)
+    odd = lax.rem(place, 2)
+    keep_pair = jnp.where(odd == 1, below, above)
+    keep_far = jnp.where(odd == 1, above, below)
     for i, c in enumerate((core, 1 - core)):
-        low_ref[i] = (result[c] * below).astype(BF)
-        up_ref[i] = (result[2 + c] * above).astype(BF)
+        pair_ref[i] = (result[2 - 2 * odd + c] * keep_pair).astype(BF)
+        far_ref[i] = (result[2 * odd + c] * keep_far).astype(BF)
         own_ref[i] = result[4 + c]
 
 
@@ -352,9 +355,9 @@
             out_ref[i, m] = moved[:, :window]
 
 
-def sum_kernel(own, below, above, mine, theirs):
+def sum_kernel(own, far, pair, mine, theirs):
     for n, out in enumerate((mine, theirs)):
-        out[...] = (own[n] + below[n].astype(F32) + above[n].astype(F32)).astype(BF)
+        out[...] = (own[n] + far[n].astype(F32) + pair[n].astype(F32)).astype(BF)
 
 
 def join_kernel(mine, other, perm_ref, out_ref, mark_ref, halves):
@@ -413,8 +416,12 @@
     def onward(e):
         return (e + 1) % en
 
-    def back(e):
-        return (e - 1) % en
+    def to_pair(e):
+        return e ^ 1 if e ^ 1 < en else e
+
+    def to_far(e):
+        other = e + 1 if e % 2 else e - 1
+        return other if 0 <= other < en else e
 
     blocks = []
     for s in range(1, chips):
@@ -446,7 +453,7 @@
         [pl.BlockSpec(memory_space=pltpu.SMEM), VMEM, VMEM],
     )
 
-    high, own, low, up = call(
+    high, own, far, pair = call(
         functools.partial(product_kernel, half=half, entries=entries, chips=chips),
         [
             shape((3, momenta * local_e, width), BF),
@@ -462,8 +469,8 @@
             pltpu.VMEM((6, rows, width), F32),
         ],
     )
-    from_below = move(up, 0, 0, onward)
-    from_above = move(low, 0, 0, back)
+    from_far = move(far, 0, 0, to_far)
+    from_pair = move(pair, 0, 0, to_pair)
     (partial,) = call(
         functools.partial(
             polar_kernel, half=half, entries=entries, momenta=momenta, local_k=local_k, local_e=local_e,
@@ -478,7 +485,7 @@
         partial.reshape(mom * en, local_k * half, LANES), ("mom", "en"), split_axis=0, concat_axis=0, tiled=True
     )
     mine, theirs = call(
-        sum_kernel, [shape((rows, width), BF)] * 2, [own, from_below, from_above], 0.1
+        sum_kernel, [shape((rows, width), BF)] * 2, [own, from_far, from_pair], 0.1
     )
     other = move(theirs, 0, 1)
     self_energy, mark = call(

time: 34.7 us -> 36.6 us (1.055)
  starting transfers between devices: 13.9 us -> 15.9 us
    all_to_all x1, starting transfers between devices: 2.99 us -> 4.71 us  [body(): lax.all_to_all(partial.reshape(mom * en, local_k * half, LANES), ('mom',...]
    ppermute x8, waiting for transfers between devices: 4.72 us -> 3.37 us  [move(): return lax.ppermute(value, ('mom', 'en'), links)]
    all_to_all x1, waiting for transfers between devices: 1.68 us -> 3.03 us  [body(): lax.all_to_all(partial.reshape(mom * en, local_k * half, LANES), ('mom',...]
  transfers between devices with their start and end apart: 9 -> 9, of which waited for: 4 -> 3; matrix products, arithmetic and copies ran while one was open for 0% -> 0% of each run, Pallas kernels for 31% -> 29%
where the time goes in v7:
time: 36.6 us; the launch traced here: 36.4 us
  starting transfers between devices  15.9 us (43%)
  Pallas kernels  13.4 us (37%)
  waiting for transfers between devices  6.4 us (17%)
  between operations  0.74 us (2%)
    pallas_call x7, Pallas kernels, call(): pl.pallas_call(kernel, out_shape=outs, in_specs=specs or [VMEM] * len(ins...  13.4 us
    ppermute x8, starting transfers between devices, move(): return lax.ppermute(value, ('mom', 'en'), links)  11.2 us
    all_to_all x1, starting transfers between devices, body(): lax.all_to_all(partial.reshape(mom * en, local_k * half, LANES), ('mom',...  4.71 us
    ppermute x8, waiting for transfers between devices, move(): return lax.ppermute(value, ('mom', 'en'), links)  3.37 us
    all_to_all x1, waiting for transfers between devices, body(): lax.all_to_all(partial.reshape(mom * en, local_k * half, LANES), ('mom',...  3.03 us
  transfers between devices with their start and end apart: 9, of which 3 were waited for; matrix products, arithmetic and copies ran while one was open for 0% of the time, Pallas kernels for 29%

profile of v7, /device:TPU:0, one launch (start us, length us, event | category | flops | bytes accessed | tf_op | source)
XLA Modules:
  0.0 36.4 jit_solution(2685708630999477835)
XLA Ops:
  0.6 0.0 copy-start.1
  0.6 0.0 copy-start
  0.7 0.0 copy-start.2
  0.7 2.1 %shard_map.68 = (bf16[48,1152]{1,0:T(8,128)(2,1)S(1)}, bf16[48,1152]{1,0:T(8,128)(2,1)S(1)}, bf16[48,1152]{1,0:T(8,128)(2,1)S(1)}, bf16[48,1152]{1,0:T(8,128)(2,1)S(1)}, bf16[2,48,1152]{2,1,0:T(8,128)(2,1)S(1)}) custom-call(bf16[2,24,8,288]{3,2,1,0:T(8,128)(2,1)} %g_hbm.1, bf16[2,24,8,288]{3,2,1,0:T(8,128)(2,1)} %b_hbm.1), custom_call_target="tpu_custom_call" | custom-call | flops 1500000000 | tf_op jit(solution)/shard_map/pallas_call | solution.py:31
  2.7 0.5 %collective-permute-start.2 = (bf16[2,48,1152]{2,1,0:T(8,128)(2,1)S(1)}, bf16[2,48,1152]{2,1,0:T(8,128)(2,1)S(1)}, u32[]{:S(2)}, u32[]{:S(2)}) collective-permute-start(bf16[2,48,1152]{2,1,0:T(8,128)(2,1)S(1)} %get-tuple-element.24), channel_id=1, source_target_pairs={{0,8},{1,9},{2,10},{3,11},{4,12},{5,13},{6,14},{7,15},{8,0},{9,1},... | collective-permute-start | bytes 663560 | tf_op jit(solution)/shard_map/ppermute | solution.py:414
  3.3 2.6 %collective-permute-start = (bf16[48,1152]{1,0:T(8,128)(2,1)S(1)}, bf16[48,1152]{1,0:T(8,128)(2,1)S(1)}, u32[]{:S(2)}, u32[]{:S(2)}) collective-permute-start(bf16[48,1152]{1,0:T(8,128)(2,1)S(1)} %get-tuple-element.22.refs_2_), channel_id=1, source_target_pairs={{0,16},{1,17},{2,18},{3,19},{4,20},{5,21},{6,22},{7,23},{8,24},{9,... | collective-permute-start | bytes 331784 | tf_op jit(solution)/shard_map/ppermute | solution.py:414
  5.8 0.1 collective-permute-start.1
  5.9 1.8 %collective-permute-start.6 = (bf16[48,1152]{1,0:T(8,128)(2,1)S(1)}, bf16[48,1152]{1,0:T(8,128)(2,1)S(1)}, u32[]{:S(2)}, u32[]{:S(2)}) collective-permute-start(bf16[48,1152]{1,0:T(8,128)(2,1)S(1)} %get-tuple-element.36.b_own), channel_id=1, source_target_pairs={{0,1},{1,2},{2,3},{3,4},{4,5},{5,6},{6,7},{7,0},{8,9},{9,10},{10,1... | collective-permute-start | bytes 331784 | tf_op jit(solution)/shard_map/ppermute | solution.py:414
  7.6 1.2 %collective-permute-start.7 = (bf16[48,1152]{1,0:T(8,128)(2,1)S(1)}, bf16[48,1152]{1,0:T(8,128)(2,1)S(1)}, u32[]{:S(2)}, u32[]{:S(2)}) collective-permute-start(bf16[48,1152]{1,0:T(8,128)(2,1)S(1)} %get-tuple-element.37), channel_id=1, source_target_pairs={{0,9},{1,10},{2,11},{3,12},{4,13},{5,14},{6,15},{7,8},{8,1},{9,2},... | collective-permute-start | bytes 331784 | tf_op jit(solution)/shard_map/ppermute | solution.py:414
  8.8 0.0 copy-done.1
  8.8 0.0 copy-done
  8.8 0.0 copy-done.2
  8.8 2.9 %shard_map.69 = (bf16[24,144,256]{2,1,0:T(8,128)(2,1)S(1)}, bf16[24,144,256]{2,1,0:T(8,128)(2,1)S(1)}, bf16[4,288,768]{2,1,0:T(8,128)(2,1)S(1)}, bf16[192,192]{1...) custom-call(s32[2,4]{1,0:T(2,128)S(1)} %copy-done.2, ...), custom_call_target="tpu_custom_call" | custom-call | flops 3000000000 | tf_op jit(solution)/shard_map/pallas_call | solution.py:31
  11.8 0.0 collective-permute-done.refs_0_
  11.8 0.0 collective-permute-done.1.refs_1_
  11.8 0.0 collective-permute-done.2.refs_3_.both_core
  11.8 3.7 %shard_map.70 = (bf16[3,192,1152]{2,1,0:T(8,128)(2,1)S(1)}, f32[2,48,1152]{2,1,0:T(8,128)S(1)}, bf16[2,48,1152]{2,1,0:T(8,128)(2,1)S(1)}, bf16[2,48,1152]{2,1,0:T(8,128)(2,1)S(1)}) custom-call(bf16[48,1152]{1,0:T(8,128)(2,1)S(1)} %collective-permute-done.refs_0_, bf16[48,1152]{1,0:T(8,128)(2,1)S(1)} %collective-permute-done.1.refs_1_, ...), custom_call_target="tpu_custom_call" | custom-call | flops 4000000000 | tf_op jit(solution)/shard_map/pallas_call | solution.py:31
  15.5 0.7 %collective-permute-start.3 = (bf16[2,48,1152]{2,1,0:T(8,128)(2,1)S(1)}, bf16[2,48,1152]{2,1,0:T(8,128)(2,1)S(1)}, u32[]{:S(2)}, u32[]{:S(2)}) collective-permute-start(bf16[2,48,1152]{2,1,0:T(8,128)(2,1)S(1)} %get-tuple-element.30), channel_id=1, source_target_pairs={{0,0},{1,2},{2,1},{3,4},{4,3},{5,6},{6,5},{7,7},{8,8},{9,10},{10,9... | collective-permute-start | bytes 663560 | tf_op jit(solution)/shard_map/ppermute | solution.py:414
  16.2 4.3 %collective-permute-start.4 = (bf16[2,48,1152]{2,1,0:T(8,128)(2,1)S(1)}, bf16[2,48,1152]{2,1,0:T(8,128)(2,1)S(1)}, u32[]{:S(2)}, u32[]{:S(2)}) collective-permute-start(bf16[2,48,1152]{2,1,0:T(8,128)(2,1)S(1)} %get-tuple-element.31), channel_id=1, source_target_pairs={{0,1},{1,0},{2,3},{3,2},{4,5},{5,4},{6,7},{7,6},{8,9},{9,8},{10,11... | collective-permute-start | bytes 663560 | tf_op jit(solution)/shard_map/ppermute | solution.py:414
  20.5 0.0 collective-permute-done.6.prev_own
  20.5 0.0 collective-permute-done.7.prev_far
  20.5 2.7 %shard_map.73 = f32[4,8,8,128]{3,2,1,0:T(8,128)} custom-call(bf16[48,1152]{1,0:T(8,128)(2,1)S(1)} %get-tuple-element.36.b_own, bf16[2,48,1152]{2,1,0:T(8,128)(2,1)S(1)} %collective-permute-done.2.refs_3_.both_core, bf16[48,1152]{1,0:T(8,128)(2,1)S(1)} %collective-permute-done.6.prev_own, bf16[48,1152]{1,0:T(8,128)(2,1)S(1)} %collective-permute-done.7.prev_far, ...), custom_call_target="tpu_custom_call" | custom-call | flops 3000000000 | tf_op jit(solution)/shard_map/pallas_call | solution.py:31
  23.3 4.7 %all-to-all-start = ((f32[32,8,128]{2,1,0:T(8,128)}), f32[32,8,128]{2,1,0:T(8,128)S(1)}, u32[]{:S(2)}, u32[]{:S(2)}) async-start(f32[32,8,128]{2,1,0:T(8,128)} %bitcast.2), calls=%async_computation | async-start | bytes 262144 | tf_op jit(solution)/shard_map/all_to_all | solution.py:484
  28.0 0.0 collective-permute-done.3.far
  28.0 2.0 %collective-permute-done.4.pair = bf16[2,48,1152]{2,1,0:T(8,128)(2,1)S(1)} collective-permute-done((bf16[2,48,1152]{2,1,0:T(8,128)(2,1)S(1)}, bf16[2,48,1152]{2,1,0:T(8,128)(2,1)S(1)}, u32[]{:S(2)}, u32[]{:S(2)}) %collective-permute-start.4) | collective-permute-done | bytes 221216 | tf_op jit(solution)/shard_map/ppermute | solution.py:414
  30.0 0.1 shard_map.71
  30.1 0.1 collective-permute-start.5
  30.2 1.3 %collective-permute-done.5.other = bf16[48,1152]{1,0:T(8,128)(2,1)S(1)} collective-permute-done((bf16[48,1152]{1,0:T(8,128)(2,1)S(1)}, bf16[48,1152]{1,0:T(8,128)(2,1)S(1)}, u32[]{:S(2)}, u32[]{:S(2)}) %collective-permute-start.5) | collective-permute-done | bytes 110624 | tf_op jit(solution)/shard_map/ppermute | solution.py:414
  31.5 1.2 %shard_map.72 = (bf16[2,24,8,288]{3,2,1,0:T(8,128)(2,1)}, f32[8,128]{1,0:T(8,128)S(1)}) custom-call(bf16[48,1152]{1,0:T(8,128)(2,1)S(1)} %get-tuple-element.32.mine, bf16[48,1152]{1,0:T(8,128)(2,1)S(1)} %collective-permute-done.5.other, bf16[384,384]{1,0:T(8,128)(2,1)S(1)} %get-tuple-element.34.perm_ref), custom_call_target="tpu_custom_call" | custom-call | flops 1000000000 | tf_op jit(solution)/shard_map/pallas_call | solution.py:31
  32.7 3.0 %all-to-all-done = f32[32,8,128]{2,1,0:T(8,128)S(1)} async-done(((f32[32,8,128]{2,1,0:T(8,128)}), f32[32,8,128]{2,1,0:T(8,128)S(1)}, u32[]{:S(2)}, u32[]{:S(2)}) %all-to-all-start) | async-done | bytes 131104 | tf_op jit(solution)/shard_map/all_to_all | solution.py:484
  35.7 0.7 %shard_map.74 = f32[2,3,8,24]{3,2,1,0:T(8,128)} custom-call(f32[4,8,8,128]{3,2,1,0:T(8,128)S(1)} %bitcast.5, f32[8,128]{1,0:T(8,128)S(1)} %get-tuple-element.41.after_ref), custom_call_target="tpu_custom_call" | custom-call | flops 500000000 | tf_op jit(solution)/shard_map/pallas_call | solution.py:31
Async XLA Ops:
  0.6 8.2 %copy-start.1 = (f32[2,3,144]{2,0,1:T(2,128)S(1)}, f32[2,3,144]{2,0,1:T(2,128)}, u32[]{:S(2)}) copy-start(f32[2,3,144]{2,0,1:T(2,128)} %param.7) | copy-start | bytes 10372
  0.6 8.2 %copy-start = (bf16[2,8,24,3,8]{2,4,3,1,0:T(8,128)(2,1)S(1)}, bf16[2,8,24,3,8]{2,4,3,1,0:T(8,128)(2,1)}, u32[]{:S(2)}) copy-start(bf16[2,8,24,3,8]{2,4,3,1,0:T(8,128)(2,1)} %param.9) | copy-start | bytes 55300
  0.7 8.2 %copy-start.2 = (s32[2,4]{1,0:T(2,128)S(1)}, s32[2,4]{1,0:T(2,128)}, u32[]{:S(2)}) copy-start(s32[2,4]{1,0:T(2,128)} %near_ref.1) | copy-start | bytes 100
  2.7 9.1 %collective-permute-start.2 = (bf16[2,48,1152]{2,1,0:T(8,128)(2,1)S(1)}, bf16[2,48,1152]{2,1,0:T(8,128)(2,1)S(1)}, u32[]{:S(2)}, u32[]{:S(2)}) collective-permute-start(bf16[2,48,1152]{2,1,0:T(8,128)(2,1)S(1)} %get-tuple-element.24), channel_id=1, source_target_pairs={{0,8},{1,9},{2,10},{3,11},{4,12},{5,13},{6,14},{7,15},{8,0},{9,1},... | collective-permute-start | bytes 663560 | tf_op jit(solution)/shard_map/ppermute | solution.py:414
  3.3 8.5 %collective-permute-start = (bf16[48,1152]{1,0:T(8,128)(2,1)S(1)}, bf16[48,1152]{1,0:T(8,128)(2,1)S(1)}, u32[]{:S(2)}, u32[]{:S(2)}) collective-permute-start(bf16[48,1152]{1,0:T(8,128)(2,1)S(1)} %get-tuple-element.22.refs_2_), channel_id=1, source_target_pairs={{0,16},{1,17},{2,18},{3,19},{4,20},{5,21},{6,22},{7,23},{8,24},{9,... | collective-permute-start | bytes 331784 | tf_op jit(solution)/shard_map/ppermute | solution.py:414
  5.8 6.0 %collective-permute-start.1 = (bf16[48,1152]{1,0:T(8,128)(2,1)S(1)}, bf16[48,1152]{1,0:T(8,128)(2,1)S(1)}, u32[]{:S(2)}, u32[]{:S(2)}) collective-permute-start(bf16[48,1152]{1,0:T(8,128)(2,1)S(1)} %get-tuple-element.23), channel_id=1, source_target_pairs={{0,24},{1,25},{2,26},{3,27},{4,28},{5,29},{6,30},{7,31},{8,16},{9,... | collective-permute-start | bytes 331784 | tf_op jit(solution)/shard_map/ppermute | solution.py:414
  5.9 14.6 %collective-permute-start.6 = (bf16[48,1152]{1,0:T(8,128)(2,1)S(1)}, bf16[48,1152]{1,0:T(8,128)(2,1)S(1)}, u32[]{:S(2)}, u32[]{:S(2)}) collective-permute-start(bf16[48,1152]{1,0:T(8,128)(2,1)S(1)} %get-tuple-element.36.b_own), channel_id=1, source_target_pairs={{0,1},{1,2},{2,3},{3,4},{4,5},{5,6},{6,7},{7,0},{8,9},{9,10},{10,1... | collective-permute-start | bytes 331784 | tf_op jit(solution)/shard_map/ppermute | solution.py:414
  7.6 12.9 %collective-permute-start.7 = (bf16[48,1152]{1,0:T(8,128)(2,1)S(1)}, bf16[48,1152]{1,0:T(8,128)(2,1)S(1)}, u32[]{:S(2)}, u32[]{:S(2)}) collective-permute-start(bf16[48,1152]{1,0:T(8,128)(2,1)S(1)} %get-tuple-element.37), channel_id=1, source_target_pairs={{0,9},{1,10},{2,11},{3,12},{4,13},{5,14},{6,15},{7,8},{8,1},{9,2},... | collective-permute-start | bytes 331784 | tf_op jit(solution)/shard_map/ppermute | solution.py:414
  15.5 12.5 %collective-permute-start.3 = (bf16[2,48,1152]{2,1,0:T(8,128)(2,1)S(1)}, bf16[2,48,1152]{2,1,0:T(8,128)(2,1)S(1)}, u32[]{:S(2)}, u32[]{:S(2)}) collective-permute-start(bf16[2,48,1152]{2,1,0:T(8,128)(2,1)S(1)} %get-tuple-element.30), channel_id=1, source_target_pairs={{0,0},{1,2},{2,1},{3,4},{4,3},{5,6},{6,5},{7,7},{8,8},{9,10},{10,9... | collective-permute-start | bytes 663560 | tf_op jit(solution)/shard_map/ppermute | solution.py:414
  16.2 13.8 %collective-permute-start.4 = (bf16[2,48,1152]{2,1,0:T(8,128)(2,1)S(1)}, bf16[2,48,1152]{2,1,0:T(8,128)(2,1)S(1)}, u32[]{:S(2)}, u32[]{:S(2)}) collective-permute-start(bf16[2,48,1152]{2,1,0:T(8,128)(2,1)S(1)} %get-tuple-element.31), channel_id=1, source_target_pairs={{0,1},{1,0},{2,3},{3,2},{4,5},{5,4},{6,7},{7,6},{8,9},{9,8},{10,11... | collective-permute-start | bytes 663560 | tf_op jit(solution)/shard_map/ppermute | solution.py:414
  23.3 12.5 %all-to-all-start = ((f32[32,8,128]{2,1,0:T(8,128)}), f32[32,8,128]{2,1,0:T(8,128)S(1)}, u32[]{:S(2)}, u32[]{:S(2)}) async-start(f32[32,8,128]{2,1,0:T(8,128)} %bitcast.2), calls=%async_computation | async-start | bytes 262144 | tf_op jit(solution)/shard_map/all_to_all | solution.py:484
  30.1 1.4 %collective-permute-start.5 = (bf16[48,1152]{1,0:T(8,128)(2,1)S(1)}, bf16[48,1152]{1,0:T(8,128)(2,1)S(1)}, u32[]{:S(2)}, u32[]{:S(2)}) collective-permute-start(bf16[48,1152]{1,0:T(8,128)(2,1)S(1)} %get-tuple-element.33), channel_id=1, source_target_pairs={{0,8},{1,9},{2,10},{3,11},{4,12},{5,13},{6,14},{7,15},{8,0},{9,1},... | collective-permute-start | bytes 331784 | tf_op jit(solution)/shard_map/ppermute | solution.py:414

commit v8 on v5

--- a/solution.py
+++ b/solution.py
@@ -308,8 +308,10 @@
             parts.append(tile.astype(BF))
         rhs = jnp.concatenate(parts, axis=1)
         held = None
+        sources = high_ref[:, :, first * LANES : (last + 1) * LANES]
+        products = dot_t(sources.reshape(-1, sources.shape[2]), rhs)
         for m in range(3):
-            s = dot_t(high_ref[m, :, first * LANES : (last + 1) * LANES], rhs)
+            s = products[m * momenta * local_e : (m + 1) * momenta * local_e]
             acc = None
             for e in range(local_e):
                 row = pltpu.roll(s[e * momenta : (e + 1) * momenta], columns - (local_e - e), 1)
@@ -407,14 +409,15 @@
         for m in range(mom):
             target = ((m // 2 + dchip) % chips) * 2 + (m % 2 if dcore == 0 else 1 - m % 2)
             for e in range(en):
-                links.append((m * en + e, target * en + to(e)))
+                if 0 <= to(e) < en:
+                    links.append((m * en + e, target * en + to(e)))
         return lax.ppermute(value, ("mom", "en"), links)
 
     def onward(e):
         return (e + 1) % en
 
     def back(e):
-        return (e - 1) % en
+        return e - 1
 
     blocks = []
     for s in range(1, chips):

time: 34.7 us -> 36.4 us (1.049)
  starting transfers between devices: 13.9 us -> 15.8 us
    all_to_all x1, starting transfers between devices: 2.99 us -> 6.81 us  [body(): lax.all_to_all(partial.reshape(mom * en, local_k * half, LANES), ('mom',...]
    ppermute x8, starting transfers between devices: 10.9 us -> 9.02 us  [move(): return lax.ppermute(value, ('mom', 'en'), links)]
  transfers between devices with their start and end apart: 9 -> 9, of which waited for: 4 -> 3; matrix products, arithmetic and copies ran while one was open for 0% -> 0% of each run, Pallas kernels for 31% -> 29%
where the time goes in v8:
time: 36.4 us; the launch traced here: 36.2 us
  starting transfers between devices  15.8 us (43%)
  Pallas kernels  13.2 us (36%)
  waiting for transfers between devices  6.39 us (18%)
  between operations  0.76 us (2%)
    pallas_call x7, Pallas kernels, call(): pl.pallas_call(kernel, out_shape=outs, in_specs=specs or [VMEM] * len(ins...  13.2 us
    ppermute x8, starting transfers between devices, move(): return lax.ppermute(value, ('mom', 'en'), links)  9.02 us
    all_to_all x1, starting transfers between devices, body(): lax.all_to_all(partial.reshape(mom * en, local_k * half, LANES), ('mom',...  6.81 us
    ppermute x8, waiting for transfers between devices, move(): return lax.ppermute(value, ('mom', 'en'), links)  4.52 us
    all_to_all x1, waiting for transfers between devices, body(): lax.all_to_all(partial.reshape(mom * en, local_k * half, LANES), ('mom',...  1.87 us
  transfers between devices with their start and end apart: 9, of which 3 were waited for; matrix products, arithmetic and copies ran while one was open for 0% of the time, Pallas kernels for 29%

profile of v8, /device:TPU:0, one launch (start us, length us, event | category | flops | bytes accessed | tf_op | source)
XLA Modules:
  0.0 36.2 jit_solution(10838746530352751907)
XLA Ops:
  0.6 0.0 copy-start.1
  0.6 0.0 copy-start
  0.7 0.0 copy-start.2
  0.7 2.1 %shard_map.68 = (bf16[48,1152]{1,0:T(8,128)(2,1)S(1)}, bf16[48,1152]{1,0:T(8,128)(2,1)S(1)}, bf16[48,1152]{1,0:T(8,128)(2,1)S(1)}, bf16[48,1152]{1,0:T(8,128)(2,1)S(1)}, bf16[2,48,1152]{2,1,0:T(8,128)(2,1)S(1)}) custom-call(bf16[2,24,8,288]{3,2,1,0:T(8,128)(2,1)} %g_hbm.1, bf16[2,24,8,288]{3,2,1,0:T(8,128)(2,1)} %b_hbm.1), custom_call_target="tpu_custom_call" | custom-call | flops 1500000000 | tf_op jit(solution)/shard_map/pallas_call | solution.py:31
  2.7 0.5 %collective-permute-start.2 = (bf16[2,48,1152]{2,1,0:T(8,128)(2,1)S(1)}, bf16[2,48,1152]{2,1,0:T(8,128)(2,1)S(1)}, u32[]{:S(2)}, u32[]{:S(2)}) collective-permute-start(bf16[2,48,1152]{2,1,0:T(8,128)(2,1)S(1)} %get-tuple-element.24), channel_id=1, source_target_pairs={{0,8},{1,9},{2,10},{3,11},{4,12},{5,13},{6,14},{7,15},{8,0},{9,1},... | collective-permute-start | bytes 663560 | tf_op jit(solution)/shard_map/ppermute | solution.py:414
  3.3 2.6 %collective-permute-start = (bf16[48,1152]{1,0:T(8,128)(2,1)S(1)}, bf16[48,1152]{1,0:T(8,128)(2,1)S(1)}, u32[]{:S(2)}, u32[]{:S(2)}) collective-permute-start(bf16[48,1152]{1,0:T(8,128)(2,1)S(1)} %get-tuple-element.22.refs_2_), channel_id=1, source_target_pairs={{0,16},{1,17},{2,18},{3,19},{4,20},{5,21},{6,22},{7,23},{8,24},{9,... | collective-permute-start | bytes 331784 | tf_op jit(solution)/shard_map/ppermute | solution.py:414
  5.8 0.1 collective-permute-start.1
  5.9 1.8 %collective-permute-start.6 = (bf16[48,1152]{1,0:T(8,128)(2,1)S(1)}, bf16[48,1152]{1,0:T(8,128)(2,1)S(1)}, u32[]{:S(2)}, u32[]{:S(2)}) collective-permute-start(bf16[48,1152]{1,0:T(8,128)(2,1)S(1)} %get-tuple-element.36.b_own), channel_id=1, source_target_pairs={{0,1},{1,2},{2,3},{3,4},{4,5},{5,6},{6,7},{7,0},{8,9},{9,10},{10,1... | collective-permute-start | bytes 331784 | tf_op jit(solution)/shard_map/ppermute | solution.py:414
  7.6 1.2 %collective-permute-start.7 = (bf16[48,1152]{1,0:T(8,128)(2,1)S(1)}, bf16[48,1152]{1,0:T(8,128)(2,1)S(1)}, u32[]{:S(2)}, u32[]{:S(2)}) collective-permute-start(bf16[48,1152]{1,0:T(8,128)(2,1)S(1)} %get-tuple-element.37), channel_id=1, source_target_pairs={{0,9},{1,10},{2,11},{3,12},{4,13},{5,14},{6,15},{7,8},{8,1},{9,2},... | collective-permute-start | bytes 331784 | tf_op jit(solution)/shard_map/ppermute | solution.py:414
  8.8 0.0 copy-done.1
  8.8 0.0 copy-done
  8.8 0.0 copy-done.2
  8.8 2.9 %shard_map.69 = (bf16[24,144,256]{2,1,0:T(8,128)(2,1)S(1)}, bf16[24,144,256]{2,1,0:T(8,128)(2,1)S(1)}, bf16[4,288,768]{2,1,0:T(8,128)(2,1)S(1)}, bf16[192,192]{1...) custom-call(s32[2,4]{1,0:T(2,128)S(1)} %copy-done.2, ...), custom_call_target="tpu_custom_call" | custom-call | flops 3000000000 | tf_op jit(solution)/shard_map/pallas_call | solution.py:31
  11.8 0.0 collective-permute-done.refs_0_
  11.8 0.0 collective-permute-done.1.refs_1_
  11.8 0.0 collective-permute-done.2.refs_3_.both_core
  11.8 3.7 %shard_map.70 = (bf16[3,192,1152]{2,1,0:T(8,128)(2,1)S(1)}, f32[2,48,1152]{2,1,0:T(8,128)S(1)}, bf16[2,48,1152]{2,1,0:T(8,128)(2,1)S(1)}, bf16[2,48,1152]{2,1,0:T(8,128)(2,1)S(1)}) custom-call(bf16[48,1152]{1,0:T(8,128)(2,1)S(1)} %collective-permute-done.refs_0_, bf16[48,1152]{1,0:T(8,128)(2,1)S(1)} %collective-permute-done.1.refs_1_, ...), custom_call_target="tpu_custom_call" | custom-call | flops 4000000000 | tf_op jit(solution)/shard_map/pallas_call | solution.py:31
  15.5 1.6 %collective-permute-start.3 = (bf16[2,48,1152]{2,1,0:T(8,128)(2,1)S(1)}, bf16[2,48,1152]{2,1,0:T(8,128)(2,1)S(1)}, u32[]{:S(2)}, u32[]{:S(2)}) collective-permute-start(bf16[2,48,1152]{2,1,0:T(8,128)(2,1)S(1)} %get-tuple-element.30), channel_id=1, source_target_pairs={{0,1},{1,2},{2,3},{3,4},{4,5},{5,6},{6,7},{7,0},{8,9},{9,10},{10,1... | collective-permute-start | bytes 663560 | tf_op jit(solution)/shard_map/ppermute | solution.py:414
  17.1 1.3 %collective-permute-start.4 = (bf16[2,48,1152]{2,1,0:T(8,128)(2,1)S(1)}, bf16[2,48,1152]{2,1,0:T(8,128)(2,1)S(1)}, u32[]{:S(2)}, u32[]{:S(2)}) collective-permute-start(bf16[2,48,1152]{2,1,0:T(8,128)(2,1)S(1)} %get-tuple-element.31), channel_id=1, source_target_pairs={{1,0},{2,1},{3,2},{4,3},{5,4},{6,5},{7,6},{9,8},{10,9},{11,10},{12... | collective-permute-start | bytes 663560 | tf_op jit(solution)/shard_map/ppermute | solution.py:414
  18.4 0.0 collective-permute-done.6.prev_own
  18.4 0.0 collective-permute-done.7.prev_far
  18.4 2.5 %shard_map.73 = f32[4,8,8,128]{3,2,1,0:T(8,128)} custom-call(bf16[48,1152]{1,0:T(8,128)(2,1)S(1)} %get-tuple-element.36.b_own, bf16[2,48,1152]{2,1,0:T(8,128)(2,1)S(1)} %collective-permute-done.2.refs_3_.both_core, bf16[48,1152]{1,0:T(8,128)(2,1)S(1)} %collective-permute-done.6.prev_own, bf16[48,1152]{1,0:T(8,128)(2,1)S(1)} %collective-permute-done.7.prev_far, ...), custom_call_target="tpu_custom_call" | custom-call | flops 3000000000 | tf_op jit(solution)/shard_map/pallas_call | solution.py:31
  20.9 6.8 %all-to-all-start = ((f32[32,8,128]{2,1,0:T(8,128)}), f32[32,8,128]{2,1,0:T(8,128)S(1)}, u32[]{:S(2)}, u32[]{:S(2)}) async-start(f32[32,8,128]{2,1,0:T(8,128)} %bitcast.2), calls=%async_computation | async-start | bytes 262144 | tf_op jit(solution)/shard_map/all_to_all | solution.py:480
  27.7 0.0 collective-permute-done.3.below
  27.7 3.2 %collective-permute-done.4.above = bf16[2,48,1152]{2,1,0:T(8,128)(2,1)S(1)} collective-permute-done((bf16[2,48,1152]{2,1,0:T(8,128)(2,1)S(1)}, bf16[2,48,1152]{2,1,0:T(8,128)(2,1)S(1)}, u32[]{:S(2)}, u32[]{:S(2)}) %collective-permute-start.4) | collective-permute-done | bytes 221216 | tf_op jit(solution)/shard_map/ppermute | solution.py:414
  30.9 0.1 shard_map.71
  31.0 0.1 collective-permute-start.5
  31.1 1.3 %collective-permute-done.5.other = bf16[48,1152]{1,0:T(8,128)(2,1)S(1)} collective-permute-done((bf16[48,1152]{1,0:T(8,128)(2,1)S(1)}, bf16[48,1152]{1,0:T(8,128)(2,1)S(1)}, u32[]{:S(2)}, u32[]{:S(2)}) %collective-permute-start.5) | collective-permute-done | bytes 110624 | tf_op jit(solution)/shard_map/ppermute | solution.py:414
  32.4 1.2 %shard_map.72 = (bf16[2,24,8,288]{3,2,1,0:T(8,128)(2,1)}, f32[8,128]{1,0:T(8,128)S(1)}) custom-call(bf16[48,1152]{1,0:T(8,128)(2,1)S(1)} %get-tuple-element.32.mine, bf16[48,1152]{1,0:T(8,128)(2,1)S(1)} %collective-permute-done.5.other, bf16[384,384]{1,0:T(8,128)(2,1)S(1)} %get-tuple-element.34.perm_ref), custom_call_target="tpu_custom_call" | custom-call | flops 1000000000 | tf_op jit(solution)/shard_map/pallas_call | solution.py:31
  33.6 1.9 %all-to-all-done = f32[32,8,128]{2,1,0:T(8,128)S(1)} async-done(((f32[32,8,128]{2,1,0:T(8,128)}), f32[32,8,128]{2,1,0:T(8,128)S(1)}, u32[]{:S(2)}, u32[]{:S(2)}) %all-to-all-start) | async-done | bytes 131104 | tf_op jit(solution)/shard_map/all_to_all | solution.py:480
  35.5 0.7 %shard_map.74 = f32[2,3,8,24]{3,2,1,0:T(8,128)} custom-call(f32[4,8,8,128]{3,2,1,0:T(8,128)S(1)} %bitcast.5, f32[8,128]{1,0:T(8,128)S(1)} %get-tuple-element.41.after_ref), custom_call_target="tpu_custom_call" | custom-call | flops 500000000 | tf_op jit(solution)/shard_map/pallas_call | solution.py:31
Async XLA Ops:
  0.6 8.2 %copy-start.1 = (f32[2,3,144]{2,0,1:T(2,128)S(1)}, f32[2,3,144]{2,0,1:T(2,128)}, u32[]{:S(2)}) copy-start(f32[2,3,144]{2,0,1:T(2,128)} %param.7) | copy-start | bytes 10372
  0.6 8.2 %copy-start = (bf16[2,8,24,3,8]{2,4,3,1,0:T(8,128)(2,1)S(1)}, bf16[2,8,24,3,8]{2,4,3,1,0:T(8,128)(2,1)}, u32[]{:S(2)}) copy-start(bf16[2,8,24,3,8]{2,4,3,1,0:T(8,128)(2,1)} %param.9) | copy-start | bytes 55300
  0.7 8.2 %copy-start.2 = (s32[2,4]{1,0:T(2,128)S(1)}, s32[2,4]{1,0:T(2,128)}, u32[]{:S(2)}) copy-start(s32[2,4]{1,0:T(2,128)} %near_ref.1) | copy-start | bytes 100
  2.7 9.1 %collective-permute-start.2 = (bf16[2,48,1152]{2,1,0:T(8,128)(2,1)S(1)}, bf16[2,48,1152]{2,1,0:T(8,128)(2,1)S(1)}, u32[]{:S(2)}, u32[]{:S(2)}) collective-permute-start(bf16[2,48,1152]{2,1,0:T(8,128)(2,1)S(1)} %get-tuple-element.24), channel_id=1, source_target_pairs={{0,8},{1,9},{2,10},{3,11},{4,12},{5,13},{6,14},{7,15},{8,0},{9,1},... | collective-permute-start | bytes 663560 | tf_op jit(solution)/shard_map/ppermute | solution.py:414
  3.3 8.5 %collective-permute-start = (bf16[48,1152]{1,0:T(8,128)(2,1)S(1)}, bf16[48,1152]{1,0:T(8,128)(2,1)S(1)}, u32[]{:S(2)}, u32[]{:S(2)}) collective-permute-start(bf16[48,1152]{1,0:T(8,128)(2,1)S(1)} %get-tuple-element.22.refs_2_), channel_id=1, source_target_pairs={{0,16},{1,17},{2,18},{3,19},{4,20},{5,21},{6,22},{7,23},{8,24},{9,... | collective-permute-start | bytes 331784 | tf_op jit(solution)/shard_map/ppermute | solution.py:414
  5.8 6.0 %collective-permute-start.1 = (bf16[48,1152]{1,0:T(8,128)(2,1)S(1)}, bf16[48,1152]{1,0:T(8,128)(2,1)S(1)}, u32[]{:S(2)}, u32[]{:S(2)}) collective-permute-start(bf16[48,1152]{1,0:T(8,128)(2,1)S(1)} %get-tuple-element.23), channel_id=1, source_target_pairs={{0,24},{1,25},{2,26},{3,27},{4,28},{5,29},{6,30},{7,31},{8,16},{9,... | collective-permute-start | bytes 331784 | tf_op jit(solution)/shard_map/ppermute | solution.py:414
  5.9 12.5 %collective-permute-start.6 = (bf16[48,1152]{1,0:T(8,128)(2,1)S(1)}, bf16[48,1152]{1,0:T(8,128)(2,1)S(1)}, u32[]{:S(2)}, u32[]{:S(2)}) collective-permute-start(bf16[48,1152]{1,0:T(8,128)(2,1)S(1)} %get-tuple-element.36.b_own), channel_id=1, source_target_pairs={{0,1},{1,2},{2,3},{3,4},{4,5},{5,6},{6,7},{7,0},{8,9},{9,10},{10,1... | collective-permute-start | bytes 331784 | tf_op jit(solution)/shard_map/ppermute | solution.py:414
  7.6 10.8 %collective-permute-start.7 = (bf16[48,1152]{1,0:T(8,128)(2,1)S(1)}, bf16[48,1152]{1,0:T(8,128)(2,1)S(1)}, u32[]{:S(2)}, u32[]{:S(2)}) collective-permute-start(bf16[48,1152]{1,0:T(8,128)(2,1)S(1)} %get-tuple-element.37), channel_id=1, source_target_pairs={{0,9},{1,10},{2,11},{3,12},{4,13},{5,14},{6,15},{7,8},{8,1},{9,2},... | collective-permute-start | bytes 331784 | tf_op jit(solution)/shard_map/ppermute | solution.py:414
  15.5 12.2 %collective-permute-start.3 = (bf16[2,48,1152]{2,1,0:T(8,128)(2,1)S(1)}, bf16[2,48,1152]{2,1,0:T(8,128)(2,1)S(1)}, u32[]{:S(2)}, u32[]{:S(2)}) collective-permute-start(bf16[2,48,1152]{2,1,0:T(8,128)(2,1)S(1)} %get-tuple-element.30), channel_id=1, source_target_pairs={{0,1},{1,2},{2,3},{3,4},{4,5},{5,6},{6,7},{7,0},{8,9},{9,10},{10,1... | collective-permute-start | bytes 663560 | tf_op jit(solution)/shard_map/ppermute | solution.py:414
  17.1 13.8 %collective-permute-start.4 = (bf16[2,48,1152]{2,1,0:T(8,128)(2,1)S(1)}, bf16[2,48,1152]{2,1,0:T(8,128)(2,1)S(1)}, u32[]{:S(2)}, u32[]{:S(2)}) collective-permute-start(bf16[2,48,1152]{2,1,0:T(8,128)(2,1)S(1)} %get-tuple-element.31), channel_id=1, source_target_pairs={{1,0},{2,1},{3,2},{4,3},{5,4},{6,5},{7,6},{9,8},{10,9},{11,10},{12... | collective-permute-start | bytes 663560 | tf_op jit(solution)/shard_map/ppermute | solution.py:414
  20.9 14.6 %all-to-all-start = ((f32[32,8,128]{2,1,0:T(8,128)}), f32[32,8,128]{2,1,0:T(8,128)S(1)}, u32[]{:S(2)}, u32[]{:S(2)}) async-start(f32[32,8,128]{2,1,0:T(8,128)} %bitcast.2), calls=%async_computation | async-start | bytes 262144 | tf_op jit(solution)/shard_map/all_to_all | solution.py:480
  31.0 1.4 %collective-permute-start.5 = (bf16[48,1152]{1,0:T(8,128)(2,1)S(1)}, bf16[48,1152]{1,0:T(8,128)(2,1)S(1)}, u32[]{:S(2)}, u32[]{:S(2)}) collective-permute-start(bf16[48,1152]{1,0:T(8,128)(2,1)S(1)} %get-tuple-element.33), channel_id=1, source_target_pairs={{0,8},{1,9},{2,10},{3,11},{4,12},{5,13},{6,14},{7,15},{8,0},{9,1},... | collective-permute-start | bytes 331784 | tf_op jit(solution)/shard_map/ppermute | solution.py:414

commit v9 on v5

--- a/solution.py
+++ b/solution.py
@@ -308,8 +308,10 @@
             parts.append(tile.astype(BF))
         rhs = jnp.concatenate(parts, axis=1)
         held = None
+        sources = high_ref[:, :, first * LANES : (last + 1) * LANES]
+        products = dot_t(sources.reshape(-1, sources.shape[2]), rhs)
         for m in range(3):
-            s = dot_t(high_ref[m, :, first * LANES : (last + 1) * LANES], rhs)
+            s = products[m * momenta * local_e : (m + 1) * momenta * local_e]
             acc = None
             for e in range(local_e):
                 row = pltpu.roll(s[e * momenta : (e + 1) * momenta], columns - (local_e - e), 1)
@@ -326,24 +328,28 @@
                 total = pltpu.roll(total, m * (LANES // 4), 1)
             held = total if held is None else held + total
         pieces.append(held)
-    targets, en = out_ref.shape[:2]
-    for t in range(targets):
-        tile = jnp.concatenate(
+    for t in range(out_ref.shape[0]):
+        out_ref[t] = jnp.concatenate(
             [pieces[p][t * local_k + i : t * local_k + i + 1] for i in range(local_k) for p in range(half)], axis=0
         )
-        for e in range(en):
-            out_ref[t, e] = tile
-
-
-def total_kernel(in_ref, after_ref, out_ref, *, half):
-    targets, en = in_ref.shape[:2]
+
+
+def spread_kernel(in_ref, out_ref):
+    for c in range(2):
+        total = in_ref[c]
+        for t in range(c + 2, in_ref.shape[0], 2):
+            total = total + in_ref[t]
+        for e in range(out_ref.shape[0]):
+            out_ref[e, c] = total
+
+
+def total_kernel(in_ref, out_ref, *, half):
     local_k, _, _, window = out_ref.shape
     sums = []
     for c in range(2):
-        total = None
-        for t in range(c, targets, 2):
-            for e in range(en):
-                total = in_ref[t, e] if total is None else total + in_ref[t, e]
+        total = in_ref[0, c]
+        for e in range(1, in_ref.shape[0]):
+            total = total + in_ref[e, c]
         sums.append(total)
     for i in range(local_k):
         tile = jnp.concatenate([sums[c][i * half : (i + 1) * half] for c in range(2)], axis=0)
@@ -357,7 +363,7 @@
         out[...] = (own[n] + below[n].astype(F32) + above[n].astype(F32)).astype(BF)
 
 
-def join_kernel(mine, other, perm_ref, out_ref, mark_ref, halves):
+def join_kernel(mine, other, perm_ref, out_ref, halves):
     core = my_core()
     pairs = out_ref.shape[2]
     entries = out_ref.shape[3]
@@ -369,7 +375,6 @@
         begin = entries * (p % half)
         parts.append(halves[p // half][:, begin : begin + entries])
     stacked = jnp.concatenate(parts, axis=0).astype(BF)
-    mark_ref[...] = jnp.zeros(mark_ref.shape, F32)
     out_ref[...] = dot(perm_ref[...], stacked).astype(BF).reshape(out_ref.shape)
 
 
@@ -469,21 +474,21 @@
             polar_kernel, half=half, entries=entries, momenta=momenta, local_k=local_k, local_e=local_e,
             scale=1.0 / (NO * float(np.sqrt(momenta * total_e))),
         ),
-        [shape((mom, en, local_k * half, LANES), F32)],
+        [shape((mom, local_k * half, LANES), F32)],
         [b_own, both_core, prev_own, prev_far, turn, sort_e, high],
         3,
         [pltpu.VMEM((4, rows, width), BF)],
     )
-    terms = lax.all_to_all(
-        partial.reshape(mom * en, local_k * half, LANES), ("mom", "en"), split_axis=0, concat_axis=0, tiled=True
-    )
+    terms = lax.all_to_all(partial, "mom", split_axis=0, concat_axis=0, tiled=True)
+    (copies,) = call(spread_kernel, [shape((en, 2, local_k * half, LANES), F32)], [terms], 0.2)
+    terms = lax.all_to_all(copies, "en", split_axis=0, concat_axis=0, tiled=True)
     mine, theirs = call(
         sum_kernel, [shape((rows, width), BF)] * 2, [own, from_below, from_above], 0.1
     )
     other = move(theirs, 0, 1)
-    self_energy, mark = call(
+    (self_energy,) = call(
         join_kernel,
-        [shape(green_less.shape, BF), shape((8, LANES), F32)],
+        [shape(green_less.shape, BF)],
         [mine, other, to_rows],
         1,
         [pltpu.VMEM((2, rows, width), F32)],
@@ -491,7 +496,7 @@
     (polar,) = call(
         functools.partial(total_kernel, half=half),
         [shape((local_k, 3, pairs, window), F32)],
-        [terms.reshape(mom, en, local_k * half, LANES), mark],
+        [terms],
         0.5,
     )
     polar = polar.transpose(0, 3, 1, 2)

time: 34.7 us -> 41.5 us (1.20)
  blocking collectives: 0 us -> 6.41 us
  starting transfers between devices: 13.9 us -> 14.4 us
    all_to_all x0 -> x1, blocking collectives: none -> 6.41 us  [body(): lax.all_to_all(partial, 'mom', split_axis=0, concat_axis=0, tiled=True)]
    all_to_all x1, waiting for transfers between devices: 1.68 us -> 6.59 us  [body(): lax.all_to_all(copies, 'en', split_axis=0, concat_axis=0, tiled=True)]
    ppermute x8, waiting for transfers between devices: 4.72 us -> 0.02 us  [move(): return lax.ppermute(value, ('mom', 'en'), links)]
    pallas_call x7 -> x8, Pallas kernels: 13.4 us -> 13.1 us  [call(): pl.pallas_call(kernel, out_shape=outs, in_specs=specs or [VMEM] * len(ins...]
  transfers between devices with their start and end apart: 9 -> 9, of which waited for: 4 -> 1; matrix products, arithmetic and copies ran while one was open for 0% -> 0% of each run, Pallas kernels for 31% -> 24%
where the time goes in v9:
time: 41.5 us; the launch traced here: 41.3 us
  starting transfers between devices  14.4 us (35%)
  Pallas kernels  13.1 us (32%)
  waiting for transfers between devices  6.62 us (16%)
  blocking collectives  6.41 us (15%)
  between operations  0.74 us (2%)
    pallas_call x8, Pallas kernels, call(): pl.pallas_call(kernel, out_shape=outs, in_specs=specs or [VMEM] * len(ins...  13.1 us
    ppermute x8, starting transfers between devices, move(): return lax.ppermute(value, ('mom', 'en'), links)  11 us
    all_to_all x1, waiting for transfers between devices, body(): lax.all_to_all(copies, 'en', split_axis=0, concat_axis=0, tiled=True)  6.59 us
    all_to_all x1, blocking collectives, body(): lax.all_to_all(partial, 'mom', split_axis=0, concat_axis=0, tiled=True)  6.41 us
    all_to_all x1, starting transfers between devices, body(): lax.all_to_all(copies, 'en', split_axis=0, concat_axis=0, tiled=True)  3.35 us
  transfers between devices with their start and end apart: 9, of which 1 were waited for; matrix products, arithmetic and copies ran while one was open for 0% of the time, Pallas kernels for 24%

profile of v9, /device:TPU:0, one launch (start us, length us, event | category | flops | bytes accessed | tf_op | source)
XLA Modules:
  0.0 41.3 jit_solution(12941063802699239081)
XLA Ops:
  0.6 0.0 copy-start.1
  0.6 0.0 copy-start
  0.7 0.0 copy-start.2
  0.7 2.1 %shard_map.68 = (bf16[48,1152]{1,0:T(8,128)(2,1)S(1)}, bf16[48,1152]{1,0:T(8,128)(2,1)S(1)}, bf16[48,1152]{1,0:T(8,128)(2,1)S(1)}, bf16[48,1152]{1,0:T(8,128)(2,1)S(1)}, bf16[2,48,1152]{2,1,0:T(8,128)(2,1)S(1)}) custom-call(bf16[2,24,8,288]{3,2,1,0:T(8,128)(2,1)} %g_hbm.1, bf16[2,24,8,288]{3,2,1,0:T(8,128)(2,1)} %b_hbm.1), custom_call_target="tpu_custom_call" | custom-call | flops 1500000000 | tf_op jit(solution)/shard_map/pallas_call | solution.py:31
  2.7 0.5 %collective-permute-start.2 = (bf16[2,48,1152]{2,1,0:T(8,128)(2,1)S(1)}, bf16[2,48,1152]{2,1,0:T(8,128)(2,1)S(1)}, u32[]{:S(2)}, u32[]{:S(2)}) collective-permute-start(bf16[2,48,1152]{2,1,0:T(8,128)(2,1)S(1)} %get-tuple-element.22), channel_id=1, source_target_pairs={{0,8},{1,9},{2,10},{3,11},{4,12},{5,13},{6,14},{7,15},{8,0},{9,1},... | collective-permute-start | bytes 663560 | tf_op jit(solution)/shard_map/ppermute | solution.py:416
  3.3 2.6 %collective-permute-start = (bf16[48,1152]{1,0:T(8,128)(2,1)S(1)}, bf16[48,1152]{1,0:T(8,128)(2,1)S(1)}, u32[]{:S(2)}, u32[]{:S(2)}) collective-permute-start(bf16[48,1152]{1,0:T(8,128)(2,1)S(1)} %get-tuple-element.20.refs_2_), channel_id=1, source_target_pairs={{0,16},{1,17},{2,18},{3,19},{4,20},{5,21},{6,22},{7,23},{8,24},{9,... | collective-permute-start | bytes 331784 | tf_op jit(solution)/shard_map/ppermute | solution.py:416
  5.8 0.1 collective-permute-start.1
  5.9 1.8 %collective-permute-start.6 = (bf16[48,1152]{1,0:T(8,128)(2,1)S(1)}, bf16[48,1152]{1,0:T(8,128)(2,1)S(1)}, u32[]{:S(2)}, u32[]{:S(2)}) collective-permute-start(bf16[48,1152]{1,0:T(8,128)(2,1)S(1)} %get-tuple-element.33.b_own), channel_id=1, source_target_pairs={{0,1},{1,2},{2,3},{3,4},{4,5},{5,6},{6,7},{7,0},{8,9},{9,10},{10,1... | collective-permute-start | bytes 331784 | tf_op jit(solution)/shard_map/ppermute | solution.py:416
  7.6 1.2 %collective-permute-start.7 = (bf16[48,1152]{1,0:T(8,128)(2,1)S(1)}, bf16[48,1152]{1,0:T(8,128)(2,1)S(1)}, u32[]{:S(2)}, u32[]{:S(2)}) collective-permute-start(bf16[48,1152]{1,0:T(8,128)(2,1)S(1)} %get-tuple-element.34), channel_id=1, source_target_pairs={{0,9},{1,10},{2,11},{3,12},{4,13},{5,14},{6,15},{7,8},{8,1},{9,2},... | collective-permute-start | bytes 331784 | tf_op jit(solution)/shard_map/ppermute | solution.py:416
  8.8 0.0 copy-done.1
  8.8 0.0 copy-done.2
  8.8 2.9 %shard_map.69 = (bf16[24,144,256]{2,1,0:T(8,128)(2,1)S(1)}, bf16[24,144,256]{2,1,0:T(8,128)(2,1)S(1)}, bf16[4,288,768]{2,1,0:T(8,128)(2,1)S(1)}, bf16[192,192]{1...) custom-call(s32[2,4]{1,0:T(2,128)S(1)} %copy-done.2, ...), custom_call_target="tpu_custom_call" | custom-call | flops 3000000000 | tf_op jit(solution)/shard_map/pallas_call | solution.py:31
  11.8 0.0 collective-permute-done.refs_0_
  11.8 0.0 collective-permute-done.1.refs_1_
  11.8 0.0 collective-permute-done.2.refs_3_.both_core
  11.8 3.7 %shard_map.70 = (bf16[3,192,1152]{2,1,0:T(8,128)(2,1)S(1)}, f32[2,48,1152]{2,1,0:T(8,128)S(1)}, bf16[2,48,1152]{2,1,0:T(8,128)(2,1)S(1)}, bf16[2,48,1152]{2,1,0:T(8,128)(2,1)S(1)}) custom-call(bf16[48,1152]{1,0:T(8,128)(2,1)S(1)} %collective-permute-done.refs_0_, bf16[48,1152]{1,0:T(8,128)(2,1)S(1)} %collective-permute-done.1.refs_1_, ...), custom_call_target="tpu_custom_call" | custom-call | flops 4000000000 | tf_op jit(solution)/shard_map/pallas_call | solution.py:31
  15.5 1.6 %collective-permute-start.3 = (bf16[2,48,1152]{2,1,0:T(8,128)(2,1)S(1)}, bf16[2,48,1152]{2,1,0:T(8,128)(2,1)S(1)}, u32[]{:S(2)}, u32[]{:S(2)}) collective-permute-start(bf16[2,48,1152]{2,1,0:T(8,128)(2,1)S(1)} %get-tuple-element.28), channel_id=1, source_target_pairs={{0,1},{1,2},{2,3},{3,4},{4,5},{5,6},{6,7},{7,0},{8,9},{9,10},{10,1... | collective-permute-start | bytes 663560 | tf_op jit(solution)/shard_map/ppermute | solution.py:416
  17.1 3.2 %collective-permute-start.4 = (bf16[2,48,1152]{2,1,0:T(8,128)(2,1)S(1)}, bf16[2,48,1152]{2,1,0:T(8,128)(2,1)S(1)}, u32[]{:S(2)}, u32[]{:S(2)}) collective-permute-start(bf16[2,48,1152]{2,1,0:T(8,128)(2,1)S(1)} %get-tuple-element.29), channel_id=1, source_target_pairs={{0,7},{1,0},{2,1},{3,2},{4,3},{5,4},{6,5},{7,6},{8,15},{9,8},{10,9... | collective-permute-start | bytes 663560 | tf_op jit(solution)/shard_map/ppermute | solution.py:416
  20.3 0.0 collective-permute-done.6.prev_own
  20.3 0.0 collective-permute-done.7.prev_far
  20.3 1.8 %shard_map.73 = f32[4,8,128]{2,1,0:T(8,128)S(1)} custom-call(bf16[48,1152]{1,0:T(8,128)(2,1)S(1)} %get-tuple-element.33.b_own, bf16[2,48,1152]{2,1,0:T(8,128)(2,1)S(1)} %collective-permute-done.2.refs_3_.both_core, bf16[48,1152]{1,0:T(8,128)(2,1)S(1)} %collective-permute-done.6.prev_own, bf16[48,1152]{1,0:T(8,128)(2,1)S(1)} %collective-permute-done.7.prev_far, ...), custom_call_target="tpu_custom_call" | custom-call | flops 3000000000 | tf_op jit(solution)/shard_map/pallas_call | solution.py:31
  22.1 6.4 %all_to_all.10.in_ref = f32[4,8,128]{2,1,0:T(8,128)S(1)} all-to-all(f32[4,8,128]{2,1,0:T(8,128)S(1)} %shard_map.73), channel_id=1, replica_groups=mesh['mom'=4,'en'=8] {'mom'}, dimensions={0} | all-to-all | bytes 32768 | tf_op jit(solution)/shard_map/all_to_all | solution.py:482
  28.5 0.6 %shard_map.74 = f32[8,2,8,128]{3,2,1,0:T(8,128)} custom-call(f32[4,8,128]{2,1,0:T(8,128)S(1)} %all_to_all.10.in_ref), custom_call_target="tpu_custom_call" | custom-call | flops 200000000 | tf_op jit(solution)/shard_map/pallas_call | solution.py:31
  29.2 3.4 %all-to-all-start.1 = ((f32[8,2,8,128]{3,2,1,0:T(8,128)}), f32[8,2,8,128]{3,2,1,0:T(8,128)S(1)}, u32[]{:S(2)}, u32[]{:S(2)}) async-start(f32[8,2,8,128]{3,2,1,0:T(8,128)} %shard_map.74), calls=%async_computation.1 | async-start | bytes 131072 | tf_op jit(solution)/shard_map/all_to_all | solution.py:484
  32.5 0.0 collective-permute-done.3.below
  32.6 0.0 collective-permute-done.4.above
  32.6 0.1 shard_map.71
  32.7 0.1 collective-permute-start.5
  32.8 6.6 %all-to-all-done.1.in_ref = f32[8,2,8,128]{3,2,1,0:T(8,128)S(1)} async-done(((f32[8,2,8,128]{3,2,1,0:T(8,128)}), f32[8,2,8,128]{3,2,1,0:T(8,128)S(1)}, u32[]{:S(2)}, u32[]{:S(2)}) %all-to-all-start.1) | async-done | bytes 65568 | tf_op jit(solution)/shard_map/all_to_all | solution.py:484
  39.4 0.7 %shard_map.75 = f32[2,3,8,24]{3,2,1,0:T(8,128)} custom-call(f32[8,2,8,128]{3,2,1,0:T(8,128)S(1)} %all-to-all-done.1.in_ref), custom_call_target="tpu_custom_call" | custom-call | flops 500000000 | tf_op jit(solution)/shard_map/pallas_call | solution.py:31
  40.1 0.0 collective-permute-done.5.other
  40.1 1.2 %shard_map.72 = bf16[2,24,8,288]{3,2,1,0:T(8,128)(2,1)} custom-call(bf16[48,1152]{1,0:T(8,128)(2,1)S(1)} %get-tuple-element.30.mine, bf16[48,1152]{1,0:T(8,128)(2,1)S(1)} %collective-permute-done.5.other, bf16[384,384]{1,0:T(8,128)(2,1)S(1)} %get-tuple-element.32.perm_ref), custom_call_target="tpu_custom_call" | custom-call | flops 1000000000 | tf_op jit(solution)/shard_map/pallas_call | solution.py:31
  (1 shorter events, 0.0 us)
Async XLA Ops:
  0.6 8.2 %copy-start.1 = (f32[2,3,144]{2,0,1:T(2,128)S(1)}, f32[2,3,144]{2,0,1:T(2,128)}, u32[]{:S(2)}) copy-start(f32[2,3,144]{2,0,1:T(2,128)} %param.7) | copy-start | bytes 10372
  0.6 8.2 %copy-start = (bf16[2,8,24,3,8]{2,4,3,1,0:T(8,128)(2,1)S(1)}, bf16[2,8,24,3,8]{2,4,3,1,0:T(8,128)(2,1)}, u32[]{:S(2)}) copy-start(bf16[2,8,24,3,8]{2,4,3,1,0:T(8,128)(2,1)} %param.9) | copy-start | bytes 55300
  0.7 8.2 %copy-start.2 = (s32[2,4]{1,0:T(2,128)S(1)}, s32[2,4]{1,0:T(2,128)}, u32[]{:S(2)}) copy-start(s32[2,4]{1,0:T(2,128)} %near_ref.1) | copy-start | bytes 100
  2.7 9.1 %collective-permute-start.2 = (bf16[2,48,1152]{2,1,0:T(8,128)(2,1)S(1)}, bf16[2,48,1152]{2,1,0:T(8,128)(2,1)S(1)}, u32[]{:S(2)}, u32[]{:S(2)}) collective-permute-start(bf16[2,48,1152]{2,1,0:T(8,128)(2,1)S(1)} %get-tuple-element.22), channel_id=1, source_target_pairs={{0,8},{1,9},{2,10},{3,11},{4,12},{5,13},{6,14},{7,15},{8,0},{9,1},... | collective-permute-start | bytes 663560 | tf_op jit(solution)/shard_map/ppermute | solution.py:416
  3.3 8.5 %collective-permute-start = (bf16[48,1152]{1,0:T(8,128)(2,1)S(1)}, bf16[48,1152]{1,0:T(8,128)(2,1)S(1)}, u32[]{:S(2)}, u32[]{:S(2)}) collective-permute-start(bf16[48,1152]{1,0:T(8,128)(2,1)S(1)} %get-tuple-element.20.refs_2_), channel_id=1, source_target_pairs={{0,16},{1,17},{2,18},{3,19},{4,20},{5,21},{6,22},{7,23},{8,24},{9,... | collective-permute-start | bytes 331784 | tf_op jit(solution)/shard_map/ppermute | solution.py:416
  5.8 6.0 %collective-permute-start.1 = (bf16[48,1152]{1,0:T(8,128)(2,1)S(1)}, bf16[48,1152]{1,0:T(8,128)(2,1)S(1)}, u32[]{:S(2)}, u32[]{:S(2)}) collective-permute-start(bf16[48,1152]{1,0:T(8,128)(2,1)S(1)} %get-tuple-element.21), channel_id=1, source_target_pairs={{0,24},{1,25},{2,26},{3,27},{4,28},{5,29},{6,30},{7,31},{8,16},{9,... | collective-permute-start | bytes 331784 | tf_op jit(solution)/shard_map/ppermute | solution.py:416
  5.9 14.4 %collective-permute-start.6 = (bf16[48,1152]{1,0:T(8,128)(2,1)S(1)}, bf16[48,1152]{1,0:T(8,128)(2,1)S(1)}, u32[]{:S(2)}, u32[]{:S(2)}) collective-permute-start(bf16[48,1152]{1,0:T(8,128)(2,1)S(1)} %get-tuple-element.33.b_own), channel_id=1, source_target_pairs={{0,1},{1,2},{2,3},{3,4},{4,5},{5,6},{6,7},{7,0},{8,9},{9,10},{10,1... | collective-permute-start | bytes 331784 | tf_op jit(solution)/shard_map/ppermute | solution.py:416
  7.6 12.7 %collective-permute-start.7 = (bf16[48,1152]{1,0:T(8,128)(2,1)S(1)}, bf16[48,1152]{1,0:T(8,128)(2,1)S(1)}, u32[]{:S(2)}, u32[]{:S(2)}) collective-permute-start(bf16[48,1152]{1,0:T(8,128)(2,1)S(1)} %get-tuple-element.34), channel_id=1, source_target_pairs={{0,9},{1,10},{2,11},{3,12},{4,13},{5,14},{6,15},{7,8},{8,1},{9,2},... | collective-permute-start | bytes 331784 | tf_op jit(solution)/shard_map/ppermute | solution.py:416
  15.5 17.0 %collective-permute-start.3 = (bf16[2,48,1152]{2,1,0:T(8,128)(2,1)S(1)}, bf16[2,48,1152]{2,1,0:T(8,128)(2,1)S(1)}, u32[]{:S(2)}, u32[]{:S(2)}) collective-permute-start(bf16[2,48,1152]{2,1,0:T(8,128)(2,1)S(1)} %get-tuple-element.28), channel_id=1, source_target_pairs={{0,1},{1,2},{2,3},{3,4},{4,5},{5,6},{6,7},{7,0},{8,9},{9,10},{10,1... | collective-permute-start | bytes 663560 | tf_op jit(solution)/shard_map/ppermute | solution.py:416
  17.1 15.4 %collective-permute-start.4 = (bf16[2,48,1152]{2,1,0:T(8,128)(2,1)S(1)}, bf16[2,48,1152]{2,1,0:T(8,128)(2,1)S(1)}, u32[]{:S(2)}, u32[]{:S(2)}) collective-permute-start(bf16[2,48,1152]{2,1,0:T(8,128)(2,1)S(1)} %get-tuple-element.29), channel_id=1, source_target_pairs={{0,7},{1,0},{2,1},{3,2},{4,3},{5,4},{6,5},{7,6},{8,15},{9,8},{10,9... | collective-permute-start | bytes 663560 | tf_op jit(solution)/shard_map/ppermute | solution.py:416
  29.2 10.2 %all-to-all-start.1 = ((f32[8,2,8,128]{3,2,1,0:T(8,128)}), f32[8,2,8,128]{3,2,1,0:T(8,128)S(1)}, u32[]{:S(2)}, u32[]{:S(2)}) async-start(f32[8,2,8,128]{3,2,1,0:T(8,128)} %shard_map.74), calls=%async_computation.1 | async-start | bytes 131072 | tf_op jit(solution)/shard_map/all_to_all | solution.py:484
  32.7 7.4 %collective-permute-start.5 = (bf16[48,1152]{1,0:T(8,128)(2,1)S(1)}, bf16[48,1152]{1,0:T(8,128)(2,1)S(1)}, u32[]{:S(2)}, u32[]{:S(2)}) collective-permute-start(bf16[48,1152]{1,0:T(8,128)(2,1)S(1)} %get-tuple-element.31), channel_id=1, source_target_pairs={{0,8},{1,9},{2,10},{3,11},{4,12},{5,13},{6,14},{7,15},{8,0},{9,1},... | collective-permute-start | bytes 331784 | tf_op jit(solution)/shard_map/ppermute | solution.py:416

commit v10 on v7

--- a/solution.py
+++ b/solution.py
@@ -311,8 +311,10 @@
             parts.append(tile.astype(BF))
         rhs = jnp.concatenate(parts, axis=1)
         held = None
+        sources = high_ref[:, :, first * LANES : (last + 1) * LANES]
+        products = dot_t(sources.reshape(-1, sources.shape[2]), rhs)
         for m in range(3):
-            s = dot_t(high_ref[m, :, first * LANES : (last + 1) * LANES], rhs)
+            s = products[m * momenta * local_e : (m + 1) * momenta * local_e]
             acc = None
             for e in range(local_e):
                 row = pltpu.roll(s[e * momenta : (e + 1) * momenta], columns - (local_e - e), 1)
@@ -421,7 +423,7 @@
 
     def to_far(e):
         other = e + 1 if e % 2 else e - 1
-        return other if 0 <= other < en else e
+        return other % en if en % 2 == 0 else max(other, 0)
 
     blocks = []
     for s in range(1, chips):

time: 36.6 us -> 35.2 us (0.962)
  starting transfers between devices: 15.9 us -> 14 us
  waiting for transfers between devices: 6.4 us -> 7.12 us
    ppermute x8, waiting for transfers between devices: 3.37 us -> 7.11 us  [move(): return lax.ppermute(value, ('mom', 'en'), links)]
    all_to_all x1, waiting for transfers between devices: 3.03 us -> 0.01 us  [body(): lax.all_to_all(partial.reshape(mom * en, local_k * half, LANES), ('mom',...]
    all_to_all x1, starting transfers between devices: 4.71 us -> 3.35 us  [body(): lax.all_to_all(partial.reshape(mom * en, local_k * half, LANES), ('mom',...]
    ppermute x8, starting transfers between devices: 11.2 us -> 10.6 us  [move(): return lax.ppermute(value, ('mom', 'en'), links)]
  transfers between devices with their start and end apart: 9 -> 9, of which waited for: 3 -> 3; matrix products, arithmetic and copies ran while one was open for 0% -> 0% of each run, Pallas kernels for 29% -> 30%
where the time goes in v10:
time: 35.2 us; the launch traced here: 35 us
  starting transfers between devices  14 us (40%)
  Pallas kernels  13.1 us (37%)
  waiting for transfers between devices  7.12 us (20%)
  between operations  0.73 us (2%)
    pallas_call x7, Pallas kernels, call(): pl.pallas_call(kernel, out_shape=outs, in_specs=specs or [VMEM] * len(ins...  13.1 us
    ppermute x8, starting transfers between devices, move(): return lax.ppermute(value, ('mom', 'en'), links)  10.6 us
    ppermute x8, waiting for transfers between devices, move(): return lax.ppermute(value, ('mom', 'en'), links)  7.11 us
    all_to_all x1, starting transfers between devices, body(): lax.all_to_all(partial.reshape(mom * en, local_k * half, LANES), ('mom',...  3.35 us
  transfers between devices with their start and end apart: 9, of which 3 were waited for; matrix products, arithmetic and copies ran while one was open for 0% of the time, Pallas kernels for 30%

profile of v10, /device:TPU:0, one launch (start us, length us, event | category | flops | bytes accessed | tf_op | source)
XLA Modules:
  0.0 35.0 jit_solution(1722256325724842225)
XLA Ops:
  0.6 0.0 copy-start.1
  0.6 0.0 copy-start
  0.7 0.0 copy-start.2
  0.7 2.1 %shard_map.68 = (bf16[48,1152]{1,0:T(8,128)(2,1)S(1)}, bf16[48,1152]{1,0:T(8,128)(2,1)S(1)}, bf16[48,1152]{1,0:T(8,128)(2,1)S(1)}, bf16[48,1152]{1,0:T(8,128)(2,1)S(1)}, bf16[2,48,1152]{2,1,0:T(8,128)(2,1)S(1)}) custom-call(bf16[2,24,8,288]{3,2,1,0:T(8,128)(2,1)} %g_hbm.1, bf16[2,24,8,288]{3,2,1,0:T(8,128)(2,1)} %b_hbm.1), custom_call_target="tpu_custom_call" | custom-call | flops 1500000000 | tf_op jit(solution)/shard_map/pallas_call | solution.py:31
  2.7 0.5 %collective-permute-start.2 = (bf16[2,48,1152]{2,1,0:T(8,128)(2,1)S(1)}, bf16[2,48,1152]{2,1,0:T(8,128)(2,1)S(1)}, u32[]{:S(2)}, u32[]{:S(2)}) collective-permute-start(bf16[2,48,1152]{2,1,0:T(8,128)(2,1)S(1)} %get-tuple-element.24), channel_id=1, source_target_pairs={{0,8},{1,9},{2,10},{3,11},{4,12},{5,13},{6,14},{7,15},{8,0},{9,1},... | collective-permute-start | bytes 663560 | tf_op jit(solution)/shard_map/ppermute | solution.py:416
  3.3 2.6 %collective-permute-start = (bf16[48,1152]{1,0:T(8,128)(2,1)S(1)}, bf16[48,1152]{1,0:T(8,128)(2,1)S(1)}, u32[]{:S(2)}, u32[]{:S(2)}) collective-permute-start(bf16[48,1152]{1,0:T(8,128)(2,1)S(1)} %get-tuple-element.22.refs_2_), channel_id=1, source_target_pairs={{0,16},{1,17},{2,18},{3,19},{4,20},{5,21},{6,22},{7,23},{8,24},{9,... | collective-permute-start | bytes 331784 | tf_op jit(solution)/shard_map/ppermute | solution.py:416
  5.8 0.1 collective-permute-start.1
  5.9 1.8 %collective-permute-start.6 = (bf16[48,1152]{1,0:T(8,128)(2,1)S(1)}, bf16[48,1152]{1,0:T(8,128)(2,1)S(1)}, u32[]{:S(2)}, u32[]{:S(2)}) collective-permute-start(bf16[48,1152]{1,0:T(8,128)(2,1)S(1)} %get-tuple-element.36.b_own), channel_id=1, source_target_pairs={{0,1},{1,2},{2,3},{3,4},{4,5},{5,6},{6,7},{7,0},{8,9},{9,10},{10,1... | collective-permute-start | bytes 331784 | tf_op jit(solution)/shard_map/ppermute | solution.py:416
  7.6 1.2 %collective-permute-start.7 = (bf16[48,1152]{1,0:T(8,128)(2,1)S(1)}, bf16[48,1152]{1,0:T(8,128)(2,1)S(1)}, u32[]{:S(2)}, u32[]{:S(2)}) collective-permute-start(bf16[48,1152]{1,0:T(8,128)(2,1)S(1)} %get-tuple-element.37), channel_id=1, source_target_pairs={{0,9},{1,10},{2,11},{3,12},{4,13},{5,14},{6,15},{7,8},{8,1},{9,2},... | collective-permute-start | bytes 331784 | tf_op jit(solution)/shard_map/ppermute | solution.py:416
  8.8 0.0 copy-done.1
  8.8 0.0 copy-done
  8.8 0.0 copy-done.2
  8.8 2.9 %shard_map.69 = (bf16[24,144,256]{2,1,0:T(8,128)(2,1)S(1)}, bf16[24,144,256]{2,1,0:T(8,128)(2,1)S(1)}, bf16[4,288,768]{2,1,0:T(8,128)(2,1)S(1)}, bf16[192,192]{1...) custom-call(s32[2,4]{1,0:T(2,128)S(1)} %copy-done.2, ...), custom_call_target="tpu_custom_call" | custom-call | flops 3000000000 | tf_op jit(solution)/shard_map/pallas_call | solution.py:31
  11.8 0.0 collective-permute-done.refs_0_
  11.8 0.0 collective-permute-done.1.refs_1_
  11.8 0.0 collective-permute-done.2.refs_3_.both_core
  11.8 3.7 %shard_map.70 = (bf16[3,192,1152]{2,1,0:T(8,128)(2,1)S(1)}, f32[2,48,1152]{2,1,0:T(8,128)S(1)}, bf16[2,48,1152]{2,1,0:T(8,128)(2,1)S(1)}, bf16[2,48,1152]{2,1,0:T(8,128)(2,1)S(1)}) custom-call(bf16[48,1152]{1,0:T(8,128)(2,1)S(1)} %collective-permute-done.refs_0_, bf16[48,1152]{1,0:T(8,128)(2,1)S(1)} %collective-permute-done.1.refs_1_, ...), custom_call_target="tpu_custom_call" | custom-call | flops 4000000000 | tf_op jit(solution)/shard_map/pallas_call | solution.py:31
  15.5 4.5 %collective-permute-start.3 = (bf16[2,48,1152]{2,1,0:T(8,128)(2,1)S(1)}, bf16[2,48,1152]{2,1,0:T(8,128)(2,1)S(1)}, u32[]{:S(2)}, u32[]{:S(2)}) collective-permute-start(bf16[2,48,1152]{2,1,0:T(8,128)(2,1)S(1)} %get-tuple-element.30), channel_id=1, source_target_pairs={{0,7},{1,2},{2,1},{3,4},{4,3},{5,6},{6,5},{7,0},{8,15},{9,10},{10,... | collective-permute-start | bytes 663560 | tf_op jit(solution)/shard_map/ppermute | solution.py:416
  20.0 0.0 collective-permute-start.4
  20.0 0.0 collective-permute-done.6.prev_own
  20.0 0.0 collective-permute-done.7.prev_far
  20.0 2.5 %shard_map.73 = f32[4,8,8,128]{3,2,1,0:T(8,128)} custom-call(bf16[48,1152]{1,0:T(8,128)(2,1)S(1)} %get-tuple-element.36.b_own, bf16[2,48,1152]{2,1,0:T(8,128)(2,1)S(1)} %collective-permute-done.2.refs_3_.both_core, bf16[48,1152]{1,0:T(8,128)(2,1)S(1)} %collective-permute-done.6.prev_own, bf16[48,1152]{1,0:T(8,128)(2,1)S(1)} %collective-permute-done.7.prev_far, ...), custom_call_target="tpu_custom_call" | custom-call | flops 3000000000 | tf_op jit(solution)/shard_map/pallas_call | solution.py:31
  22.5 3.3 %all-to-all-start = ((f32[32,8,128]{2,1,0:T(8,128)}), f32[32,8,128]{2,1,0:T(8,128)S(1)}, u32[]{:S(2)}, u32[]{:S(2)}) async-start(f32[32,8,128]{2,1,0:T(8,128)} %bitcast.2), calls=%async_computation | async-start | bytes 262144 | tf_op jit(solution)/shard_map/all_to_all | solution.py:486
  25.8 0.4 %collective-permute-done.3.far = bf16[2,48,1152]{2,1,0:T(8,128)(2,1)S(1)} collective-permute-done((bf16[2,48,1152]{2,1,0:T(8,128)(2,1)S(1)}, bf16[2,48,1152]{2,1,0:T(8,128)(2,1)S(1)}, u32[]{:S(2)}, u32[]{:S(2)}) %collective-permute-start.3) | collective-permute-done | bytes 221216 | tf_op jit(solution)/shard_map/ppermute | solution.py:416
  26.2 5.4 %collective-permute-done.4.pair = bf16[2,48,1152]{2,1,0:T(8,128)(2,1)S(1)} collective-permute-done((bf16[2,48,1152]{2,1,0:T(8,128)(2,1)S(1)}, bf16[2,48,1152]{2,1,0:T(8,128)(2,1)S(1)}, u32[]{:S(2)}, u32[]{:S(2)}) %collective-permute-start.4) | collective-permute-done | bytes 221216 | tf_op jit(solution)/shard_map/ppermute | solution.py:416
  31.6 0.1 shard_map.71
  31.7 0.1 collective-permute-start.5
  31.8 1.3 %collective-permute-done.5.other = bf16[48,1152]{1,0:T(8,128)(2,1)S(1)} collective-permute-done((bf16[48,1152]{1,0:T(8,128)(2,1)S(1)}, bf16[48,1152]{1,0:T(8,128)(2,1)S(1)}, u32[]{:S(2)}, u32[]{:S(2)}) %collective-permute-start.5) | collective-permute-done | bytes 110624 | tf_op jit(solution)/shard_map/ppermute | solution.py:416
  33.1 1.2 %shard_map.72 = (bf16[2,24,8,288]{3,2,1,0:T(8,128)(2,1)}, f32[8,128]{1,0:T(8,128)S(1)}) custom-call(bf16[48,1152]{1,0:T(8,128)(2,1)S(1)} %get-tuple-element.32.mine, bf16[48,1152]{1,0:T(8,128)(2,1)S(1)} %collective-permute-done.5.other, bf16[384,384]{1,0:T(8,128)(2,1)S(1)} %get-tuple-element.34.perm_ref), custom_call_target="tpu_custom_call" | custom-call | flops 1000000000 | tf_op jit(solution)/shard_map/pallas_call | solution.py:31
  34.3 0.0 all-to-all-done
  34.3 0.7 %shard_map.74 = f32[2,3,8,24]{3,2,1,0:T(8,128)} custom-call(f32[4,8,8,128]{3,2,1,0:T(8,128)S(1)} %bitcast.5, f32[8,128]{1,0:T(8,128)S(1)} %get-tuple-element.41.after_ref), custom_call_target="tpu_custom_call" | custom-call | flops 500000000 | tf_op jit(solution)/shard_map/pallas_call | solution.py:31
Async XLA Ops:
  0.6 8.2 %copy-start.1 = (f32[2,3,144]{2,0,1:T(2,128)S(1)}, f32[2,3,144]{2,0,1:T(2,128)}, u32[]{:S(2)}) copy-start(f32[2,3,144]{2,0,1:T(2,128)} %param.7) | copy-start | bytes 10372
  0.6 8.2 %copy-start = (bf16[2,8,24,3,8]{2,4,3,1,0:T(8,128)(2,1)S(1)}, bf16[2,8,24,3,8]{2,4,3,1,0:T(8,128)(2,1)}, u32[]{:S(2)}) copy-start(bf16[2,8,24,3,8]{2,4,3,1,0:T(8,128)(2,1)} %param.9) | copy-start | bytes 55300
  0.7 8.2 %copy-start.2 = (s32[2,4]{1,0:T(2,128)S(1)}, s32[2,4]{1,0:T(2,128)}, u32[]{:S(2)}) copy-start(s32[2,4]{1,0:T(2,128)} %near_ref.1) | copy-start | bytes 100
  2.7 9.1 %collective-permute-start.2 = (bf16[2,48,1152]{2,1,0:T(8,128)(2,1)S(1)}, bf16[2,48,1152]{2,1,0:T(8,128)(2,1)S(1)}, u32[]{:S(2)}, u32[]{:S(2)}) collective-permute-start(bf16[2,48,1152]{2,1,0:T(8,128)(2,1)S(1)} %get-tuple-element.24), channel_id=1, source_target_pairs={{0,8},{1,9},{2,10},{3,11},{4,12},{5,13},{6,14},{7,15},{8,0},{9,1},... | collective-permute-start | bytes 663560 | tf_op jit(solution)/shard_map/ppermute | solution.py:416
  3.3 8.5 %collective-permute-start = (bf16[48,1152]{1,0:T(8,128)(2,1)S(1)}, bf16[48,1152]{1,0:T(8,128)(2,1)S(1)}, u32[]{:S(2)}, u32[]{:S(2)}) collective-permute-start(bf16[48,1152]{1,0:T(8,128)(2,1)S(1)} %get-tuple-element.22.refs_2_), channel_id=1, source_target_pairs={{0,16},{1,17},{2,18},{3,19},{4,20},{5,21},{6,22},{7,23},{8,24},{9,... | collective-permute-start | bytes 331784 | tf_op jit(solution)/shard_map/ppermute | solution.py:416
  5.8 6.0 %collective-permute-start.1 = (bf16[48,1152]{1,0:T(8,128)(2,1)S(1)}, bf16[48,1152]{1,0:T(8,128)(2,1)S(1)}, u32[]{:S(2)}, u32[]{:S(2)}) collective-permute-start(bf16[48,1152]{1,0:T(8,128)(2,1)S(1)} %get-tuple-element.23), channel_id=1, source_target_pairs={{0,24},{1,25},{2,26},{3,27},{4,28},{5,29},{6,30},{7,31},{8,16},{9,... | collective-permute-start | bytes 331784 | tf_op jit(solution)/shard_map/ppermute | solution.py:416
  5.9 14.1 %collective-permute-start.6 = (bf16[48,1152]{1,0:T(8,128)(2,1)S(1)}, bf16[48,1152]{1,0:T(8,128)(2,1)S(1)}, u32[]{:S(2)}, u32[]{:S(2)}) collective-permute-start(bf16[48,1152]{1,0:T(8,128)(2,1)S(1)} %get-tuple-element.36.b_own), channel_id=1, source_target_pairs={{0,1},{1,2},{2,3},{3,4},{4,5},{5,6},{6,7},{7,0},{8,9},{9,10},{10,1... | collective-permute-start | bytes 331784 | tf_op jit(solution)/shard_map/ppermute | solution.py:416
  7.6 12.3 %collective-permute-start.7 = (bf16[48,1152]{1,0:T(8,128)(2,1)S(1)}, bf16[48,1152]{1,0:T(8,128)(2,1)S(1)}, u32[]{:S(2)}, u32[]{:S(2)}) collective-permute-start(bf16[48,1152]{1,0:T(8,128)(2,1)S(1)} %get-tuple-element.37), channel_id=1, source_target_pairs={{0,9},{1,10},{2,11},{3,12},{4,13},{5,14},{6,15},{7,8},{8,1},{9,2},... | collective-permute-start | bytes 331784 | tf_op jit(solution)/shard_map/ppermute | solution.py:416
  15.5 10.7 %collective-permute-start.3 = (bf16[2,48,1152]{2,1,0:T(8,128)(2,1)S(1)}, bf16[2,48,1152]{2,1,0:T(8,128)(2,1)S(1)}, u32[]{:S(2)}, u32[]{:S(2)}) collective-permute-start(bf16[2,48,1152]{2,1,0:T(8,128)(2,1)S(1)} %get-tuple-element.30), channel_id=1, source_target_pairs={{0,7},{1,2},{2,1},{3,4},{4,3},{5,6},{6,5},{7,0},{8,15},{9,10},{10,... | collective-permute-start | bytes 663560 | tf_op jit(solution)/shard_map/ppermute | solution.py:416
  20.0 11.7 %collective-permute-start.4 = (bf16[2,48,1152]{2,1,0:T(8,128)(2,1)S(1)}, bf16[2,48,1152]{2,1,0:T(8,128)(2,1)S(1)}, u32[]{:S(2)}, u32[]{:S(2)}) collective-permute-start(bf16[2,48,1152]{2,1,0:T(8,128)(2,1)S(1)} %get-tuple-element.31), channel_id=1, source_target_pairs={{0,1},{1,0},{2,3},{3,2},{4,5},{5,4},{6,7},{7,6},{8,9},{9,8},{10,11... | collective-permute-start | bytes 663560 | tf_op jit(solution)/shard_map/ppermute | solution.py:416
  22.5 11.8 %all-to-all-start = ((f32[32,8,128]{2,1,0:T(8,128)}), f32[32,8,128]{2,1,0:T(8,128)S(1)}, u32[]{:S(2)}, u32[]{:S(2)}) async-start(f32[32,8,128]{2,1,0:T(8,128)} %bitcast.2), calls=%async_computation | async-start | bytes 262144 | tf_op jit(solution)/shard_map/all_to_all | solution.py:486
  31.7 1.4 %collective-permute-start.5 = (bf16[48,1152]{1,0:T(8,128)(2,1)S(1)}, bf16[48,1152]{1,0:T(8,128)(2,1)S(1)}, u32[]{:S(2)}, u32[]{:S(2)}) collective-permute-start(bf16[48,1152]{1,0:T(8,128)(2,1)S(1)} %get-tuple-element.33), channel_id=1, source_target_pairs={{0,8},{1,9},{2,10},{3,11},{4,12},{5,13},{6,14},{7,15},{8,0},{9,1},... | collective-permute-start | bytes 331784 | tf_op jit(solution)/shard_map/ppermute | solution.py:416

commit v11 on v5

--- a/solution.py
+++ b/solution.py
@@ -308,8 +308,10 @@
             parts.append(tile.astype(BF))
         rhs = jnp.concatenate(parts, axis=1)
         held = None
+        sources = high_ref[:, :, first * LANES : (last + 1) * LANES]
+        products = dot_t(sources.reshape(-1, sources.shape[2]), rhs)
         for m in range(3):
-            s = dot_t(high_ref[m, :, first * LANES : (last + 1) * LANES], rhs)
+            s = products[m * momenta * local_e : (m + 1) * momenta * local_e]
             acc = None
             for e in range(local_e):
                 row = pltpu.roll(s[e * momenta : (e + 1) * momenta], columns - (local_e - e), 1)

time: 34.7 us -> 34.4 us (level)
  transfers between devices with their start and end apart: 9 -> 9, of which waited for: 4 -> 4; matrix products, arithmetic and copies ran while one was open for 0% -> 0% of each run, Pallas kernels for 31% -> 30%
where the time goes in v11:
time: 34.4 us; the launch traced here: 34.2 us
  starting transfers between devices  13.9 us (40%)
  Pallas kernels  13.2 us (38%)
  waiting for transfers between devices  6.4 us (19%)
  between operations  0.73 us (2%)
    pallas_call x7, Pallas kernels, call(): pl.pallas_call(kernel, out_shape=outs, in_specs=specs or [VMEM] * len(ins...  13.2 us
    ppermute x8, starting transfers between devices, move(): return lax.ppermute(value, ('mom', 'en'), links)  10.9 us
    ppermute x8, waiting for transfers between devices, move(): return lax.ppermute(value, ('mom', 'en'), links)  4.94 us
    all_to_all x1, starting transfers between devices, body(): lax.all_to_all(partial.reshape(mom * en, local_k * half, LANES), ('mom',...  2.99 us
    all_to_all x1, waiting for transfers between devices, body(): lax.all_to_all(partial.reshape(mom * en, local_k * half, LANES), ('mom',...  1.46 us
  transfers between devices with their start and end apart: 9, of which 4 were waited for; matrix products, arithmetic and copies ran while one was open for 0% of the time, Pallas kernels for 30%

profile of v11, /device:TPU:0, one launch (start us, length us, event | category | flops | bytes accessed | tf_op | source)
XLA Modules:
  0.0 34.2 jit_solution(11756918619506942832)
XLA Ops:
  0.6 0.0 copy-start.1
  0.6 0.0 copy-start
  0.7 0.0 copy-start.2
  0.7 2.1 %shard_map.68 = (bf16[48,1152]{1,0:T(8,128)(2,1)S(1)}, bf16[48,1152]{1,0:T(8,128)(2,1)S(1)}, bf16[48,1152]{1,0:T(8,128)(2,1)S(1)}, bf16[48,1152]{1,0:T(8,128)(2,1)S(1)}, bf16[2,48,1152]{2,1,0:T(8,128)(2,1)S(1)}) custom-call(bf16[2,24,8,288]{3,2,1,0:T(8,128)(2,1)} %g_hbm.1, bf16[2,24,8,288]{3,2,1,0:T(8,128)(2,1)} %b_hbm.1), custom_call_target="tpu_custom_call" | custom-call | flops 1500000000 | tf_op jit(solution)/shard_map/pallas_call | solution.py:31
  2.7 0.5 %collective-permute-start.2 = (bf16[2,48,1152]{2,1,0:T(8,128)(2,1)S(1)}, bf16[2,48,1152]{2,1,0:T(8,128)(2,1)S(1)}, u32[]{:S(2)}, u32[]{:S(2)}) collective-permute-start(bf16[2,48,1152]{2,1,0:T(8,128)(2,1)S(1)} %get-tuple-element.24), channel_id=1, source_target_pairs={{0,8},{1,9},{2,10},{3,11},{4,12},{5,13},{6,14},{7,15},{8,0},{9,1},... | collective-permute-start | bytes 663560 | tf_op jit(solution)/shard_map/ppermute | solution.py:413
  3.3 2.6 %collective-permute-start = (bf16[48,1152]{1,0:T(8,128)(2,1)S(1)}, bf16[48,1152]{1,0:T(8,128)(2,1)S(1)}, u32[]{:S(2)}, u32[]{:S(2)}) collective-permute-start(bf16[48,1152]{1,0:T(8,128)(2,1)S(1)} %get-tuple-element.22.refs_2_), channel_id=1, source_target_pairs={{0,16},{1,17},{2,18},{3,19},{4,20},{5,21},{6,22},{7,23},{8,24},{9,... | collective-permute-start | bytes 331784 | tf_op jit(solution)/shard_map/ppermute | solution.py:413
  5.8 0.1 collective-permute-start.1
  5.9 1.8 %collective-permute-start.6 = (bf16[48,1152]{1,0:T(8,128)(2,1)S(1)}, bf16[48,1152]{1,0:T(8,128)(2,1)S(1)}, u32[]{:S(2)}, u32[]{:S(2)}) collective-permute-start(bf16[48,1152]{1,0:T(8,128)(2,1)S(1)} %get-tuple-element.36.b_own), channel_id=1, source_target_pairs={{0,1},{1,2},{2,3},{3,4},{4,5},{5,6},{6,7},{7,0},{8,9},{9,10},{10,1... | collective-permute-start | bytes 331784 | tf_op jit(solution)/shard_map/ppermute | solution.py:413
  7.6 1.2 %collective-permute-start.7 = (bf16[48,1152]{1,0:T(8,128)(2,1)S(1)}, bf16[48,1152]{1,0:T(8,128)(2,1)S(1)}, u32[]{:S(2)}, u32[]{:S(2)}) collective-permute-start(bf16[48,1152]{1,0:T(8,128)(2,1)S(1)} %get-tuple-element.37), channel_id=1, source_target_pairs={{0,9},{1,10},{2,11},{3,12},{4,13},{5,14},{6,15},{7,8},{8,1},{9,2},... | collective-permute-start | bytes 331784 | tf_op jit(solution)/shard_map/ppermute | solution.py:413
  8.8 0.0 copy-done.1
  8.8 0.0 copy-done
  8.8 0.0 copy-done.2
  8.8 2.9 %shard_map.69 = (bf16[24,144,256]{2,1,0:T(8,128)(2,1)S(1)}, bf16[24,144,256]{2,1,0:T(8,128)(2,1)S(1)}, bf16[4,288,768]{2,1,0:T(8,128)(2,1)S(1)}, bf16[192,192]{1...) custom-call(s32[2,4]{1,0:T(2,128)S(1)} %copy-done.2, ...), custom_call_target="tpu_custom_call" | custom-call | flops 3000000000 | tf_op jit(solution)/shard_map/pallas_call | solution.py:31
  11.8 0.0 collective-permute-done.refs_0_
  11.8 0.0 collective-permute-done.1.refs_1_
  11.8 0.0 collective-permute-done.2.refs_3_.both_core
  11.8 3.7 %shard_map.70 = (bf16[3,192,1152]{2,1,0:T(8,128)(2,1)S(1)}, f32[2,48,1152]{2,1,0:T(8,128)S(1)}, bf16[2,48,1152]{2,1,0:T(8,128)(2,1)S(1)}, bf16[2,48,1152]{2,1,0:T(8,128)(2,1)S(1)}) custom-call(bf16[48,1152]{1,0:T(8,128)(2,1)S(1)} %collective-permute-done.refs_0_, bf16[48,1152]{1,0:T(8,128)(2,1)S(1)} %collective-permute-done.1.refs_1_, ...), custom_call_target="tpu_custom_call" | custom-call | flops 4000000000 | tf_op jit(solution)/shard_map/pallas_call | solution.py:31
  15.5 1.6 %collective-permute-start.3 = (bf16[2,48,1152]{2,1,0:T(8,128)(2,1)S(1)}, bf16[2,48,1152]{2,1,0:T(8,128)(2,1)S(1)}, u32[]{:S(2)}, u32[]{:S(2)}) collective-permute-start(bf16[2,48,1152]{2,1,0:T(8,128)(2,1)S(1)} %get-tuple-element.30), channel_id=1, source_target_pairs={{0,1},{1,2},{2,3},{3,4},{4,5},{5,6},{6,7},{7,0},{8,9},{9,10},{10,1... | collective-permute-start | bytes 663560 | tf_op jit(solution)/shard_map/ppermute | solution.py:413
  17.1 3.2 %collective-permute-start.4 = (bf16[2,48,1152]{2,1,0:T(8,128)(2,1)S(1)}, bf16[2,48,1152]{2,1,0:T(8,128)(2,1)S(1)}, u32[]{:S(2)}, u32[]{:S(2)}) collective-permute-start(bf16[2,48,1152]{2,1,0:T(8,128)(2,1)S(1)} %get-tuple-element.31), channel_id=1, source_target_pairs={{0,7},{1,0},{2,1},{3,2},{4,3},{5,4},{6,5},{7,6},{8,15},{9,8},{10,9... | collective-permute-start | bytes 663560 | tf_op jit(solution)/shard_map/ppermute | solution.py:413
  20.3 0.0 collective-permute-done.6.prev_own
  20.3 0.0 collective-permute-done.7.prev_far
  20.3 2.5 %shard_map.73 = f32[4,8,8,128]{3,2,1,0:T(8,128)} custom-call(bf16[48,1152]{1,0:T(8,128)(2,1)S(1)} %get-tuple-element.36.b_own, bf16[2,48,1152]{2,1,0:T(8,128)(2,1)S(1)} %collective-permute-done.2.refs_3_.both_core, bf16[48,1152]{1,0:T(8,128)(2,1)S(1)} %collective-permute-done.6.prev_own, bf16[48,1152]{1,0:T(8,128)(2,1)S(1)} %collective-permute-done.7.prev_far, ...), custom_call_target="tpu_custom_call" | custom-call | flops 3000000000 | tf_op jit(solution)/shard_map/pallas_call | solution.py:31
  22.8 3.0 %all-to-all-start = ((f32[32,8,128]{2,1,0:T(8,128)}), f32[32,8,128]{2,1,0:T(8,128)S(1)}, u32[]{:S(2)}, u32[]{:S(2)}) async-start(f32[32,8,128]{2,1,0:T(8,128)} %bitcast.2), calls=%async_computation | async-start | bytes 262144 | tf_op jit(solution)/shard_map/all_to_all | solution.py:479
  25.8 1.4 %collective-permute-done.3.below = bf16[2,48,1152]{2,1,0:T(8,128)(2,1)S(1)} collective-permute-done((bf16[2,48,1152]{2,1,0:T(8,128)(2,1)S(1)}, bf16[2,48,1152]{2,1,0:T(8,128)(2,1)S(1)}, u32[]{:S(2)}, u32[]{:S(2)}) %collective-permute-start.3) | collective-permute-done | bytes 221216 | tf_op jit(solution)/shard_map/ppermute | solution.py:413
  27.2 2.2 %collective-permute-done.4.above = bf16[2,48,1152]{2,1,0:T(8,128)(2,1)S(1)} collective-permute-done((bf16[2,48,1152]{2,1,0:T(8,128)(2,1)S(1)}, bf16[2,48,1152]{2,1,0:T(8,128)(2,1)S(1)}, u32[]{:S(2)}, u32[]{:S(2)}) %collective-permute-start.4) | collective-permute-done | bytes 221216 | tf_op jit(solution)/shard_map/ppermute | solution.py:413
  29.4 0.1 shard_map.71
  29.5 0.1 collective-permute-start.5
  29.6 1.3 %collective-permute-done.5.other = bf16[48,1152]{1,0:T(8,128)(2,1)S(1)} collective-permute-done((bf16[48,1152]{1,0:T(8,128)(2,1)S(1)}, bf16[48,1152]{1,0:T(8,128)(2,1)S(1)}, u32[]{:S(2)}, u32[]{:S(2)}) %collective-permute-start.5) | collective-permute-done | bytes 110624 | tf_op jit(solution)/shard_map/ppermute | solution.py:413
  30.9 1.2 %shard_map.72 = (bf16[2,24,8,288]{3,2,1,0:T(8,128)(2,1)}, f32[8,128]{1,0:T(8,128)S(1)}) custom-call(bf16[48,1152]{1,0:T(8,128)(2,1)S(1)} %get-tuple-element.32.mine, bf16[48,1152]{1,0:T(8,128)(2,1)S(1)} %collective-permute-done.5.other, bf16[384,384]{1,0:T(8,128)(2,1)S(1)} %get-tuple-element.34.perm_ref), custom_call_target="tpu_custom_call" | custom-call | flops 1000000000 | tf_op jit(solution)/shard_map/pallas_call | solution.py:31
  32.1 1.5 %all-to-all-done = f32[32,8,128]{2,1,0:T(8,128)S(1)} async-done(((f32[32,8,128]{2,1,0:T(8,128)}), f32[32,8,128]{2,1,0:T(8,128)S(1)}, u32[]{:S(2)}, u32[]{:S(2)}) %all-to-all-start) | async-done | bytes 131104 | tf_op jit(solution)/shard_map/all_to_all | solution.py:479
  33.5 0.7 %shard_map.74 = f32[2,3,8,24]{3,2,1,0:T(8,128)} custom-call(f32[4,8,8,128]{3,2,1,0:T(8,128)S(1)} %bitcast.5, f32[8,128]{1,0:T(8,128)S(1)} %get-tuple-element.41.after_ref), custom_call_target="tpu_custom_call" | custom-call | flops 500000000 | tf_op jit(solution)/shard_map/pallas_call | solution.py:31
Async XLA Ops:
  0.6 8.2 %copy-start.1 = (f32[2,3,144]{2,0,1:T(2,128)S(1)}, f32[2,3,144]{2,0,1:T(2,128)}, u32[]{:S(2)}) copy-start(f32[2,3,144]{2,0,1:T(2,128)} %param.7) | copy-start | bytes 10372
  0.6 8.2 %copy-start = (bf16[2,8,24,3,8]{2,4,3,1,0:T(8,128)(2,1)S(1)}, bf16[2,8,24,3,8]{2,4,3,1,0:T(8,128)(2,1)}, u32[]{:S(2)}) copy-start(bf16[2,8,24,3,8]{2,4,3,1,0:T(8,128)(2,1)} %param.9) | copy-start | bytes 55300
  0.7 8.2 %copy-start.2 = (s32[2,4]{1,0:T(2,128)S(1)}, s32[2,4]{1,0:T(2,128)}, u32[]{:S(2)}) copy-start(s32[2,4]{1,0:T(2,128)} %near_ref.1) | copy-start | bytes 100
  2.7 9.1 %collective-permute-start.2 = (bf16[2,48,1152]{2,1,0:T(8,128)(2,1)S(1)}, bf16[2,48,1152]{2,1,0:T(8,128)(2,1)S(1)}, u32[]{:S(2)}, u32[]{:S(2)}) collective-permute-start(bf16[2,48,1152]{2,1,0:T(8,128)(2,1)S(1)} %get-tuple-element.24), channel_id=1, source_target_pairs={{0,8},{1,9},{2,10},{3,11},{4,12},{5,13},{6,14},{7,15},{8,0},{9,1},... | collective-permute-start | bytes 663560 | tf_op jit(solution)/shard_map/ppermute | solution.py:413
  3.3 8.5 %collective-permute-start = (bf16[48,1152]{1,0:T(8,128)(2,1)S(1)}, bf16[48,1152]{1,0:T(8,128)(2,1)S(1)}, u32[]{:S(2)}, u32[]{:S(2)}) collective-permute-start(bf16[48,1152]{1,0:T(8,128)(2,1)S(1)} %get-tuple-element.22.refs_2_), channel_id=1, source_target_pairs={{0,16},{1,17},{2,18},{3,19},{4,20},{5,21},{6,22},{7,23},{8,24},{9,... | collective-permute-start | bytes 331784 | tf_op jit(solution)/shard_map/ppermute | solution.py:413
  5.8 6.0 %collective-permute-start.1 = (bf16[48,1152]{1,0:T(8,128)(2,1)S(1)}, bf16[48,1152]{1,0:T(8,128)(2,1)S(1)}, u32[]{:S(2)}, u32[]{:S(2)}) collective-permute-start(bf16[48,1152]{1,0:T(8,128)(2,1)S(1)} %get-tuple-element.23), channel_id=1, source_target_pairs={{0,24},{1,25},{2,26},{3,27},{4,28},{5,29},{6,30},{7,31},{8,16},{9,... | collective-permute-start | bytes 331784 | tf_op jit(solution)/shard_map/ppermute | solution.py:413
  5.9 14.4 %collective-permute-start.6 = (bf16[48,1152]{1,0:T(8,128)(2,1)S(1)}, bf16[48,1152]{1,0:T(8,128)(2,1)S(1)}, u32[]{:S(2)}, u32[]{:S(2)}) collective-permute-start(bf16[48,1152]{1,0:T(8,128)(2,1)S(1)} %get-tuple-element.36.b_own), channel_id=1, source_target_pairs={{0,1},{1,2},{2,3},{3,4},{4,5},{5,6},{6,7},{7,0},{8,9},{9,10},{10,1... | collective-permute-start | bytes 331784 | tf_op jit(solution)/shard_map/ppermute | solution.py:413
  7.6 12.7 %collective-permute-start.7 = (bf16[48,1152]{1,0:T(8,128)(2,1)S(1)}, bf16[48,1152]{1,0:T(8,128)(2,1)S(1)}, u32[]{:S(2)}, u32[]{:S(2)}) collective-permute-start(bf16[48,1152]{1,0:T(8,128)(2,1)S(1)} %get-tuple-element.37), channel_id=1, source_target_pairs={{0,9},{1,10},{2,11},{3,12},{4,13},{5,14},{6,15},{7,8},{8,1},{9,2},... | collective-permute-start | bytes 331784 | tf_op jit(solution)/shard_map/ppermute | solution.py:413
  15.5 11.7 %collective-permute-start.3 = (bf16[2,48,1152]{2,1,0:T(8,128)(2,1)S(1)}, bf16[2,48,1152]{2,1,0:T(8,128)(2,1)S(1)}, u32[]{:S(2)}, u32[]{:S(2)}) collective-permute-start(bf16[2,48,1152]{2,1,0:T(8,128)(2,1)S(1)} %get-tuple-element.30), channel_id=1, source_target_pairs={{0,1},{1,2},{2,3},{3,4},{4,5},{5,6},{6,7},{7,0},{8,9},{9,10},{10,1... | collective-permute-start | bytes 663560 | tf_op jit(solution)/shard_map/ppermute | solution.py:413
  17.1 12.3 %collective-permute-start.4 = (bf16[2,48,1152]{2,1,0:T(8,128)(2,1)S(1)}, bf16[2,48,1152]{2,1,0:T(8,128)(2,1)S(1)}, u32[]{:S(2)}, u32[]{:S(2)}) collective-permute-start(bf16[2,48,1152]{2,1,0:T(8,128)(2,1)S(1)} %get-tuple-element.31), channel_id=1, source_target_pairs={{0,7},{1,0},{2,1},{3,2},{4,3},{5,4},{6,5},{7,6},{8,15},{9,8},{10,9... | collective-permute-start | bytes 663560 | tf_op jit(solution)/shard_map/ppermute | solution.py:413
  22.8 10.7 %all-to-all-start = ((f32[32,8,128]{2,1,0:T(8,128)}), f32[32,8,128]{2,1,0:T(8,128)S(1)}, u32[]{:S(2)}, u32[]{:S(2)}) async-start(f32[32,8,128]{2,1,0:T(8,128)} %bitcast.2), calls=%async_computation | async-start | bytes 262144 | tf_op jit(solution)/shard_map/all_to_all | solution.py:479
  29.5 1.4 %collective-permute-start.5 = (bf16[48,1152]{1,0:T(8,128)(2,1)S(1)}, bf16[48,1152]{1,0:T(8,128)(2,1)S(1)}, u32[]{:S(2)}, u32[]{:S(2)}) collective-permute-start(bf16[48,1152]{1,0:T(8,128)(2,1)S(1)} %get-tuple-element.33), channel_id=1, source_target_pairs={{0,8},{1,9},{2,10},{3,11},{4,12},{5,13},{6,14},{7,15},{8,0},{9,1},... | collective-permute-start | bytes 331784 | tf_op jit(solution)/shard_map/ppermute | solution.py:413

commit v12 on v11

--- a/solution.py
+++ b/solution.py
@@ -45,6 +45,14 @@
 
 def index(dims, axis):
     return lax.broadcasted_iota(jnp.int32, dims, axis)
+
+
+def column(dims):
+    return index((dims[0], 1), 0)
+
+
+def row(dims):
+    return index((1, dims[1]), 1)
 
 
 def split(value, count):
@@ -94,35 +102,34 @@
     size = NO * NO
     chip_k = 2 * local_k
     dims = perm_ref.shape
-    e, k = split(index(dims, 0), momenta)
-    perm_ref[...] = ones_at(index(dims, 1) == k * local_e + e)
+    e, k = split(column(dims), momenta)
+    perm_ref[...] = ones_at(row(dims) == k * local_e + e)
     dims = join_ref.shape
-    row, p = split(index(dims, 0), pairs)
-    join_ref[...] = ones_at(index(dims, 1) == p * (local_k * local_e) + row)
+    n, p = split(column(dims), pairs)
+    join_ref[...] = ones_at(row(dims) == p * (local_k * local_e) + n)
     dims = sort_ref.shape
-    k, i = split(index(dims, 0), 2 * local_e)
+    k, i = split(column(dims), 2 * local_e)
     at = jnp.where(i < local_e, (chip_k + k) * local_e + local_e - 1 - i, k * local_e + 2 * local_e - 1 - i)
-    sort_ref[...] = ones_at((index(dims, 1) == at) & (k < chip_k))
+    sort_ref[...] = ones_at(row(dims) == jnp.where(k < chip_k, at, -1))
     dims = turn_ref.shape[1:]
-    u, i = split(index(dims, 0), NO)
-    turn = ((index(dims, 1) == i * NO + u) & (u < NO)).astype(F32)
+    u, i = split(column(dims), NO)
+    turn = (row(dims) == jnp.where(u < NO, i * NO + u, -1)).astype(F32)
     for j in range(2 * half):
         shift = size * j % LANES
         moved = pltpu.roll(pltpu.roll(turn, shift, 0), shift, 1) if shift else turn
         turn_ref[j] = (moved * (1.0 - 2.0 * (j % 2))).astype(BF)
     x = (size, 2 * LANES)
-    outer, inner = split(index(x, 0), NO)
-    lane_outer, lane_inner = split(index(x, 1), NO)
+    outer, inner = split(column(x), NO)
+    lane_outer, lane_inner = split(row(x), NO)
     pick_l = ones_at(outer == lane_outer)
-    pick_r = ones_at((outer == lane_inner) & (lane_outer < NO))
+    pick_r = ones_at(outer == jnp.where(lane_outer < NO, lane_inner, -1))
     picks = jnp.concatenate([pick_l, pick_r], axis=1)
     x = (size, 32)
-    outer, inner = split(index(x, 0), NO)
-    slot = split(index(x, 1), 16)[1]
+    slot = split(row(x), 16)[1]
     rows_l = ones_at(outer == slot)
     rows_r = ones_at(inner == slot)
     x = (16, size)
-    mask = (split(index(x, 1), NO)[1] == index(x, 0)).astype(F32)
+    mask = (split(row(x), NO)[1] == column(x)).astype(F32)
     atoms = deriv_ref.shape[1]
     spread = []
     for m in range(3):
@@ -178,8 +185,8 @@
         for m in range(3):
             grid = {}
             for a in range(chip_k):
-                row = bases[a, m, pl.ds(core * half + p, 1), :]
-                block = pltpu.roll(jnp.broadcast_to(row, (8, length)), 0, 1, stride=momenta, stride_axis=0)
+                line = bases[a, m, pl.ds(core * half + p, 1), :]
+                block = pltpu.roll(jnp.broadcast_to(line, (8, length)), 0, 1, stride=momenta, stride_axis=0)
                 moved = {0: block}
                 for t in range(tiles):
                     offset = first - step * t

time: 34.4 us -> 34.4 us (level)
  no operation moved by 1% of the time
where the time goes in v12:
time: 34.4 us; the launch traced here: 34.2 us
  starting transfers between devices  13.9 us (40%)
  Pallas kernels  13.2 us (38%)
  waiting for transfers between devices  6.41 us (19%)
  between operations  0.73 us (2%)
    pallas_call x7, Pallas kernels, call(): pl.pallas_call(kernel, out_shape=outs, in_specs=specs or [VMEM] * len(ins...  13.2 us
    ppermute x8, starting transfers between devices, move(): return lax.ppermute(value, ('mom', 'en'), links)  10.9 us
    ppermute x8, waiting for transfers between devices, move(): return lax.ppermute(value, ('mom', 'en'), links)  4.95 us
    all_to_all x1, starting transfers between devices, body(): lax.all_to_all(partial.reshape(mom * en, local_k * half, LANES), ('mom',...  2.98 us
    all_to_all x1, waiting for transfers between devices, body(): lax.all_to_all(partial.reshape(mom * en, local_k * half, LANES), ('mom',...  1.46 us
  transfers between devices with their start and end apart: 9, of which 4 were waited for; matrix products, arithmetic and copies ran while one was open for 0% of the time, Pallas kernels for 30%

profile of v12, /device:TPU:0, one launch (start us, length us, event | category | flops | bytes accessed | tf_op | source)
XLA Modules:
  0.0 34.2 jit_solution(14471754705707381)
XLA Ops:
  0.6 0.0 copy-start.1
  0.6 0.0 copy-start
  0.7 0.0 copy-start.2
  0.7 2.1 %shard_map.68 = (bf16[48,1152]{1,0:T(8,128)(2,1)S(1)}, bf16[48,1152]{1,0:T(8,128)(2,1)S(1)}, bf16[48,1152]{1,0:T(8,128)(2,1)S(1)}, bf16[48,1152]{1,0:T(8,128)(2,1)S(1)}, bf16[2,48,1152]{2,1,0:T(8,128)(2,1)S(1)}) custom-call(bf16[2,24,8,288]{3,2,1,0:T(8,128)(2,1)} %g_hbm.1, bf16[2,24,8,288]{3,2,1,0:T(8,128)(2,1)} %b_hbm.1), custom_call_target="tpu_custom_call" | custom-call | flops 1500000000 | tf_op jit(solution)/shard_map/pallas_call | solution.py:31
  2.7 0.5 %collective-permute-start.2 = (bf16[2,48,1152]{2,1,0:T(8,128)(2,1)S(1)}, bf16[2,48,1152]{2,1,0:T(8,128)(2,1)S(1)}, u32[]{:S(2)}, u32[]{:S(2)}) collective-permute-start(bf16[2,48,1152]{2,1,0:T(8,128)(2,1)S(1)} %get-tuple-element.24), channel_id=1, source_target_pairs={{0,8},{1,9},{2,10},{3,11},{4,12},{5,13},{6,14},{7,15},{8,0},{9,1},... | collective-permute-start | bytes 663560 | tf_op jit(solution)/shard_map/ppermute | solution.py:420
  3.3 2.6 %collective-permute-start = (bf16[48,1152]{1,0:T(8,128)(2,1)S(1)}, bf16[48,1152]{1,0:T(8,128)(2,1)S(1)}, u32[]{:S(2)}, u32[]{:S(2)}) collective-permute-start(bf16[48,1152]{1,0:T(8,128)(2,1)S(1)} %get-tuple-element.22.refs_2_), channel_id=1, source_target_pairs={{0,16},{1,17},{2,18},{3,19},{4,20},{5,21},{6,22},{7,23},{8,24},{9,... | collective-permute-start | bytes 331784 | tf_op jit(solution)/shard_map/ppermute | solution.py:420
  5.8 0.1 collective-permute-start.1
  5.9 1.8 %collective-permute-start.6 = (bf16[48,1152]{1,0:T(8,128)(2,1)S(1)}, bf16[48,1152]{1,0:T(8,128)(2,1)S(1)}, u32[]{:S(2)}, u32[]{:S(2)}) collective-permute-start(bf16[48,1152]{1,0:T(8,128)(2,1)S(1)} %get-tuple-element.36.b_own), channel_id=1, source_target_pairs={{0,1},{1,2},{2,3},{3,4},{4,5},{5,6},{6,7},{7,0},{8,9},{9,10},{10,1... | collective-permute-start | bytes 331784 | tf_op jit(solution)/shard_map/ppermute | solution.py:420
  7.6 1.2 %collective-permute-start.7 = (bf16[48,1152]{1,0:T(8,128)(2,1)S(1)}, bf16[48,1152]{1,0:T(8,128)(2,1)S(1)}, u32[]{:S(2)}, u32[]{:S(2)}) collective-permute-start(bf16[48,1152]{1,0:T(8,128)(2,1)S(1)} %get-tuple-element.37), channel_id=1, source_target_pairs={{0,9},{1,10},{2,11},{3,12},{4,13},{5,14},{6,15},{7,8},{8,1},{9,2},... | collective-permute-start | bytes 331784 | tf_op jit(solution)/shard_map/ppermute | solution.py:420
  8.8 0.0 copy-done.1
  8.8 0.0 copy-done
  8.8 0.0 copy-done.2
  8.8 2.9 %shard_map.69 = (bf16[24,144,256]{2,1,0:T(8,128)(2,1)S(1)}, bf16[24,144,256]{2,1,0:T(8,128)(2,1)S(1)}, bf16[4,288,768]{2,1,0:T(8,128)(2,1)S(1)}, bf16[192,192]{1...) custom-call(s32[2,4]{1,0:T(2,128)S(1)} %copy-done.2, ...), custom_call_target="tpu_custom_call" | custom-call | flops 3000000000 | tf_op jit(solution)/shard_map/pallas_call | solution.py:31
  11.8 0.0 collective-permute-done.refs_0_
  11.8 0.0 collective-permute-done.1.refs_1_
  11.8 0.0 collective-permute-done.2.refs_3_.both_core
  11.8 3.7 %shard_map.70 = (bf16[3,192,1152]{2,1,0:T(8,128)(2,1)S(1)}, f32[2,48,1152]{2,1,0:T(8,128)S(1)}, bf16[2,48,1152]{2,1,0:T(8,128)(2,1)S(1)}, bf16[2,48,1152]{2,1,0:T(8,128)(2,1)S(1)}) custom-call(bf16[48,1152]{1,0:T(8,128)(2,1)S(1)} %collective-permute-done.refs_0_, bf16[48,1152]{1,0:T(8,128)(2,1)S(1)} %collective-permute-done.1.refs_1_, ...), custom_call_target="tpu_custom_call" | custom-call | flops 4000000000 | tf_op jit(solution)/shard_map/pallas_call | solution.py:31
  15.5 1.6 %collective-permute-start.3 = (bf16[2,48,1152]{2,1,0:T(8,128)(2,1)S(1)}, bf16[2,48,1152]{2,1,0:T(8,128)(2,1)S(1)}, u32[]{:S(2)}, u32[]{:S(2)}) collective-permute-start(bf16[2,48,1152]{2,1,0:T(8,128)(2,1)S(1)} %get-tuple-element.30), channel_id=1, source_target_pairs={{0,1},{1,2},{2,3},{3,4},{4,5},{5,6},{6,7},{7,0},{8,9},{9,10},{10,1... | collective-permute-start | bytes 663560 | tf_op jit(solution)/shard_map/ppermute | solution.py:420
  17.1 3.2 %collective-permute-start.4 = (bf16[2,48,1152]{2,1,0:T(8,128)(2,1)S(1)}, bf16[2,48,1152]{2,1,0:T(8,128)(2,1)S(1)}, u32[]{:S(2)}, u32[]{:S(2)}) collective-permute-start(bf16[2,48,1152]{2,1,0:T(8,128)(2,1)S(1)} %get-tuple-element.31), channel_id=1, source_target_pairs={{0,7},{1,0},{2,1},{3,2},{4,3},{5,4},{6,5},{7,6},{8,15},{9,8},{10,9... | collective-permute-start | bytes 663560 | tf_op jit(solution)/shard_map/ppermute | solution.py:420
  20.3 0.0 collective-permute-done.6.prev_own
  20.3 0.0 collective-permute-done.7.prev_far
  20.3 2.5 %shard_map.73 = f32[4,8,8,128]{3,2,1,0:T(8,128)} custom-call(bf16[48,1152]{1,0:T(8,128)(2,1)S(1)} %get-tuple-element.36.b_own, bf16[2,48,1152]{2,1,0:T(8,128)(2,1)S(1)} %collective-permute-done.2.refs_3_.both_core, bf16[48,1152]{1,0:T(8,128)(2,1)S(1)} %collective-permute-done.6.prev_own, bf16[48,1152]{1,0:T(8,128)(2,1)S(1)} %collective-permute-done.7.prev_far, ...), custom_call_target="tpu_custom_call" | custom-call | flops 3000000000 | tf_op jit(solution)/shard_map/pallas_call | solution.py:31
  22.8 3.0 %all-to-all-start = ((f32[32,8,128]{2,1,0:T(8,128)}), f32[32,8,128]{2,1,0:T(8,128)S(1)}, u32[]{:S(2)}, u32[]{:S(2)}) async-start(f32[32,8,128]{2,1,0:T(8,128)} %bitcast.2), calls=%async_computation | async-start | bytes 262144 | tf_op jit(solution)/shard_map/all_to_all | solution.py:486
  25.8 1.4 %collective-permute-done.3.below = bf16[2,48,1152]{2,1,0:T(8,128)(2,1)S(1)} collective-permute-done((bf16[2,48,1152]{2,1,0:T(8,128)(2,1)S(1)}, bf16[2,48,1152]{2,1,0:T(8,128)(2,1)S(1)}, u32[]{:S(2)}, u32[]{:S(2)}) %collective-permute-start.3) | collective-permute-done | bytes 221216 | tf_op jit(solution)/shard_map/ppermute | solution.py:420
  27.2 2.2 %collective-permute-done.4.above = bf16[2,48,1152]{2,1,0:T(8,128)(2,1)S(1)} collective-permute-done((bf16[2,48,1152]{2,1,0:T(8,128)(2,1)S(1)}, bf16[2,48,1152]{2,1,0:T(8,128)(2,1)S(1)}, u32[]{:S(2)}, u32[]{:S(2)}) %collective-permute-start.4) | collective-permute-done | bytes 221216 | tf_op jit(solution)/shard_map/ppermute | solution.py:420
  29.4 0.1 shard_map.71
  29.5 0.1 collective-permute-start.5
  29.6 1.3 %collective-permute-done.5.other = bf16[48,1152]{1,0:T(8,128)(2,1)S(1)} collective-permute-done((bf16[48,1152]{1,0:T(8,128)(2,1)S(1)}, bf16[48,1152]{1,0:T(8,128)(2,1)S(1)}, u32[]{:S(2)}, u32[]{:S(2)}) %collective-permute-start.5) | collective-permute-done | bytes 110624 | tf_op jit(solution)/shard_map/ppermute | solution.py:420
  30.9 1.2 %shard_map.72 = (bf16[2,24,8,288]{3,2,1,0:T(8,128)(2,1)}, f32[8,128]{1,0:T(8,128)S(1)}) custom-call(bf16[48,1152]{1,0:T(8,128)(2,1)S(1)} %get-tuple-element.32.mine, bf16[48,1152]{1,0:T(8,128)(2,1)S(1)} %collective-permute-done.5.other, bf16[384,384]{1,0:T(8,128)(2,1)S(1)} %get-tuple-element.34.perm_ref), custom_call_target="tpu_custom_call" | custom-call | flops 1000000000 | tf_op jit(solution)/shard_map/pallas_call | solution.py:31
  32.1 1.5 %all-to-all-done = f32[32,8,128]{2,1,0:T(8,128)S(1)} async-done(((f32[32,8,128]{2,1,0:T(8,128)}), f32[32,8,128]{2,1,0:T(8,128)S(1)}, u32[]{:S(2)}, u32[]{:S(2)}) %all-to-all-start) | async-done | bytes 131104 | tf_op jit(solution)/shard_map/all_to_all | solution.py:486
  33.5 0.7 %shard_map.74 = f32[2,3,8,24]{3,2,1,0:T(8,128)} custom-call(f32[4,8,8,128]{3,2,1,0:T(8,128)S(1)} %bitcast.5, f32[8,128]{1,0:T(8,128)S(1)} %get-tuple-element.41.after_ref), custom_call_target="tpu_custom_call" | custom-call | flops 500000000 | tf_op jit(solution)/shard_map/pallas_call | solution.py:31
Async XLA Ops:
  0.6 8.2 %copy-start.1 = (f32[2,3,144]{2,0,1:T(2,128)S(1)}, f32[2,3,144]{2,0,1:T(2,128)}, u32[]{:S(2)}) copy-start(f32[2,3,144]{2,0,1:T(2,128)} %param.7) | copy-start | bytes 10372
  0.6 8.2 %copy-start = (bf16[2,8,24,3,8]{2,4,3,1,0:T(8,128)(2,1)S(1)}, bf16[2,8,24,3,8]{2,4,3,1,0:T(8,128)(2,1)}, u32[]{:S(2)}) copy-start(bf16[2,8,24,3,8]{2,4,3,1,0:T(8,128)(2,1)} %param.9) | copy-start | bytes 55300
  0.7 8.2 %copy-start.2 = (s32[2,4]{1,0:T(2,128)S(1)}, s32[2,4]{1,0:T(2,128)}, u32[]{:S(2)}) copy-start(s32[2,4]{1,0:T(2,128)} %near_ref.1) | copy-start | bytes 100
  2.7 9.1 %collective-permute-start.2 = (bf16[2,48,1152]{2,1,0:T(8,128)(2,1)S(1)}, bf16[2,48,1152]{2,1,0:T(8,128)(2,1)S(1)}, u32[]{:S(2)}, u32[]{:S(2)}) collective-permute-start(bf16[2,48,1152]{2,1,0:T(8,128)(2,1)S(1)} %get-tuple-element.24), channel_id=1, source_target_pairs={{0,8},{1,9},{2,10},{3,11},{4,12},{5,13},{6,14},{7,15},{8,0},{9,1},... | collective-permute-start | bytes 663560 | tf_op jit(solution)/shard_map/ppermute | solution.py:420
  3.3 8.5 %collective-permute-start = (bf16[48,1152]{1,0:T(8,128)(2,1)S(1)}, bf16[48,1152]{1,0:T(8,128)(2,1)S(1)}, u32[]{:S(2)}, u32[]{:S(2)}) collective-permute-start(bf16[48,1152]{1,0:T(8,128)(2,1)S(1)} %get-tuple-element.22.refs_2_), channel_id=1, source_target_pairs={{0,16},{1,17},{2,18},{3,19},{4,20},{5,21},{6,22},{7,23},{8,24},{9,... | collective-permute-start | bytes 331784 | tf_op jit(solution)/shard_map/ppermute | solution.py:420
  5.8 6.0 %collective-permute-start.1 = (bf16[48,1152]{1,0:T(8,128)(2,1)S(1)}, bf16[48,1152]{1,0:T(8,128)(2,1)S(1)}, u32[]{:S(2)}, u32[]{:S(2)}) collective-permute-start(bf16[48,1152]{1,0:T(8,128)(2,1)S(1)} %get-tuple-element.23), channel_id=1, source_target_pairs={{0,24},{1,25},{2,26},{3,27},{4,28},{5,29},{6,30},{7,31},{8,16},{9,... | collective-permute-start | bytes 331784 | tf_op jit(solution)/shard_map/ppermute | solution.py:420
  5.9 14.4 %collective-permute-start.6 = (bf16[48,1152]{1,0:T(8,128)(2,1)S(1)}, bf16[48,1152]{1,0:T(8,128)(2,1)S(1)}, u32[]{:S(2)}, u32[]{:S(2)}) collective-permute-start(bf16[48,1152]{1,0:T(8,128)(2,1)S(1)} %get-tuple-element.36.b_own), channel_id=1, source_target_pairs={{0,1},{1,2},{2,3},{3,4},{4,5},{5,6},{6,7},{7,0},{8,9},{9,10},{10,1... | collective-permute-start | bytes 331784 | tf_op jit(solution)/shard_map/ppermute | solution.py:420
  7.6 12.7 %collective-permute-start.7 = (bf16[48,1152]{1,0:T(8,128)(2,1)S(1)}, bf16[48,1152]{1,0:T(8,128)(2,1)S(1)}, u32[]{:S(2)}, u32[]{:S(2)}) collective-permute-start(bf16[48,1152]{1,0:T(8,128)(2,1)S(1)} %get-tuple-element.37), channel_id=1, source_target_pairs={{0,9},{1,10},{2,11},{3,12},{4,13},{5,14},{6,15},{7,8},{8,1},{9,2},... | collective-permute-start | bytes 331784 | tf_op jit(solution)/shard_map/ppermute | solution.py:420
  15.5 11.7 %collective-permute-start.3 = (bf16[2,48,1152]{2,1,0:T(8,128)(2,1)S(1)}, bf16[2,48,1152]{2,1,0:T(8,128)(2,1)S(1)}, u32[]{:S(2)}, u32[]{:S(2)}) collective-permute-start(bf16[2,48,1152]{2,1,0:T(8,128)(2,1)S(1)} %get-tuple-element.30), channel_id=1, source_target_pairs={{0,1},{1,2},{2,3},{3,4},{4,5},{5,6},{6,7},{7,0},{8,9},{9,10},{10,1... | collective-permute-start | bytes 663560 | tf_op jit(solution)/shard_map/ppermute | solution.py:420
  17.1 12.3 %collective-permute-start.4 = (bf16[2,48,1152]{2,1,0:T(8,128)(2,1)S(1)}, bf16[2,48,1152]{2,1,0:T(8,128)(2,1)S(1)}, u32[]{:S(2)}, u32[]{:S(2)}) collective-permute-start(bf16[2,48,1152]{2,1,0:T(8,128)(2,1)S(1)} %get-tuple-element.31), channel_id=1, source_target_pairs={{0,7},{1,0},{2,1},{3,2},{4,3},{5,4},{6,5},{7,6},{8,15},{9,8},{10,9... | collective-permute-start | bytes 663560 | tf_op jit(solution)/shard_map/ppermute | solution.py:420
  22.8 10.7 %all-to-all-start = ((f32[32,8,128]{2,1,0:T(8,128)}), f32[32,8,128]{2,1,0:T(8,128)S(1)}, u32[]{:S(2)}, u32[]{:S(2)}) async-start(f32[32,8,128]{2,1,0:T(8,128)} %bitcast.2), calls=%async_computation | async-start | bytes 262144 | tf_op jit(solution)/shard_map/all_to_all | solution.py:486
  29.5 1.4 %collective-permute-start.5 = (bf16[48,1152]{1,0:T(8,128)(2,1)S(1)}, bf16[48,1152]{1,0:T(8,128)(2,1)S(1)}, u32[]{:S(2)}, u32[]{:S(2)}) collective-permute-start(bf16[48,1152]{1,0:T(8,128)(2,1)S(1)} %get-tuple-element.33), channel_id=1, source_target_pairs={{0,8},{1,9},{2,10},{3,11},{4,12},{5,13},{6,14},{7,15},{8,0},{9,1},... | collective-permute-start | bytes 331784 | tf_op jit(solution)/shard_map/ppermute | solution.py:420

commit v13 on v10

--- a/solution.py
+++ b/solution.py
@@ -407,11 +407,12 @@
         limit=53.12,
     )
 
-    def move(value, dchip, dcore, to=lambda e: e):
+    def move(value, dchip, dcore, to=lambda e: e, cross=False):
         links = []
         for m in range(mom):
-            target = ((m // 2 + dchip) % chips) * 2 + (m % 2 if dcore == 0 else 1 - m % 2)
             for e in range(en):
+                other = (m + dcore + (cross and e == 0)) % 2
+                target = ((m // 2 + dchip) % chips) * 2 + other
                 links.append((m * en + e, target * en + to(e)))
         return lax.ppermute(value, ("mom", "en"), links)
 
@@ -471,7 +472,7 @@
             pltpu.VMEM((6, rows, width), F32),
         ],
     )
-    from_far = move(far, 0, 0, to_far)
+    from_far = move(far, 0, 0, to_far, True)
     from_pair = move(pair, 0, 0, to_pair)
     (partial,) = call(
         functools.partial(

time: 35.2 us -> 35.2 us (level)
  no operation moved by 1% of the time
where the time goes in v13:
time: 35.2 us; the launch traced here: 35 us
  starting transfers between devices  14.1 us (40%)
  Pallas kernels  13.1 us (37%)
  waiting for transfers between devices  7.02 us (20%)
  between operations  0.73 us (2%)
    pallas_call x7, Pallas kernels, call(): pl.pallas_call(kernel, out_shape=outs, in_specs=specs or [VMEM] * len(ins...  13.1 us
    ppermute x8, starting transfers between devices, move(): return lax.ppermute(value, ('mom', 'en'), links)  10.8 us
    ppermute x8, waiting for transfers between devices, move(): return lax.ppermute(value, ('mom', 'en'), links)  7.02 us
    all_to_all x1, starting transfers between devices, body(): lax.all_to_all(partial.reshape(mom * en, local_k * half, LANES), ('mom',...  3.31 us
  transfers between devices with their start and end apart: 9, of which 3 were waited for; matrix products, arithmetic and copies ran while one was open for 0% of the time, Pallas kernels for 30%

profile of v13, /device:TPU:0, one launch (start us, length us, event | category | flops | bytes accessed | tf_op | source)
XLA Modules:
  0.0 35.0 jit_solution(5616307142218535867)
XLA Ops:
  0.6 0.0 copy-start.1
  0.6 0.0 copy-start
  0.7 0.0 copy-start.2
  0.7 2.1 %shard_map.68 = (bf16[48,1152]{1,0:T(8,128)(2,1)S(1)}, bf16[48,1152]{1,0:T(8,128)(2,1)S(1)}, bf16[48,1152]{1,0:T(8,128)(2,1)S(1)}, bf16[48,1152]{1,0:T(8,128)(2,1)S(1)}, bf16[2,48,1152]{2,1,0:T(8,128)(2,1)S(1)}) custom-call(bf16[2,24,8,288]{3,2,1,0:T(8,128)(2,1)} %g_hbm.1, bf16[2,24,8,288]{3,2,1,0:T(8,128)(2,1)} %b_hbm.1), custom_call_target="tpu_custom_call" | custom-call | flops 1500000000 | tf_op jit(solution)/shard_map/pallas_call | solution.py:31
  2.7 0.5 %collective-permute-start.2 = (bf16[2,48,1152]{2,1,0:T(8,128)(2,1)S(1)}, bf16[2,48,1152]{2,1,0:T(8,128)(2,1)S(1)}, u32[]{:S(2)}, u32[]{:S(2)}) collective-permute-start(bf16[2,48,1152]{2,1,0:T(8,128)(2,1)S(1)} %get-tuple-element.24), channel_id=1, source_target_pairs={{0,8},{1,9},{2,10},{3,11},{4,12},{5,13},{6,14},{7,15},{8,0},{9,1},... | collective-permute-start | bytes 663560 | tf_op jit(solution)/shard_map/ppermute | solution.py:417
  3.3 2.6 %collective-permute-start = (bf16[48,1152]{1,0:T(8,128)(2,1)S(1)}, bf16[48,1152]{1,0:T(8,128)(2,1)S(1)}, u32[]{:S(2)}, u32[]{:S(2)}) collective-permute-start(bf16[48,1152]{1,0:T(8,128)(2,1)S(1)} %get-tuple-element.22.refs_2_), channel_id=1, source_target_pairs={{0,16},{1,17},{2,18},{3,19},{4,20},{5,21},{6,22},{7,23},{8,24},{9,... | collective-permute-start | bytes 331784 | tf_op jit(solution)/shard_map/ppermute | solution.py:417
  5.8 0.1 collective-permute-start.1
  5.9 1.8 %collective-permute-start.6 = (bf16[48,1152]{1,0:T(8,128)(2,1)S(1)}, bf16[48,1152]{1,0:T(8,128)(2,1)S(1)}, u32[]{:S(2)}, u32[]{:S(2)}) collective-permute-start(bf16[48,1152]{1,0:T(8,128)(2,1)S(1)} %get-tuple-element.36.b_own), channel_id=1, source_target_pairs={{0,1},{1,2},{2,3},{3,4},{4,5},{5,6},{6,7},{7,0},{8,9},{9,10},{10,1... | collective-permute-start | bytes 331784 | tf_op jit(solution)/shard_map/ppermute | solution.py:417
  7.6 1.2 %collective-permute-start.7 = (bf16[48,1152]{1,0:T(8,128)(2,1)S(1)}, bf16[48,1152]{1,0:T(8,128)(2,1)S(1)}, u32[]{:S(2)}, u32[]{:S(2)}) collective-permute-start(bf16[48,1152]{1,0:T(8,128)(2,1)S(1)} %get-tuple-element.37), channel_id=1, source_target_pairs={{0,9},{1,10},{2,11},{3,12},{4,13},{5,14},{6,15},{7,8},{8,1},{9,2},... | collective-permute-start | bytes 331784 | tf_op jit(solution)/shard_map/ppermute | solution.py:417
  8.8 0.0 copy-done.1
  8.8 0.0 copy-done
  8.8 0.0 copy-done.2
  8.8 2.9 %shard_map.69 = (bf16[24,144,256]{2,1,0:T(8,128)(2,1)S(1)}, bf16[24,144,256]{2,1,0:T(8,128)(2,1)S(1)}, bf16[4,288,768]{2,1,0:T(8,128)(2,1)S(1)}, bf16[192,192]{1...) custom-call(s32[2,4]{1,0:T(2,128)S(1)} %copy-done.2, ...), custom_call_target="tpu_custom_call" | custom-call | flops 3000000000 | tf_op jit(solution)/shard_map/pallas_call | solution.py:31
  11.8 0.0 collective-permute-done.refs_0_
  11.8 0.0 collective-permute-done.1.refs_1_
  11.8 0.0 collective-permute-done.2.refs_3_.both_core
  11.8 3.7 %shard_map.70 = (bf16[3,192,1152]{2,1,0:T(8,128)(2,1)S(1)}, f32[2,48,1152]{2,1,0:T(8,128)S(1)}, bf16[2,48,1152]{2,1,0:T(8,128)(2,1)S(1)}, bf16[2,48,1152]{2,1,0:T(8,128)(2,1)S(1)}) custom-call(bf16[48,1152]{1,0:T(8,128)(2,1)S(1)} %collective-permute-done.refs_0_, bf16[48,1152]{1,0:T(8,128)(2,1)S(1)} %collective-permute-done.1.refs_1_, ...), custom_call_target="tpu_custom_call" | custom-call | flops 4000000000 | tf_op jit(solution)/shard_map/pallas_call | solution.py:31
  15.5 4.6 %collective-permute-start.3 = (bf16[2,48,1152]{2,1,0:T(8,128)(2,1)S(1)}, bf16[2,48,1152]{2,1,0:T(8,128)(2,1)S(1)}, u32[]{:S(2)}, u32[]{:S(2)}) collective-permute-start(bf16[2,48,1152]{2,1,0:T(8,128)(2,1)S(1)} %get-tuple-element.30), channel_id=1, source_target_pairs={{0,15},{1,2},{2,1},{3,4},{4,3},{5,6},{6,5},{7,0},{8,7},{9,10},{10,... | collective-permute-start | bytes 663560 | tf_op jit(solution)/shard_map/ppermute | solution.py:417
  20.1 0.0 collective-permute-start.4
  20.1 0.0 collective-permute-done.6.prev_own
  20.1 0.0 collective-permute-done.7.prev_far
  20.1 2.5 %shard_map.73 = f32[4,8,8,128]{3,2,1,0:T(8,128)} custom-call(bf16[48,1152]{1,0:T(8,128)(2,1)S(1)} %get-tuple-element.36.b_own, bf16[2,48,1152]{2,1,0:T(8,128)(2,1)S(1)} %collective-permute-done.2.refs_3_.both_core, bf16[48,1152]{1,0:T(8,128)(2,1)S(1)} %collective-permute-done.6.prev_own, bf16[48,1152]{1,0:T(8,128)(2,1)S(1)} %collective-permute-done.7.prev_far, ...), custom_call_target="tpu_custom_call" | custom-call | flops 3000000000 | tf_op jit(solution)/shard_map/pallas_call | solution.py:31
  22.6 3.3 %all-to-all-start = ((f32[32,8,128]{2,1,0:T(8,128)}), f32[32,8,128]{2,1,0:T(8,128)S(1)}, u32[]{:S(2)}, u32[]{:S(2)}) async-start(f32[32,8,128]{2,1,0:T(8,128)} %bitcast.2), calls=%async_computation | async-start | bytes 262144 | tf_op jit(solution)/shard_map/all_to_all | solution.py:487
  25.9 0.3 collective-permute-done.3.far
  26.2 5.4 %collective-permute-done.4.pair = bf16[2,48,1152]{2,1,0:T(8,128)(2,1)S(1)} collective-permute-done((bf16[2,48,1152]{2,1,0:T(8,128)(2,1)S(1)}, bf16[2,48,1152]{2,1,0:T(8,128)(2,1)S(1)}, u32[]{:S(2)}, u32[]{:S(2)}) %collective-permute-start.4) | collective-permute-done | bytes 221216 | tf_op jit(solution)/shard_map/ppermute | solution.py:417
  31.6 0.1 shard_map.71
  31.7 0.1 collective-permute-start.5
  31.8 1.3 %collective-permute-done.5.other = bf16[48,1152]{1,0:T(8,128)(2,1)S(1)} collective-permute-done((bf16[48,1152]{1,0:T(8,128)(2,1)S(1)}, bf16[48,1152]{1,0:T(8,128)(2,1)S(1)}, u32[]{:S(2)}, u32[]{:S(2)}) %collective-permute-start.5) | collective-permute-done | bytes 110624 | tf_op jit(solution)/shard_map/ppermute | solution.py:417
  33.1 1.2 %shard_map.72 = (bf16[2,24,8,288]{3,2,1,0:T(8,128)(2,1)}, f32[8,128]{1,0:T(8,128)S(1)}) custom-call(bf16[48,1152]{1,0:T(8,128)(2,1)S(1)} %get-tuple-element.32.mine, bf16[48,1152]{1,0:T(8,128)(2,1)S(1)} %collective-permute-done.5.other, bf16[384,384]{1,0:T(8,128)(2,1)S(1)} %get-tuple-element.34.perm_ref), custom_call_target="tpu_custom_call" | custom-call | flops 1000000000 | tf_op jit(solution)/shard_map/pallas_call | solution.py:31
  34.3 0.0 all-to-all-done
  34.3 0.7 %shard_map.74 = f32[2,3,8,24]{3,2,1,0:T(8,128)} custom-call(f32[4,8,8,128]{3,2,1,0:T(8,128)S(1)} %bitcast.5, f32[8,128]{1,0:T(8,128)S(1)} %get-tuple-element.41.after_ref), custom_call_target="tpu_custom_call" | custom-call | flops 500000000 | tf_op jit(solution)/shard_map/pallas_call | solution.py:31
Async XLA Ops:
  0.6 8.2 %copy-start.1 = (f32[2,3,144]{2,0,1:T(2,128)S(1)}, f32[2,3,144]{2,0,1:T(2,128)}, u32[]{:S(2)}) copy-start(f32[2,3,144]{2,0,1:T(2,128)} %param.7) | copy-start | bytes 10372
  0.6 8.2 %copy-start = (bf16[2,8,24,3,8]{2,4,3,1,0:T(8,128)(2,1)S(1)}, bf16[2,8,24,3,8]{2,4,3,1,0:T(8,128)(2,1)}, u32[]{:S(2)}) copy-start(bf16[2,8,24,3,8]{2,4,3,1,0:T(8,128)(2,1)} %param.9) | copy-start | bytes 55300
  0.7 8.2 %copy-start.2 = (s32[2,4]{1,0:T(2,128)S(1)}, s32[2,4]{1,0:T(2,128)}, u32[]{:S(2)}) copy-start(s32[2,4]{1,0:T(2,128)} %near_ref.1) | copy-start | bytes 100
  2.7 9.1 %collective-permute-start.2 = (bf16[2,48,1152]{2,1,0:T(8,128)(2,1)S(1)}, bf16[2,48,1152]{2,1,0:T(8,128)(2,1)S(1)}, u32[]{:S(2)}, u32[]{:S(2)}) collective-permute-start(bf16[2,48,1152]{2,1,0:T(8,128)(2,1)S(1)} %get-tuple-element.24), channel_id=1, source_target_pairs={{0,8},{1,9},{2,10},{3,11},{4,12},{5,13},{6,14},{7,15},{8,0},{9,1},... | collective-permute-start | bytes 663560 | tf_op jit(solution)/shard_map/ppermute | solution.py:417
  3.3 8.5 %collective-permute-start = (bf16[48,1152]{1,0:T(8,128)(2,1)S(1)}, bf16[48,1152]{1,0:T(8,128)(2,1)S(1)}, u32[]{:S(2)}, u32[]{:S(2)}) collective-permute-start(bf16[48,1152]{1,0:T(8,128)(2,1)S(1)} %get-tuple-element.22.refs_2_), channel_id=1, source_target_pairs={{0,16},{1,17},{2,18},{3,19},{4,20},{5,21},{6,22},{7,23},{8,24},{9,... | collective-permute-start | bytes 331784 | tf_op jit(solution)/shard_map/ppermute | solution.py:417
  5.8 6.0 %collective-permute-start.1 = (bf16[48,1152]{1,0:T(8,128)(2,1)S(1)}, bf16[48,1152]{1,0:T(8,128)(2,1)S(1)}, u32[]{:S(2)}, u32[]{:S(2)}) collective-permute-start(bf16[48,1152]{1,0:T(8,128)(2,1)S(1)} %get-tuple-element.23), channel_id=1, source_target_pairs={{0,24},{1,25},{2,26},{3,27},{4,28},{5,29},{6,30},{7,31},{8,16},{9,... | collective-permute-start | bytes 331784 | tf_op jit(solution)/shard_map/ppermute | solution.py:417
  5.9 14.2 %collective-permute-start.6 = (bf16[48,1152]{1,0:T(8,128)(2,1)S(1)}, bf16[48,1152]{1,0:T(8,128)(2,1)S(1)}, u32[]{:S(2)}, u32[]{:S(2)}) collective-permute-start(bf16[48,1152]{1,0:T(8,128)(2,1)S(1)} %get-tuple-element.36.b_own), channel_id=1, source_target_pairs={{0,1},{1,2},{2,3},{3,4},{4,5},{5,6},{6,7},{7,0},{8,9},{9,10},{10,1... | collective-permute-start | bytes 331784 | tf_op jit(solution)/shard_map/ppermute | solution.py:417
  7.6 12.5 %collective-permute-start.7 = (bf16[48,1152]{1,0:T(8,128)(2,1)S(1)}, bf16[48,1152]{1,0:T(8,128)(2,1)S(1)}, u32[]{:S(2)}, u32[]{:S(2)}) collective-permute-start(bf16[48,1152]{1,0:T(8,128)(2,1)S(1)} %get-tuple-element.37), channel_id=1, source_target_pairs={{0,9},{1,10},{2,11},{3,12},{4,13},{5,14},{6,15},{7,8},{8,1},{9,2},... | collective-permute-start | bytes 331784 | tf_op jit(solution)/shard_map/ppermute | solution.py:417
  15.5 10.7 %collective-permute-start.3 = (bf16[2,48,1152]{2,1,0:T(8,128)(2,1)S(1)}, bf16[2,48,1152]{2,1,0:T(8,128)(2,1)S(1)}, u32[]{:S(2)}, u32[]{:S(2)}) collective-permute-start(bf16[2,48,1152]{2,1,0:T(8,128)(2,1)S(1)} %get-tuple-element.30), channel_id=1, source_target_pairs={{0,15},{1,2},{2,1},{3,4},{4,3},{5,6},{6,5},{7,0},{8,7},{9,10},{10,... | collective-permute-start | bytes 663560 | tf_op jit(solution)/shard_map/ppermute | solution.py:417
  20.1 11.5 %collective-permute-start.4 = (bf16[2,48,1152]{2,1,0:T(8,128)(2,1)S(1)}, bf16[2,48,1152]{2,1,0:T(8,128)(2,1)S(1)}, u32[]{:S(2)}, u32[]{:S(2)}) collective-permute-start(bf16[2,48,1152]{2,1,0:T(8,128)(2,1)S(1)} %get-tuple-element.31), channel_id=1, source_target_pairs={{0,1},{1,0},{2,3},{3,2},{4,5},{5,4},{6,7},{7,6},{8,9},{9,8},{10,11... | collective-permute-start | bytes 663560 | tf_op jit(solution)/shard_map/ppermute | solution.py:417
  22.6 11.7 %all-to-all-start = ((f32[32,8,128]{2,1,0:T(8,128)}), f32[32,8,128]{2,1,0:T(8,128)S(1)}, u32[]{:S(2)}, u32[]{:S(2)}) async-start(f32[32,8,128]{2,1,0:T(8,128)} %bitcast.2), calls=%async_computation | async-start | bytes 262144 | tf_op jit(solution)/shard_map/all_to_all | solution.py:487
  31.7 1.4 %collective-permute-start.5 = (bf16[48,1152]{1,0:T(8,128)(2,1)S(1)}, bf16[48,1152]{1,0:T(8,128)(2,1)S(1)}, u32[]{:S(2)}, u32[]{:S(2)}) collective-permute-start(bf16[48,1152]{1,0:T(8,128)(2,1)S(1)} %get-tuple-element.33), channel_id=1, source_target_pairs={{0,8},{1,9},{2,10},{3,11},{4,12},{5,13},{6,14},{7,15},{8,0},{9,1},... | collective-permute-start | bytes 331784 | tf_op jit(solution)/shard_map/ppermute | solution.py:417
